TPU v7x, 512 devices: a whole 4x4x16 slice. The times are simulated.
512 devices in a mesh: layer: 8 (over y, x_hi), latent: 64 (over z, x_lo, core).
Axes of the slice: x: 4 (x_hi: 2, x_lo: 2; x = x_hi * 2 + x_lo), y: 4, z: 16, core: 2. Of those that a mesh axis runs over, the one named last changes fastest.
Arguments:
- acts: bfloat16 [1280, 4608], P(None, 'layer'), may hold values from -6 to 6
- enc_weight: bfloat16 [4608, 32768], P('layer', 'latent'), may hold values from -0.09375 to 0.09375
- enc_bias: float32 [32768], P('latent'), may hold values from -3 to 3
- dec_weight: bfloat16 [32768, 4608], P('latent', 'layer'), may hold values from -0.3314563 to 0.3314563, as said below
- dec_bias: float32 [4608], P('layer'), may hold values from -2 to 2
Outputs:
- grad_enc: float32 [4608, 32768], P('layer', 'latent')
- grad_enc_bias: float32 [32768], P('latent')
- grad_dec: float32 [32768, 4608], P('latent', 'layer')
- grad_dec_bias: float32 [4608], P('layer')
Inputs may be any that keep to these rules, and one draw needn't show every extreme that they name: `dec_weight`: decoder entries lie within 60 / sqrt(32768) of zero.
All inputs are finite; a program needn't handle non-finite values.
Results may differ from a plain program's by a relative error of at most 0.0045.
Values may be sent and summed in bfloat16 or wider, within the bound.
No kernel may reach another device: no remote copies, remote signals or barrier semaphores. Data moves between devices by JAX's collectives and lax.ppermute only.
A program may use at most 64 MiB of HBM per device.

v0:
```python
import jax
import jax.numpy as jnp
from jax import lax
from jax.sharding import PartitionSpec as P


def per_device(acts, enc_weight, enc_bias, dec_weight, dec_bias):
    rows_all = acts.shape[0]
    scale = 1.0 / jnp.sqrt(jnp.float32(rows_all))
    sparsity = 1.0
    dec_f = dec_weight.astype(jnp.float32)
    squares = jnp.sum(dec_f * dec_f, axis=1)
    partial_pre = jnp.dot(acts, enc_weight, preferred_element_type=jnp.float32)
    summed_pre, summed_sq = lax.psum((partial_pre, squares), "layer")
    pre = summed_pre + enc_bias
    codes = jax.nn.softplus(pre).astype(jnp.bfloat16)
    slope = jax.nn.sigmoid(pre)
    norms = jnp.sqrt(summed_sq + 1e-06)
    partial_recon = jnp.dot(codes, dec_weight, preferred_element_type=jnp.float32)
    recon = lax.psum(partial_recon, "latent") + dec_bias
    err_grad = (2.0 * scale * (recon - acts.astype(jnp.float32))).astype(jnp.bfloat16)
    grad_dec_bias = jnp.sum(err_grad.astype(jnp.float32), axis=0)
    column = jnp.sum(codes.astype(jnp.float32), axis=0)
    grad_dec = lax.dot_general(
        codes, err_grad, (((0,), (0,)), ((), ())), preferred_element_type=jnp.float32
    )
    grad_dec = grad_dec + (sparsity * scale * column / norms)[:, None] * dec_f
    partial_back = lax.dot_general(
        err_grad, dec_weight, (((1,), (1,)), ((), ())), preferred_element_type=jnp.float32
    )
    back = lax.psum(partial_back, "layer") + sparsity * scale * norms
    delta = (back * slope).astype(jnp.bfloat16)
    grad_enc = lax.dot_general(
        acts, delta, (((0,), (0,)), ((), ())), preferred_element_type=jnp.float32
    )
    grad_enc_bias = jnp.sum(delta.astype(jnp.float32), axis=0)
    return (grad_enc, grad_enc_bias, grad_dec, grad_dec_bias)


def solution(mesh):
    return jax.shard_map(
        per_device,
        mesh=mesh,
        in_specs=(
            P(None, "layer"),
            P("layer", "latent"),
            P("latent"),
            P("latent", "layer"),
            P("layer"),
        ),
        out_specs=(P("layer", "latent"), P("latent"), P("latent", "layer"), P("layer")),
        check_vma=False,
    )
```

profile of v0, /device:TPU:1, one launch (start us, length us, event | category | flops | bytes accessed | tf_op | source)
XLA Modules:
  0.0 770.5 jit_solution(1237081623290816993)
XLA Ops:
  7.2 0.0 copy-start
  7.2 0.0 all-reduce.4.cloned.1.call-start
  7.2 1.0 copy-done
  8.2 4.1 fusion.4
  12.4 0.0 all-reduce.4.cloned.1.call-update
  12.4 0.0 copy-start.3
  12.4 0.0 all-reduce.6.cloned.1.call-start
  12.4 146.8 %all-reduce.4.cloned.1.call-done = f32[1280,512]{1,0:T(8,128)} async-done(((f32[1280,512]{1,0:T(8,128)}), f32[1280,512]{1,0:T(8,128)}) %all-reduce.4.cloned.1.call-update) | async-done | bytes 2621456 | tf_op jit(solution)/shard_map/psum | solution.py:14
  159.3 3.3 convert_reduce_fusion.1
  162.6 1.1 copy-done.2
  163.7 2.6 fusion.5
  166.3 0.0 all-reduce.6.cloned.1.call-update
  166.3 0.0 all-reduce.8.cloned.1.call-start
  166.4 442.4 %all-reduce.6.cloned.1.call-done = f32[1280,576]{0,1:T(8,128)} async-done(((f32[1280,576]{0,1:T(8,128)}), f32[1280,576]{0,1:T(8,128)}) %all-reduce.6.cloned.1.call-update) | async-done | bytes 2949136 | tf_op jit(solution)/shard_map/psum | solution.py:20
  608.8 3.1 convert_reduce_fusion
  611.9 1.1 copy-done.6
  613.0 2.8 fusion.6
  615.8 0.0 all-reduce.8.cloned.1.call-update
  615.9 0.2 fusion.1
  616.0 20.4 %psum.31 = f32[512]{0:T(512)S(1)} all-reduce(f32[512]{0:T(512)S(1)} %fusion.1), channel_id=1, replica_groups=mesh['layer'=8,'latent'=64] {'layer'}, use_global_device_ids=true, to_apply=%region_4.5 | all-reduce | flops 512 | bytes 4096 | tf_op jit(solution)/shard_map/psum | solution.py:14
  636.4 4.0 convolution_add_fusion
  640.4 118.4 %all-reduce.8.cloned.1.call-done = f32[1280,512]{1,0:T(8,128)} async-done(((f32[1280,512]{1,0:T(8,128)}), f32[1280,512]{1,0:T(8,128)}) %all-reduce.8.cloned.1.call-update) | async-done | bytes 2621456 | tf_op jit(solution)/shard_map/psum | solution.py:31
  758.9 3.2 convert_reduce_fusion.2
  762.0 1.9 convolution_bitcast_fusion
  (14 shorter events, 0.0 us)
Async XLA Ops:
  7.2 1.1 copy-start
  7.2 152.1 %all-reduce.4.cloned.1.call-start = ((), (), s32[]{:S(2)}) async-start(), calls=%async_computation | async-start | bytes 5242880 | tf_op jit(solution)/shard_map/psum | solution.py:14
  12.4 146.9 %copy-start.7 = (f32[512]{0:T(512)S(1)}, f32[512]{0:T(512)}, u32[]{:S(2)}) copy-start(f32[512]{0:T(512)} %param.7) | copy-start | bytes 6148
  12.4 151.3 %copy-start.3 = (bf16[512,576]{0,1:T(8,128)(2,1)S(1)}, bf16[512,576]{0,1:T(8,128)(2,1)}, u32[]{:S(2)}) copy-start(bf16[512,576]{0,1:T(8,128)(2,1)} %param.8) | copy-start | bytes 1769476
  12.4 596.4 %all-reduce.6.cloned.1.call-start = ((), (), s32[]{:S(2)}) async-start(), calls=%async_computation.1 | async-start | bytes 5898240 | tf_op jit(solution)/shard_map/psum | solution.py:20
  162.6 1.1 copy-start.2
  166.3 442.5 %copy-start.4 = (bf16[1280,576]{0,1:T(8,128)(2,1)S(1)}, bf16[1280,576]{0,1:T(8,128)(2,1)}, u32[]{:S(2)}) copy-start(bf16[1280,576]{0,1:T(8,128)(2,1)} %param.5) | copy-start | bytes 4423684
  166.3 442.5 %copy-start.8 = (f32[576]{0:T(1024)S(1)}, f32[576]{0:T(1024)}, u32[]{:S(2)}) copy-start(f32[576]{0:T(1024)} %param.9) | copy-start | bytes 6916
  166.3 592.5 %all-reduce.8.cloned.1.call-start = ((), (), s32[]{:S(2)}) async-start(), calls=%async_computation.2 | async-start | bytes 5242880 | tf_op jit(solution)/shard_map/psum | solution.py:31
  611.9 1.1 copy-start.6
  636.4 122.4 %copy-start.1 = (f32[1280,512]{1,0:T(8,128)S(1)}, f32[1280,512]{1,0:T(8,128)}, u32[]{:S(2)}) copy-start(f32[1280,512]{1,0:T(8,128)} %all-reduce.4.cloned.1.call-done) | copy-start | bytes 7864324
  758.9 3.2 copy-start.5
Sparse Core Ops, SparseCore 0:
  12.5 146.7 all-reduce.3
  166.5 442.3 all-reduce.5
  616.0 142.8 all-reduce.7
where the time goes:
time: 771 us
  waiting for transfers between devices  708 us (92%)
  blocking collectives  20.4 us (3%)
  matrix products  15.4 us (2%)
  between operations  13.8 us (2%)
  other arithmetic  9.78 us (1%)
    psum x1, waiting for transfers between devices, per_device(): recon = lax.psum(partial_recon, 'latent') + dec_bias  442 us
    psum x1, waiting for transfers between devices, per_device(): summed_pre, summed_sq = lax.psum((partial_pre, squares), 'layer')  147 us
    psum x1, waiting for transfers between devices, per_device(): back = lax.psum(partial_back, 'layer') + sparsity * scale * norms  118 us
    psum x1, blocking collectives, per_device(): summed_pre, summed_sq = lax.psum((partial_pre, squares), 'layer')  20.4 us
  transfers between devices with their start and end apart: 3, of which 3 were waited for; matrix products, arithmetic and copies ran while one was open for 1% of the time, Pallas kernels for 0%

commit v1 on v0

v1 whole, which is shorter than its diff:
```python
import jax
import jax.numpy as jnp
from jax import lax
from jax.sharding import PartitionSpec as P

NZ, NXL, NC = 16, 2, 2
ZLO = 4
ZHI = NZ // ZLO


def latent_index(z, xl, c):
    return (z * NXL + xl) * NC + c


NEAR = [
    [latent_index(zh * ZLO + zl, xl, c) for zl in range(ZLO) for xl in range(NXL)]
    for zh in range(ZHI)
    for c in range(NC)
]
FAR = [
    [latent_index(zh * ZLO + zl, xl, c) for zh in range(ZHI)]
    for zl in range(ZLO)
    for xl in range(NXL)
    for c in range(NC)
]
CORE = [
    (latent_index(z, xl, c), latent_index(z, xl, 1 - c))
    for z in range(NZ)
    for xl in range(NXL)
    for c in range(NC)
]

F32 = jnp.float32
BF16 = jnp.bfloat16


def dot(a, b, dims):
    return lax.dot_general(a, b, (dims, ((), ())), preferred_element_type=F32)


def add_up(blocks, me, own):
    total = own
    for j in range(blocks.shape[0]):
        total = total + jnp.where(me == j, 0.0, blocks[j].astype(F32))
    return total


def per_device(acts, enc_weight, enc_bias, dec_weight, dec_bias):
    rows, feat = acts.shape
    lat = enc_weight.shape[1]
    scale = 1.0 / jnp.sqrt(F32(rows))
    sparsity = 1.0
    me_layer = lax.axis_index("layer")
    me_latent = lax.axis_index("latent")
    n_layer = 8
    part = rows // n_layer
    core = me_latent % NC
    near = (me_latent // NC) % (ZLO * NXL)
    half = rows // NC
    block = half // (ZLO * NXL)

    with jax.named_scope("norms"):
        dec_f = dec_weight.astype(F32)
        squares = jnp.sum(dec_f * dec_f, axis=1)
        norms = jnp.sqrt(lax.psum(squares, "layer") + 1e-06)

    with jax.named_scope("encode"):
        partial_pre = dot(acts, enc_weight, ((1,), (0,))).astype(BF16)
        got = lax.all_to_all(partial_pre, "layer", 0, 0, tiled=True)
        own_acts = lax.dynamic_slice_in_dim(acts, me_layer * part, part, 0)
        own_pre = dot(own_acts, enc_weight, ((1,), (0,)))
        pre = add_up(got.reshape(n_layer, part, lat), me_layer, own_pre) + enc_bias
        codes_part = jax.nn.softplus(pre).astype(BF16)
        slope = jax.nn.sigmoid(pre)
        codes = lax.all_to_all(
            jnp.broadcast_to(codes_part, (n_layer, part, lat)).reshape(rows, lat),
            "layer", 0, 0, tiled=True,
        )

    with jax.named_scope("decode"):
        other_codes = lax.dynamic_slice_in_dim(codes, (1 - core) * half, half, 0)
        core_codes = lax.dynamic_slice_in_dim(codes, core * half, half, 0)
        away = dot(other_codes, dec_weight, ((1,), (0,))).astype(BF16)
        arrived = lax.ppermute(away, "latent", CORE)
        recon = dot(core_codes, dec_weight, ((1,), (0,))) + arrived.astype(F32)
        got = lax.all_to_all(
            recon.astype(BF16), "latent", 0, 0, axis_index_groups=NEAR, tiled=True
        )
        own_recon = lax.dynamic_slice_in_dim(recon, near * block, block, 0)
        recon = add_up(got.reshape(ZLO * NXL, block, feat), near, own_recon).astype(BF16)
        got = lax.all_to_all(
            jnp.broadcast_to(recon, (ZHI, block, feat)).reshape(ZHI * block, feat),
            "latent", 0, 0, axis_index_groups=FAR, tiled=True,
        )
        recon = jnp.sum(got.reshape(ZHI, block, feat).astype(F32), axis=0) + dec_bias
        acts_part = lax.dynamic_slice_in_dim(acts, core * half + near * block, block, 0)
        err_part = (2.0 * scale * (recon - acts_part.astype(F32))).astype(BF16)

    with jax.named_scope("spread_error"):
        err_half = lax.all_to_all(
            jnp.broadcast_to(err_part, (ZLO * NXL, block, feat)).reshape(half, feat),
            "latent", 0, 0, axis_index_groups=NEAR, tiled=True,
        )
        err_other = lax.ppermute(err_half, "latent", CORE)
        first = jnp.where(core == 0, err_half, err_other)
        second = jnp.where(core == 0, err_other, err_half)
        err_grad = jnp.concatenate([first, second], axis=0)

    with jax.named_scope("back"):
        partial_back = dot(err_grad, dec_weight, ((1,), (1,))).astype(BF16)
        got = lax.all_to_all(partial_back, "layer", 0, 0, tiled=True)
        own_err = lax.dynamic_slice_in_dim(err_grad, me_layer * part, part, 0)
        own_back = dot(own_err, dec_weight, ((1,), (1,)))
        back = add_up(got.reshape(n_layer, part, lat), me_layer, own_back)
        back = back + sparsity * scale * norms
        delta_part = (back * slope).astype(BF16)
        delta = lax.all_to_all(
            jnp.broadcast_to(delta_part, (n_layer, part, lat)).reshape(rows, lat),
            "layer", 0, 0, tiled=True,
        )

    with jax.named_scope("grads"):
        grad_dec_bias = jnp.sum(err_grad.astype(F32), axis=0)
        column = jnp.sum(codes.astype(F32), axis=0)
        grad_dec = dot(codes, err_grad, ((0,), (0,)))
        grad_dec = grad_dec + (sparsity * scale * column / norms)[:, None] * dec_f
        grad_enc = dot(acts, delta, ((0,), (0,)))
        grad_enc_bias = jnp.sum(delta.astype(F32), axis=0)
    return (grad_enc, grad_enc_bias, grad_dec, grad_dec_bias)


def solution(mesh):
    return jax.shard_map(
        per_device,
        mesh=mesh,
        in_specs=(
            P(None, "layer"),
            P("layer", "latent"),
            P("latent"),
            P("latent", "layer"),
            P("layer"),
        ),
        out_specs=(P("layer", "latent"), P("latent"), P("latent", "layer"), P("layer")),
        check_vma=False,
    )
```

time: 771 us -> 247 us (0.32)
  waiting for transfers between devices: 708 us -> 91.8 us
  starting transfers between devices: 0.12 us -> 53 us
  blocking collectives: 20.4 us -> 50.7 us
  local copies, waits for them, and re-layouts: 3.24 us -> 19.3 us
  between operations: 13.8 us -> 0.82 us
    psum x3 -> x0, waiting for transfers between devices: 708 us -> none  [the longest x1 442 us: per_device(): recon = lax.psum(partial_recon, 'latent') + dec_bias]
    all_to_all x0 -> x6, waiting for transfers between devices: none -> 87.6 us  [the longest x1 22.1 us: per_device(): lax.all_to_all(jnp.broadcast_to(recon, (ZHI, block, feat)).reshape(ZHI *...]
    all_to_all x0 -> x6, starting transfers between devices: none -> 41.3 us  [the longest x1 13.5 us: per_device(): lax.all_to_all(jnp.broadcast_to(recon, (ZHI, block, feat)).reshape(ZHI *...]
    all_to_all x0 -> x1, blocking collectives: none -> 22.5 us  [per_device(): lax.all_to_all(jnp.broadcast_to(err_part, (ZLO * NXL, block, feat)).resha...]
    ppermute x0 -> x2, starting transfers between devices: none -> 11.7 us  [the longest x1 6.59 us: per_device(): arrived = lax.ppermute(away, 'latent', CORE)]
    psum x1, blocking collectives: 20.4 us -> 28.3 us  [per_device(): norms = jnp.sqrt(lax.psum(squares, 'layer') + 1e-06)]
    dot_general x5 -> x8, matrix products: 15.4 us -> 19.1 us  [dot(): return lax.dot_general(a, b, (dims, ((), ())), preferred_element_type=F32)]
  transfers between devices with their start and end apart: 3 -> 8, of which waited for: 3 -> 7; matrix products, arithmetic and copies ran while one was open for 1% -> 2% of each run, Pallas kernels for 0% -> 0%
where the time goes in v1:
time: 247 us; the launch traced here: 244 us
  waiting for transfers between devices  91.8 us (37%)
  starting transfers between devices  53 us (21%)
  blocking collectives  50.7 us (21%)
  local copies, waits for them, and re-layouts  19.3 us (8%)
  matrix products  19.1 us (8%)
  other arithmetic  8.94 us (4%)
    psum x1, blocking collectives, per_device(): norms = jnp.sqrt(lax.psum(squares, 'layer') + 1e-06)  28.3 us
    all_to_all x1, blocking collectives, per_device(): lax.all_to_all(jnp.broadcast_to(err_part, (ZLO * NXL, block, feat)).resha...  22.5 us
    all_to_all x1, waiting for transfers between devices, per_device(): lax.all_to_all(jnp.broadcast_to(recon, (ZHI, block, feat)).reshape(ZHI *...  22.1 us
    all_to_all x1, waiting for transfers between devices, per_device(): lax.all_to_all(recon.astype(BF16), 'latent', 0, 0, axis_index_groups=NEAR...  20.4 us
    dot_general x8, matrix products, dot(): return lax.dot_general(a, b, (dims, ((), ())), preferred_element_type=F32)  19.1 us
    all_to_all x1, waiting for transfers between devices, per_device(): got = lax.all_to_all(partial_pre, 'layer', 0, 0, tiled=True)  17.1 us
    all_to_all x1, waiting for transfers between devices, per_device(): lax.all_to_all(jnp.broadcast_to(codes_part, (n_layer, part, lat)).reshape...  16.2 us
    all_to_all x1, starting transfers between devices, per_device(): lax.all_to_all(jnp.broadcast_to(recon, (ZHI, block, feat)).reshape(ZHI *...  13.5 us
  transfers between devices with their start and end apart: 8, of which 7 were waited for; matrix products, arithmetic and copies ran while one was open for 2% of the time, Pallas kernels for 0%

profile of v1, /device:TPU:1, one launch (start us, length us, event | category | flops | bytes accessed | tf_op | source)
XLA Modules:
  0.0 243.8 jit_solution(12245796816440691403)
XLA Ops:
  2.0 3.4 %convolution_convert_fusion.1 = bf16[1280,512]{1,0:T(8,128)(2,1)} fusion(bf16[1280,576]{0,1:T(8,128)(2,1)S(1)} %copy-done, bf16[576,512]{1,0:T(8,128)(2,1)} %param.6), kind=kOutput, calls=%fused_computation.2 | convolution fusion | flops 755630080 | bytes 3375104 | tf_op jit(solution)/shard_map/encode/dot_general | solution.py:38
  5.4 7.6 %all-to-all-start = ((bf16[8,160,512]{2,1,0:T(8,128)(2,1)}), bf16[8,160,512]{2,1,0:T(8,128)(2,1)S(1)}, u32[]{:S(2)}, u32[]{:S(2)}) async-start(bf16[8,160,512]{2,1,0:T(8,128)(2,1)} %bitcast.89), calls=%async_computation | async-start | bytes 2621440 | tf_op jit(solution)/shard_map/encode/all_to_all | solution.py:69
  13.0 17.1 %all-to-all-done = bf16[8,160,512]{2,1,0:T(8,128)(2,1)S(1)} async-done(((bf16[8,160,512]{2,1,0:T(8,128)(2,1)}), bf16[8,160,512]{2,1,0:T(8,128)(2,1)S(1)}, u32[]{:S(2)}, u32[]{:S(2)}) %all-to-all-start) | async-done | bytes 1310752 | tf_op jit(solution)/shard_map/encode/all_to_all | solution.py:69
  32.9 3.7 %all-to-all-start.1 = ((bf16[8,160,512]{2,1,0:T(8,128)(2,1)}), bf16[8,160,512]{2,1,0:T(8,128)(2,1)S(1)}, u32[]{:S(2)}, u32[]{:S(2)}) async-start(bf16[8,160,512]{2,1,0:T(8,128)(2,1)} %broadcast_in_dim.50), calls=%async_computation.1 | async-start | bytes 2621440 | tf_op jit(solution)/shard_map/encode/all_to_all | solution.py:75
  36.6 16.2 %all-to-all-done.1 = bf16[8,160,512]{2,1,0:T(8,128)(2,1)S(1)} async-done(((bf16[8,160,512]{2,1,0:T(8,128)(2,1)}), bf16[8,160,512]{2,1,0:T(8,128)(2,1)S(1)}, u32[]{:S(2)}, u32[]{:S(2)}) %all-to-all-start.1) | async-done | bytes 1310752 | tf_op jit(solution)/shard_map/encode/all_to_all | solution.py:75
  54.4 6.6 %collective-permute-start = (bf16[640,576]{0,1:T(8,128)(2,1)}, bf16[640,576]{0,1:T(8,128)(2,1)}, u32[]{:S(2)}, u32[]{:S(2)}) collective-permute-start(bf16[640,576]{0,1:T(8,128)(2,1)} %convolution_convert_fusion.2), channel_id=1, source_target_pairs={{0,1},{1,0},{2,3},{3,2},{4,5},{5,4},{6,7},{7,6},{8,9},{9,8},{10,11... | collective-permute-start | bytes 2211848 | tf_op jit(solution)/shard_map/decode/ppermute | solution.py:84
  61.0 2.2 collective-permute-done
  63.1 3.1 %fusion.38 = (bf16[640,576]{0,1:T(8,128)(2,1)S(1)}, f32[640,576]{0,1:T(8,128)}) fusion(bf16[640,576]{0,1:T(8,128)(2,1)} %collective-permute-done, bf16[512,576]{0,1:T(8,128)(2,1)} %param.8, bf16[1280,512]{1,0:T(8,128)(2,1)S(1)} %bitcast.85, s32[]{:T(128)S(6)} %select_n.279), kind=kOutput, calls=%fused_computation.67 | convolution fusion | flops 378593280 | bytes 4194308 | tf_op jit(solution)/shard_map/decode/dot_general | solution.py:38
  67.4 7.9 %all-to-all-start.2 = ((bf16[8,80,576]{2,1,0:T(8,128)(2,1)}), bf16[8,80,576]{2,1,0:T(8,128)(2,1)}, u32[]{:S(2)}, u32[]{:S(2)}) async-start(bf16[8,80,576]{2,1,0:T(8,128)(2,1)} %bitcast.88), calls=%async_computation.2 | async-start | bytes 1638400 | tf_op jit(solution)/shard_map/decode/all_to_all | solution.py:86
  75.3 20.4 %all-to-all-done.2 = bf16[8,80,576]{2,1,0:T(8,128)(2,1)} async-done(((bf16[8,80,576]{2,1,0:T(8,128)(2,1)}), bf16[8,80,576]{2,1,0:T(8,128)(2,1)}, u32[]{:S(2)}, u32[]{:S(2)}) %all-to-all-start.2) | async-done | bytes 737312 | tf_op jit(solution)/shard_map/decode/all_to_all | solution.py:86
  104.4 2.2 fusion.25
  108.5 13.5 %all-to-all-start.3 = ((bf16[4,80,576]{2,1,0:T(8,128)(2,1)}), bf16[4,80,576]{2,1,0:T(8,128)(2,1)S(1)}, u32[]{:S(2)}, u32[]{:S(2)}) async-start(bf16[4,80,576]{2,1,0:T(8,128)(2,1)} %broadcast_in_dim.52), calls=%async_computation.3 | async-start | bytes 819200 | tf_op jit(solution)/shard_map/decode/all_to_all | solution.py:91
  122.3 22.1 %all-to-all-done.3 = bf16[4,80,576]{2,1,0:T(8,128)(2,1)S(1)} async-done(((bf16[4,80,576]{2,1,0:T(8,128)(2,1)}), bf16[4,80,576]{2,1,0:T(8,128)(2,1)S(1)}, u32[]{:S(2)}, u32[]{:S(2)}) %all-to-all-start.3) | async-done | bytes 368672 | tf_op jit(solution)/shard_map/decode/all_to_all | solution.py:91
  144.6 22.5 %all_to_all.60 = bf16[8,80,576]{2,1,0:T(8,128)(2,1)} all-to-all(bf16[8,80,576]{2,1,0:T(8,128)(2,1)S(1)} %broadcast_in_dim.53), channel_id=1, replica_groups={{0,2,4,6,8,10,12,14},{1,3,5,7,9,11,13,15},{16,18,20,22,24,26,28,30},{17..., dimensions={0} | all-to-all | bytes 1474560 | tf_op jit(solution)/shard_map/spread_error/all_to_all | solution.py:100
  167.1 2.3 copy.51
  169.4 5.1 %collective-permute-start.1 = (bf16[640,576]{0,1:T(8,128)(2,1)}, bf16[640,576]{0,1:T(8,128)(2,1)S(1)}, u32[]{:S(2)}, u32[]{:S(2)}) collective-permute-start(bf16[640,576]{0,1:T(8,128)(2,1)} %copy.51), channel_id=1, source_target_pairs={{0,1},{1,0},{2,3},{3,2},{4,5},{5,4},{6,7},{7,6},{8,9},{9,8},{10,11... | collective-permute-start | bytes 2211848 | tf_op jit(solution)/shard_map/spread_error/ppermute | solution.py:104
  179.4 2.3 convolution_convert_fusion
  181.7 4.3 %all-to-all-start.5 = ((bf16[8,160,512]{2,1,0:T(8,128)(2,1)}), bf16[8,160,512]{2,1,0:T(8,128)(2,1)}, u32[]{:S(2)}, u32[]{:S(2)}) async-start(bf16[8,160,512]{2,1,0:T(8,128)(2,1)} %bitcast.90), calls=%async_computation.5 | async-start | bytes 2621440 | tf_op jit(solution)/shard_map/back/all_to_all | solution.py:111
  186.1 28.3 %psum.7 = f32[512]{0:T(512)S(1)} all-reduce(f32[512]{0:T(512)S(1)} %fusion.17), channel_id=1, replica_groups=mesh['layer'=8,'latent'=64] {'layer'}, use_global_device_ids=true, to_apply=%region_2.3 | all-reduce | flops 512 | bytes 4096 | tf_op jit(solution)/shard_map/norms/psum | solution.py:65
  217.9 4.3 %all-to-all-start.6 = ((bf16[8,160,512]{2,1,0:T(8,128)(2,1)}), bf16[8,160,512]{2,1,0:T(8,128)(2,1)}, u32[]{:S(2)}, u32[]{:S(2)}) async-start(bf16[8,160,512]{2,1,0:T(8,128)(2,1)} %broadcast_in_dim.54), calls=%async_computation.6 | async-start | bytes 2621440 | tf_op jit(solution)/shard_map/back/all_to_all | solution.py:117
  222.2 2.4 convert_reduce_fusion
  226.7 11.7 %all-to-all-done.6 = bf16[8,160,512]{2,1,0:T(8,128)(2,1)} async-done(((bf16[8,160,512]{2,1,0:T(8,128)(2,1)}), bf16[8,160,512]{2,1,0:T(8,128)(2,1)}, u32[]{:S(2)}, u32[]{:S(2)}) %all-to-all-start.6) | async-done | bytes 1310752 | tf_op jit(solution)/shard_map/back/all_to_all | solution.py:117
  238.4 3.3 %convolution_bitcast_fusion = f32[576,512]{1,0:T(8,128)} fusion(bf16[1280,576]{0,1:T(8,128)(2,1)S(1)} %copy-done, bf16[1280,512]{1,0:T(8,128)(2,1)} %bitcast.29), kind=kOutput, calls=%fused_computation.12 | convolution fusion | flops 754974720 | bytes 3964928 | tf_op jit(solution)/shard_map/grads/dot_general | solution.py:38
  241.6 2.1 convert_reduce_fusion.2
  (50 shorter events, 28.4 us)
Async XLA Ops:
  0.6 1.4 copy-start
  5.4 24.8 %copy-start.8 = (bf16[576,512]{1,0:T(8,128)(2,1)S(1)}, bf16[576,512]{1,0:T(8,128)(2,1)}, u32[]{:S(2)}) copy-start(bf16[576,512]{1,0:T(8,128)(2,1)} %param.6) | copy-start | bytes 1769476
  5.4 24.8 %copy-start.9 = (f32[512]{0:T(512)S(1)}, f32[512]{0:T(512)}, u32[]{:S(2)}) copy-start(f32[512]{0:T(512)} %param.7) | copy-start | bytes 6148
  5.4 24.7 %all-to-all-start = ((bf16[8,160,512]{2,1,0:T(8,128)(2,1)}), bf16[8,160,512]{2,1,0:T(8,128)(2,1)S(1)}, u32[]{:S(2)}, u32[]{:S(2)}) async-start(bf16[8,160,512]{2,1,0:T(8,128)(2,1)} %bitcast.89), calls=%async_computation | async-start | bytes 2621440 | tf_op jit(solution)/shard_map/encode/all_to_all | solution.py:69
  32.9 20.0 %copy-start.5 = (bf16[512,576]{0,1:T(8,128)(2,1)S(1)}, bf16[512,576]{0,1:T(8,128)(2,1)}, u32[]{:S(2)}) copy-start(bf16[512,576]{0,1:T(8,128)(2,1)} %param.8) | copy-start | bytes 1769476
  32.9 20.0 %all-to-all-start.1 = ((bf16[8,160,512]{2,1,0:T(8,128)(2,1)}), bf16[8,160,512]{2,1,0:T(8,128)(2,1)S(1)}, u32[]{:S(2)}, u32[]{:S(2)}) async-start(bf16[8,160,512]{2,1,0:T(8,128)(2,1)} %broadcast_in_dim.50), calls=%async_computation.1 | async-start | bytes 2621440 | tf_op jit(solution)/shard_map/encode/all_to_all | solution.py:75
  54.4 8.8 %collective-permute-start = (bf16[640,576]{0,1:T(8,128)(2,1)}, bf16[640,576]{0,1:T(8,128)(2,1)}, u32[]{:S(2)}, u32[]{:S(2)}) collective-permute-start(bf16[640,576]{0,1:T(8,128)(2,1)} %convolution_convert_fusion.2), channel_id=1, source_target_pairs={{0,1},{1,0},{2,3},{3,2},{4,5},{5,4},{6,7},{7,6},{8,9},{9,8},{10,11... | collective-permute-start | bytes 2211848 | tf_op jit(solution)/shard_map/decode/ppermute | solution.py:84
  67.4 28.3 %all-to-all-start.2 = ((bf16[8,80,576]{2,1,0:T(8,128)(2,1)}), bf16[8,80,576]{2,1,0:T(8,128)(2,1)}, u32[]{:S(2)}, u32[]{:S(2)}) async-start(bf16[8,80,576]{2,1,0:T(8,128)(2,1)} %bitcast.88), calls=%async_computation.2 | async-start | bytes 1638400 | tf_op jit(solution)/shard_map/decode/all_to_all | solution.py:86
  106.7 37.8 %copy-start.7 = (f32[576]{0:T(1024)S(1)}, f32[576]{0:T(1024)}, u32[]{:S(2)}) copy-start(f32[576]{0:T(1024)} %param.9) | copy-start | bytes 6916
  108.5 35.9 %all-to-all-start.3 = ((bf16[4,80,576]{2,1,0:T(8,128)(2,1)}), bf16[4,80,576]{2,1,0:T(8,128)(2,1)S(1)}, u32[]{:S(2)}, u32[]{:S(2)}) async-start(bf16[4,80,576]{2,1,0:T(8,128)(2,1)} %broadcast_in_dim.52), calls=%async_computation.3 | async-start | bytes 819200 | tf_op jit(solution)/shard_map/decode/all_to_all | solution.py:91
  169.4 7.2 %collective-permute-start.1 = (bf16[640,576]{0,1:T(8,128)(2,1)}, bf16[640,576]{0,1:T(8,128)(2,1)S(1)}, u32[]{:S(2)}, u32[]{:S(2)}) collective-permute-start(bf16[640,576]{0,1:T(8,128)(2,1)} %copy.51), channel_id=1, source_target_pairs={{0,1},{1,0},{2,3},{3,2},{4,5},{5,4},{6,7},{7,6},{8,9},{9,8},{10,11... | collective-permute-start | bytes 2211848 | tf_op jit(solution)/shard_map/spread_error/ppermute | solution.py:104
  177.8 1.6 copy-start.6
  179.4 2.3 copy-start.1
  179.4 2.3 copy-start.3
  181.7 33.0 %all-to-all-start.5 = ((bf16[8,160,512]{2,1,0:T(8,128)(2,1)}), bf16[8,160,512]{2,1,0:T(8,128)(2,1)}, u32[]{:S(2)}, u32[]{:S(2)}) async-start(bf16[8,160,512]{2,1,0:T(8,128)(2,1)} %bitcast.90), calls=%async_computation.5 | async-start | bytes 2621440 | tf_op jit(solution)/shard_map/back/all_to_all | solution.py:111
  217.9 20.5 %all-to-all-start.6 = ((bf16[8,160,512]{2,1,0:T(8,128)(2,1)}), bf16[8,160,512]{2,1,0:T(8,128)(2,1)}, u32[]{:S(2)}, u32[]{:S(2)}) async-start(bf16[8,160,512]{2,1,0:T(8,128)(2,1)} %broadcast_in_dim.54), calls=%async_computation.6 | async-start | bytes 2621440 | tf_op jit(solution)/shard_map/back/all_to_all | solution.py:117
  222.2 2.5 %copy-start.2 = (bf16[640,576]{1,0:T(8,128)(2,1)S(1)}, bf16[640,576]{1,0:T(8,128)(2,1)}, u32[]{:S(2)}) copy-start(bf16[640,576]{1,0:T(8,128)(2,1)} %copy-done.1) | copy-start | bytes 2211844
  222.2 2.4 %copy-start.4 = (bf16[640,576]{1,0:T(8,128)(2,1)S(1)}, bf16[640,576]{1,0:T(8,128)(2,1)}, u32[]{:S(2)}) copy-start(bf16[640,576]{1,0:T(8,128)(2,1)} %copy-done.3) | copy-start | bytes 2211844

commit v2 on v1

--- a/solution.py
+++ b/solution.py
@@ -4,12 +4,17 @@
 from jax.sharding import PartitionSpec as P
 
 NZ, NXL, NC = 16, 2, 2
+NY, NXH = 4, 2
 ZLO = 4
 ZHI = NZ // ZLO
 
 
 def latent_index(z, xl, c):
     return (z * NXL + xl) * NC + c
+
+
+def layer_index(y, xh):
+    return y * NXH + xh
 
 
 NEAR = [
@@ -28,6 +33,11 @@
     for z in range(NZ)
     for xl in range(NXL)
     for c in range(NC)
+]
+LAYER_STEPS = [
+    [(layer_index(y, xh), layer_index(y ^ 1, xh)) for y in range(NY) for xh in range(NXH)],
+    [(layer_index(y, xh), layer_index(3 - y, xh)) for y in range(NY) for xh in range(NXH)],
+    [(layer_index(y, xh), layer_index(y, 1 - xh)) for y in range(NY) for xh in range(NXH)],
 ]
 
 F32 = jnp.float32
@@ -52,17 +62,22 @@
     sparsity = 1.0
     me_layer = lax.axis_index("layer")
     me_latent = lax.axis_index("latent")
-    n_layer = 8
+    n_layer = NY * NXH
+    n_near = ZLO * NXL
     part = rows // n_layer
     core = me_latent % NC
-    near = (me_latent // NC) % (ZLO * NXL)
+    near = (me_latent // NC) % n_near
     half = rows // NC
-    block = half // (ZLO * NXL)
+    block = feat // n_near
 
-    with jax.named_scope("norms"):
-        dec_f = dec_weight.astype(F32)
-        squares = jnp.sum(dec_f * dec_f, axis=1)
-        norms = jnp.sqrt(lax.psum(squares, "layer") + 1e-06)
+    with jax.named_scope("local_rows"):
+        acts = jnp.concatenate(
+            [
+                lax.dynamic_slice_in_dim(acts, core * half, half, 0),
+                lax.dynamic_slice_in_dim(acts, (1 - core) * half, half, 0),
+            ],
+            axis=0,
+        )
 
     with jax.named_scope("encode"):
         partial_pre = dot(acts, enc_weight, ((1,), (0,))).astype(BF16)
@@ -77,40 +92,46 @@
             "layer", 0, 0, tiled=True,
         )
 
+    with jax.named_scope("norms"):
+        dec_f = dec_weight.astype(F32)
+        squares = jnp.sum(dec_f * dec_f, axis=1)
+        squares, _ = lax.optimization_barrier((squares, codes_part))
+        for pairs in LAYER_STEPS:
+            squares = squares + lax.ppermute(squares, "layer", pairs)
+        norms = jnp.sqrt(squares + 1e-06)
+
     with jax.named_scope("decode"):
-        other_codes = lax.dynamic_slice_in_dim(codes, (1 - core) * half, half, 0)
-        core_codes = lax.dynamic_slice_in_dim(codes, core * half, half, 0)
-        away = dot(other_codes, dec_weight, ((1,), (0,))).astype(BF16)
+        away = dot(dec_weight, codes[half:], ((0,), (1,))).astype(BF16)
         arrived = lax.ppermute(away, "latent", CORE)
-        recon = dot(core_codes, dec_weight, ((1,), (0,))) + arrived.astype(F32)
+        recon = lax.optimization_barrier(dot(dec_weight, codes[:half], ((0,), (1,))))
+        recon = recon + arrived.astype(F32)
         got = lax.all_to_all(
             recon.astype(BF16), "latent", 0, 0, axis_index_groups=NEAR, tiled=True
         )
         own_recon = lax.dynamic_slice_in_dim(recon, near * block, block, 0)
-        recon = add_up(got.reshape(ZLO * NXL, block, feat), near, own_recon).astype(BF16)
+        recon = add_up(got.reshape(n_near, block, half), near, own_recon).astype(BF16)
         got = lax.all_to_all(
-            jnp.broadcast_to(recon, (ZHI, block, feat)).reshape(ZHI * block, feat),
+            jnp.broadcast_to(recon, (ZHI, block, half)).reshape(ZHI * block, half),
             "latent", 0, 0, axis_index_groups=FAR, tiled=True,
         )
-        recon = jnp.sum(got.reshape(ZHI, block, feat).astype(F32), axis=0) + dec_bias
-        acts_part = lax.dynamic_slice_in_dim(acts, core * half + near * block, block, 0)
+        own_bias = lax.dynamic_slice_in_dim(dec_bias, near * block, block, 0)
+        recon = jnp.sum(got.reshape(ZHI, block, half).astype(F32), axis=0) + own_bias[:, None]
+        acts_part = lax.dynamic_slice(acts, (0, near * block), (half, block)).T
         err_part = (2.0 * scale * (recon - acts_part.astype(F32))).astype(BF16)
 
     with jax.named_scope("spread_error"):
-        err_half = lax.all_to_all(
-            jnp.broadcast_to(err_part, (ZLO * NXL, block, feat)).reshape(half, feat),
+        err_own = lax.all_to_all(
+            jnp.broadcast_to(err_part, (n_near, block, half)).reshape(feat, half),
             "latent", 0, 0, axis_index_groups=NEAR, tiled=True,
         )
-        err_other = lax.ppermute(err_half, "latent", CORE)
-        first = jnp.where(core == 0, err_half, err_other)
-        second = jnp.where(core == 0, err_other, err_half)
-        err_grad = jnp.concatenate([first, second], axis=0)
+        err_other = lax.ppermute(err_own, "latent", CORE)
+        err_grad = jnp.concatenate([err_own, err_other], axis=1)
 
     with jax.named_scope("back"):
-        partial_back = dot(err_grad, dec_weight, ((1,), (1,))).astype(BF16)
+        partial_back = dot(err_grad, dec_weight, ((0,), (1,))).astype(BF16)
         got = lax.all_to_all(partial_back, "layer", 0, 0, tiled=True)
-        own_err = lax.dynamic_slice_in_dim(err_grad, me_layer * part, part, 0)
-        own_back = dot(own_err, dec_weight, ((1,), (1,)))
+        own_err = lax.dynamic_slice_in_dim(err_grad, me_layer * part, part, 1)
+        own_back = dot(own_err, dec_weight, ((0,), (1,)))
         back = add_up(got.reshape(n_layer, part, lat), me_layer, own_back)
         back = back + sparsity * scale * norms
         delta_part = (back * slope).astype(BF16)
@@ -120,9 +141,9 @@
         )
 
     with jax.named_scope("grads"):
-        grad_dec_bias = jnp.sum(err_grad.astype(F32), axis=0)
+        grad_dec_bias = jnp.sum(err_own.astype(F32), axis=1) + jnp.sum(err_other.astype(F32), axis=1)
         column = jnp.sum(codes.astype(F32), axis=0)
-        grad_dec = dot(codes, err_grad, ((0,), (0,)))
+        grad_dec = dot(codes, err_grad, ((0,), (1,)))
         grad_dec = grad_dec + (sparsity * scale * column / norms)[:, None] * dec_f
         grad_enc = dot(acts, delta, ((0,), (0,)))
         grad_enc_bias = jnp.sum(delta.astype(F32), axis=0)

time: 247 us -> 222 us (0.90)
  local copies, waits for them, and re-layouts: 19.3 us -> 5.59 us
  blocking collectives: 50.7 us -> 40.5 us
  waiting for transfers between devices: 91.8 us -> 83.2 us
  starting transfers between devices: 53 us -> 61 us
    psum x1 -> x0, blocking collectives: 28.3 us -> none  [per_device(): norms = jnp.sqrt(lax.psum(squares, 'layer') + 1e-06)]
    all_to_all x2 -> x1, waiting for transfers between devices: 38.3 us -> 19.2 us  [per_device(): lax.all_to_all(jnp.broadcast_to(recon, (ZHI, block, half)).reshape(ZHI *...]
    all_to_all x1 -> x2, blocking collectives: 22.5 us -> 40.5 us  [the longest x1 21.3 us: per_device(): lax.all_to_all(jnp.broadcast_to(codes_part, (n_layer, part, lat)).reshape...]
    ppermute x1 -> x4, waiting for transfers between devices: 2.02 us -> 18.4 us  [the longest x3 16.6 us: per_device(): squares = squares + lax.ppermute(squares, 'layer', pairs)]
    ppermute x1 -> x4, starting transfers between devices: 5.13 us -> 17.3 us  [the longest x3 11 us: per_device(): squares = squares + lax.ppermute(squares, 'layer', pairs)]
    unnamed x29 -> x18, local copies, waits for them, and re-layouts: 8.22 us -> 1.01 us
    all_to_all x2 -> x1, starting transfers between devices: 17.2 us -> 13.1 us  [per_device(): lax.all_to_all(jnp.broadcast_to(recon, (ZHI, block, half)).reshape(ZHI *...]
  transfers between devices with their start and end apart: 8 -> 10, of which waited for: 7 -> 9; matrix products, arithmetic and copies ran while one was open for 2% -> 4% of each run, Pallas kernels for 0% -> 0%
where the time goes in v2:
time: 222 us; the launch traced here: 218 us
  waiting for transfers between devices  83.2 us (37%)
  starting transfers between devices  61 us (27%)
  blocking collectives  40.5 us (18%)
  matrix products  18.2 us (8%)
  other arithmetic  8.24 us (4%)
  local copies, waits for them, and re-layouts  5.59 us (3%)
    all_to_all x1, blocking collectives, per_device(): lax.all_to_all(jnp.broadcast_to(codes_part, (n_layer, part, lat)).reshape...  21.3 us
    all_to_all x1, waiting for transfers between devices, per_device(): lax.all_to_all(jnp.broadcast_to(recon, (ZHI, block, half)).reshape(ZHI *...  19.2 us
    all_to_all x1, blocking collectives, per_device(): lax.all_to_all(jnp.broadcast_to(err_part, (n_near, block, half)).reshape(...  19.2 us
    all_to_all x1, waiting for transfers between devices, per_device(): lax.all_to_all(recon.astype(BF16), 'latent', 0, 0, axis_index_groups=NEAR...  18.3 us
    dot_general x8, matrix products, dot(): return lax.dot_general(a, b, (dims, ((), ())), preferred_element_type=F32)  18.2 us
    all_to_all x1, waiting for transfers between devices, per_device(): got = lax.all_to_all(partial_pre, 'layer', 0, 0, tiled=True)  16.6 us
    ppermute x3, waiting for transfers between devices, per_device(): squares = squares + lax.ppermute(squares, 'layer', pairs)  16.6 us
    all_to_all x1, starting transfers between devices, per_device(): lax.all_to_all(jnp.broadcast_to(recon, (ZHI, block, half)).reshape(ZHI *...  13.1 us
  transfers between devices with their start and end apart: 10, of which 9 were waited for; matrix products, arithmetic and copies ran while one was open for 4% of the time, Pallas kernels for 0%

profile of v2, /device:TPU:1, one launch (start us, length us, event | category | flops | bytes accessed | tf_op | source)
XLA Modules:
  0.0 217.5 jit_solution(6290804257052698064)
XLA Ops:
  2.2 2.3 %convolution_convert_fusion.1 = bf16[1280,512]{1,0:T(8,128)(2,1)} fusion(bf16[576,512]{1,0:T(8,128)(2,1)S(1)} %copy-done, bf16[640,576]{0,1:T(8,128)(2,1)S(1)} %get-tuple-element.8, bf16[640,576]{0,1:T(8,128)(2,1)S(1)} %get-tuple-element.9), kind=kOutput, calls=%fused_computation.1 | convolution fusion | flops 758579200 | bytes 3375104 | tf_op jit(solution)/shard_map/encode/dot_general | solution.py:48
  4.5 7.6 %all-to-all-start = ((bf16[8,160,512]{2,1,0:T(8,128)(2,1)}), bf16[8,160,512]{2,1,0:T(8,128)(2,1)}, u32[]{:S(2)}, u32[]{:S(2)}) async-start(bf16[8,160,512]{2,1,0:T(8,128)(2,1)} %bitcast.101), calls=%async_computation | async-start | bytes 2621440 | tf_op jit(solution)/shard_map/encode/all_to_all | solution.py:84
  12.1 16.6 %all-to-all-done = bf16[8,160,512]{2,1,0:T(8,128)(2,1)} async-done(((bf16[8,160,512]{2,1,0:T(8,128)(2,1)}), bf16[8,160,512]{2,1,0:T(8,128)(2,1)}, u32[]{:S(2)}, u32[]{:S(2)}) %all-to-all-start) | async-done | bytes 1310752 | tf_op jit(solution)/shard_map/encode/all_to_all | solution.py:84
  28.7 3.2 %fusion.21 = (bf16[160,512]{1,0:T(8,128)(2,1)S(1)}, f32[160,512]{1,0:T(8,128)}) fusion(f32[512]{0:T(512)S(1)} %copy-done.8, bf16[8,160,512]{2,1,0:T(8,128)(2,1)} %all-to-all-done, pred[]{:T(512)S(6)} %eq.66, pred[]{:T(512)S(6)} %eq.65, pred[]{:T(512)S(6)} %eq.64, pred[]{:T(512)S(6)} %eq.63, pred[]{:T(512)S(6)} %eq.62, pred[]{:T(512)S(6)} %eq.61, ...), kind=kOutput, calls=%fused_computation.45 | convolution fusion | flops 97361920 | bytes 3868684 | tf_op jit(solution)/shard_map/encode/dot_general | solution.py:48
  32.0 21.3 %all_to_all.60 = bf16[8,160,512]{2,1,0:T(8,128)(2,1)S(1)} all-to-all(bf16[8,160,512]{2,1,0:T(8,128)(2,1)S(1)} %broadcast_in_dim.50), channel_id=1, replica_groups=mesh['layer'=8,'latent'=64] {'layer'}, dimensions={0} | all-to-all | bytes 2621440 | tf_op jit(solution)/shard_map/encode/all_to_all | solution.py:90
  55.0 5.7 %collective-permute-start = (bf16[576,640]{1,0:T(8,128)(2,1)S(1)}, bf16[576,640]{1,0:T(8,128)(2,1)S(1)}, u32[]{:S(2)}, u32[]{:S(2)}) collective-permute-start(bf16[576,640]{1,0:T(8,128)(2,1)S(1)} %fusion), channel_id=1, source_target_pairs={{0,1},{1,0},{2,3},{3,2},{4,5},{5,4},{6,7},{7,6},{8,9},{9,8},{10,11... | collective-permute-start | bytes 2211848 | tf_op jit(solution)/shard_map/decode/ppermute | solution.py:105
  64.1 7.9 %all-to-all-start.2 = ((bf16[8,72,640]{2,1,0:T(8,128)(2,1)}), bf16[8,72,640]{2,1,0:T(8,128)(2,1)S(1)}, u32[]{:S(2)}, u32[]{:S(2)}) async-start(bf16[8,72,640]{2,1,0:T(8,128)(2,1)} %bitcast.98), calls=%async_computation.2 | async-start | bytes 1474560 | tf_op jit(solution)/shard_map/decode/all_to_all | solution.py:108
  72.0 18.3 %all-to-all-done.2 = bf16[8,72,640]{2,1,0:T(8,128)(2,1)S(1)} async-done(((bf16[8,72,640]{2,1,0:T(8,128)(2,1)}), bf16[8,72,640]{2,1,0:T(8,128)(2,1)S(1)}, u32[]{:S(2)}, u32[]{:S(2)}) %all-to-all-start.2) | async-done | bytes 737312 | tf_op jit(solution)/shard_map/decode/all_to_all | solution.py:108
  92.1 13.1 %all-to-all-start.3 = ((bf16[4,72,640]{2,1,0:T(8,128)(2,1)}), bf16[4,72,640]{2,1,0:T(8,128)(2,1)}, u32[]{:S(2)}, u32[]{:S(2)}) async-start(bf16[4,72,640]{2,1,0:T(8,128)(2,1)} %broadcast_in_dim.52), calls=%async_computation.3 | async-start | bytes 737280 | tf_op jit(solution)/shard_map/decode/all_to_all | solution.py:113
  105.9 19.2 %all-to-all-done.3 = bf16[4,72,640]{2,1,0:T(8,128)(2,1)} async-done(((bf16[4,72,640]{2,1,0:T(8,128)(2,1)}), bf16[4,72,640]{2,1,0:T(8,128)(2,1)}, u32[]{:S(2)}, u32[]{:S(2)}) %all-to-all-start.3) | async-done | bytes 368672 | tf_op jit(solution)/shard_map/decode/all_to_all | solution.py:113
  126.4 19.2 %all_to_all.61 = bf16[8,72,640]{2,1,0:T(8,128)(2,1)S(1)} all-to-all(bf16[8,72,640]{2,1,0:T(8,128)(2,1)S(1)} %broadcast_in_dim.53), channel_id=1, replica_groups={{0,2,4,6,8,10,12,14},{1,3,5,7,9,11,13,15},{16,18,20,22,24,26,28,30},{17..., dimensions={0} | all-to-all | bytes 1474560 | tf_op jit(solution)/shard_map/spread_error/all_to_all | solution.py:123
  145.7 6.3 %collective-permute-start.1 = (bf16[576,640]{1,0:T(8,128)(2,1)S(1)}, bf16[576,640]{1,0:T(8,128)(2,1)S(1)}, u32[]{:S(2)}, u32[]{:S(2)}) collective-permute-start(bf16[576,640]{1,0:T(8,128)(2,1)S(1)} %bitcast.94), channel_id=1, source_target_pairs={{0,1},{1,0},{2,3},{3,2},{4,5},{5,4},{6,7},{7,6},{8,9},{9,8},{10,11... | collective-permute-start | bytes 2211848 | tf_op jit(solution)/shard_map/spread_error/ppermute | solution.py:127
  153.8 2.3 %convolution_convert_fusion = bf16[1280,512]{1,0:T(8,128)(2,1)} fusion(bf16[512,576]{0,1:T(8,128)(2,1)S(1)} %copy-done.6, bf16[576,640]{1,0:T(8,128)(2,1)S(1)} %collective-permute-done.1, bf16[576,640]{1,0:T(8,128)(2,1)S(1)} %bitcast.95), kind=kOutput, calls=%fused_computation | convolution fusion | flops 758579200 | bytes 3375104 | tf_op jit(solution)/shard_map/back/dot_general | solution.py:48
  156.1 4.3 %all-to-all-start.5 = ((bf16[8,160,512]{2,1,0:T(8,128)(2,1)}), bf16[8,160,512]{2,1,0:T(8,128)(2,1)}, u32[]{:S(2)}, u32[]{:S(2)}) async-start(bf16[8,160,512]{2,1,0:T(8,128)(2,1)} %bitcast.100), calls=%async_computation.5 | async-start | bytes 2621440 | tf_op jit(solution)/shard_map/back/all_to_all | solution.py:132
  160.5 3.2 %collective-permute-start.2 = (f32[512]{0:T(512)S(1)}, f32[512]{0:T(512)S(1)}, u32[]{:S(2)}, u32[]{:S(2)}) collective-permute-start(f32[512]{0:T(512)S(1)} %fusion.18), channel_id=1, source_target_pairs={{0,128},{64,192},{128,0},{192,64},{256,384},{320,448},{384,256},{4... | collective-permute-start | bytes 6152 | tf_op jit(solution)/shard_map/norms/ppermute | solution.py:100
  163.8 12.2 %collective-permute-done.2 = f32[512]{0:T(512)S(1)} collective-permute-done((f32[512]{0:T(512)S(1)}, f32[512]{0:T(512)S(1)}, u32[]{:S(2)}, u32[]{:S(2)}) %collective-permute-start.2) | collective-permute-done | bytes 2080 | tf_op jit(solution)/shard_map/norms/ppermute | solution.py:100
  176.0 1.9 collective-permute-start.3
  177.9 3.6 %collective-permute-done.3 = f32[512]{0:T(512)S(1)} collective-permute-done((f32[512]{0:T(512)S(1)}, f32[512]{0:T(512)S(1)}, u32[]{:S(2)}, u32[]{:S(2)}) %collective-permute-start.3) | collective-permute-done | bytes 2080 | tf_op jit(solution)/shard_map/norms/ppermute | solution.py:100
  181.5 5.8 %collective-permute-start.4 = (f32[512]{0:T(512)S(1)}, f32[512]{0:T(512)S(1)}, u32[]{:S(2)}, u32[]{:S(2)}) collective-permute-start(f32[512]{0:T(512)S(1)} %add.187), channel_id=1, source_target_pairs={{0,64},{64,0},{128,192},{192,128},{256,320},{320,256},{384,448},{4... | collective-permute-start | bytes 6152 | tf_op jit(solution)/shard_map/norms/ppermute | solution.py:100
  188.4 2.3 %fusion.19 = bf16[160,512]{1,0:T(8,128)(2,1)S(1)} fusion(bf16[512,576]{0,1:T(8,128)(2,1)S(1)} %copy-done.6, f32[160,512]{1,0:T(8,128)} %get-tuple-element.15, s32[]{:T(128)S(6)} %select_n.241, bf16[576,640]{1,0:T(8,128)(2,1)S(1)} %bitcast.96, bf16[576,640]{1,0:T(8,128)(2,1)} %copy-done.7, bf16[8,160,512]{2,1,0:T(8,128)(2,1)} %all-to-all-done.5, ...), kind=kOutput, calls=%fused_computation.41 | convolution fusion | flops 97198080 | bytes 3868684 | tf_op jit(solution)/shard_map/back/dot_general | solution.py:48
  191.9 5.1 %all-to-all-start.6 = ((bf16[8,160,512]{2,1,0:T(8,128)(2,1)}), bf16[8,160,512]{2,1,0:T(8,128)(2,1)S(1)}, u32[]{:S(2)}, u32[]{:S(2)}) async-start(bf16[8,160,512]{2,1,0:T(8,128)(2,1)} %broadcast_in_dim.54), calls=%async_computation.6 | async-start | bytes 2621440 | tf_op jit(solution)/shard_map/back/all_to_all | solution.py:138
  200.4 3.5 %convolution_add_fusion = f32[512,576]{0,1:T(8,128)} fusion(bf16[1280,512]{1,0:T(8,128)(2,1)S(1)} %bitcast.92, bf16[512,576]{0,1:T(8,128)(2,1)} %param.8, bf16[576,640]{1,0:T(8,128)(2,1)} %copy-done.7, bf16[576,640]{1,0:T(8,128)(2,1)} %bitcast.97, f32[512]{0:T(512)S(1)} %get-tuple-element.12), kind=kOutput, calls=%fused_computation.18 | convolution fusion | flops 758808576 | bytes 4556800 | tf_op jit(solution)/shard_map/grads/dot_general | solution.py:48
  203.9 9.5 %all-to-all-done.6 = bf16[8,160,512]{2,1,0:T(8,128)(2,1)S(1)} async-done(((bf16[8,160,512]{2,1,0:T(8,128)(2,1)}), bf16[8,160,512]{2,1,0:T(8,128)(2,1)S(1)}, u32[]{:S(2)}, u32[]{:S(2)}) %all-to-all-start.6) | async-done | bytes 1310752 | tf_op jit(solution)/shard_map/back/all_to_all | solution.py:138
  213.4 3.3 %fusion.20 = f32[576,512]{1,0:T(8,128)} fusion(bf16[1280,512]{1,0:T(8,128)(2,1)S(1)} %bitcast.93, bf16[640,576]{0,1:T(8,128)(2,1)} %copy-done.1, bf16[640,576]{0,1:T(8,128)(2,1)} %copy-done.2), kind=kOutput, calls=%fused_computation.43 | convolution fusion | flops 757923840 | bytes 3964928 | tf_op jit(solution)/shard_map/grads/dot_general | solution.py:48
  (45 shorter events, 18.8 us)
Async XLA Ops:
  0.6 1.6 copy-start
  2.2 26.5 %copy-start.2 = (bf16[640,576]{0,1:T(8,128)(2,1)}, bf16[640,576]{0,1:T(8,128)(2,1)S(1)}, u32[]{:S(2)}) copy-start(bf16[640,576]{0,1:T(8,128)(2,1)S(1)} %get-tuple-element.9) | copy-start | bytes 2211844
  2.2 124.0 %copy-start.1 = (bf16[640,576]{0,1:T(8,128)(2,1)}, bf16[640,576]{0,1:T(8,128)(2,1)S(1)}, u32[]{:S(2)}) copy-start(bf16[640,576]{0,1:T(8,128)(2,1)S(1)} %get-tuple-element.8) | copy-start | bytes 2211844
  4.5 24.2 %copy-start.8 = (f32[512]{0:T(512)S(1)}, f32[512]{0:T(512)}, u32[]{:S(2)}) copy-start(f32[512]{0:T(512)} %param.7) | copy-start | bytes 6148
  4.5 24.2 %all-to-all-start = ((bf16[8,160,512]{2,1,0:T(8,128)(2,1)}), bf16[8,160,512]{2,1,0:T(8,128)(2,1)}, u32[]{:S(2)}, u32[]{:S(2)}) async-start(bf16[8,160,512]{2,1,0:T(8,128)(2,1)} %bitcast.101), calls=%async_computation | async-start | bytes 2621440 | tf_op jit(solution)/shard_map/encode/all_to_all | solution.py:84
  53.3 1.1 copy-start.5
  55.0 7.6 %collective-permute-start = (bf16[576,640]{1,0:T(8,128)(2,1)S(1)}, bf16[576,640]{1,0:T(8,128)(2,1)S(1)}, u32[]{:S(2)}, u32[]{:S(2)}) collective-permute-start(bf16[576,640]{1,0:T(8,128)(2,1)S(1)} %fusion), channel_id=1, source_target_pairs={{0,1},{1,0},{2,3},{3,2},{4,5},{5,4},{6,7},{7,6},{8,9},{9,8},{10,11... | collective-permute-start | bytes 2211848 | tf_op jit(solution)/shard_map/decode/ppermute | solution.py:105
  64.1 26.2 %all-to-all-start.2 = ((bf16[8,72,640]{2,1,0:T(8,128)(2,1)}), bf16[8,72,640]{2,1,0:T(8,128)(2,1)S(1)}, u32[]{:S(2)}, u32[]{:S(2)}) async-start(bf16[8,72,640]{2,1,0:T(8,128)(2,1)} %bitcast.98), calls=%async_computation.2 | async-start | bytes 1474560 | tf_op jit(solution)/shard_map/decode/all_to_all | solution.py:108
  91.3 34.9 %copy-start.3 = (bf16[640,576]{0,1:T(8,128)(2,1)S(1)}, bf16[640,576]{0,1:T(8,128)(2,1)}, u32[]{:S(2)}) copy-start(bf16[640,576]{0,1:T(8,128)(2,1)} %copy-done.2) | copy-start | bytes 2211844
  92.1 33.1 %all-to-all-start.3 = ((bf16[4,72,640]{2,1,0:T(8,128)(2,1)}), bf16[4,72,640]{2,1,0:T(8,128)(2,1)}, u32[]{:S(2)}, u32[]{:S(2)}) async-start(bf16[4,72,640]{2,1,0:T(8,128)(2,1)} %broadcast_in_dim.52), calls=%async_computation.3 | async-start | bytes 737280 | tf_op jit(solution)/shard_map/decode/all_to_all | solution.py:113
  126.4 27.5 %copy-start.6 = (bf16[512,576]{0,1:T(8,128)(2,1)S(1)}, bf16[512,576]{0,1:T(8,128)(2,1)}, u32[]{:S(2)}) copy-start(bf16[512,576]{0,1:T(8,128)(2,1)} %param.8) | copy-start | bytes 1769476
  145.7 42.7 %copy-start.4 = (bf16[8,72,640]{2,1,0:T(8,128)(2,1)}, bf16[8,72,640]{2,1,0:T(8,128)(2,1)S(1)}, u32[]{:S(2)}) copy-start(bf16[8,72,640]{2,1,0:T(8,128)(2,1)S(1)} %all_to_all.61) | copy-start | bytes 2211844
  145.7 8.2 %collective-permute-start.1 = (bf16[576,640]{1,0:T(8,128)(2,1)S(1)}, bf16[576,640]{1,0:T(8,128)(2,1)S(1)}, u32[]{:S(2)}, u32[]{:S(2)}) collective-permute-start(bf16[576,640]{1,0:T(8,128)(2,1)S(1)} %bitcast.94), channel_id=1, source_target_pairs={{0,1},{1,0},{2,3},{3,2},{4,5},{5,4},{6,7},{7,6},{8,9},{9,8},{10,11... | collective-permute-start | bytes 2211848 | tf_op jit(solution)/shard_map/spread_error/ppermute | solution.py:127
  153.8 2.3 %copy-start.7 = (bf16[576,640]{1,0:T(8,128)(2,1)}, bf16[576,640]{1,0:T(8,128)(2,1)S(1)}, u32[]{:S(2)}) copy-start(bf16[576,640]{1,0:T(8,128)(2,1)S(1)} %collective-permute-done.1) | copy-start | bytes 2211844
  156.1 32.3 %all-to-all-start.5 = ((bf16[8,160,512]{2,1,0:T(8,128)(2,1)}), bf16[8,160,512]{2,1,0:T(8,128)(2,1)}, u32[]{:S(2)}, u32[]{:S(2)}) async-start(bf16[8,160,512]{2,1,0:T(8,128)(2,1)} %bitcast.100), calls=%async_computation.5 | async-start | bytes 2621440 | tf_op jit(solution)/shard_map/back/all_to_all | solution.py:132
  160.5 15.5 %collective-permute-start.2 = (f32[512]{0:T(512)S(1)}, f32[512]{0:T(512)S(1)}, u32[]{:S(2)}, u32[]{:S(2)}) collective-permute-start(f32[512]{0:T(512)S(1)} %fusion.18), channel_id=1, source_target_pairs={{0,128},{64,192},{128,0},{192,64},{256,384},{320,448},{384,256},{4... | collective-permute-start | bytes 6152 | tf_op jit(solution)/shard_map/norms/ppermute | solution.py:100
  176.0 5.5 %collective-permute-start.3 = (f32[512]{0:T(512)S(1)}, f32[512]{0:T(512)S(1)}, u32[]{:S(2)}, u32[]{:S(2)}) collective-permute-start(f32[512]{0:T(512)S(1)} %add.186), channel_id=1, source_target_pairs={{0,384},{64,448},{128,256},{192,320},{256,128},{320,192},{384,0},{... | collective-permute-start | bytes 6152 | tf_op jit(solution)/shard_map/norms/ppermute | solution.py:100
  181.5 6.8 %collective-permute-start.4 = (f32[512]{0:T(512)S(1)}, f32[512]{0:T(512)S(1)}, u32[]{:S(2)}, u32[]{:S(2)}) collective-permute-start(f32[512]{0:T(512)S(1)} %add.187), channel_id=1, source_target_pairs={{0,64},{64,0},{128,192},{192,128},{256,320},{320,256},{384,448},{4... | collective-permute-start | bytes 6152 | tf_op jit(solution)/shard_map/norms/ppermute | solution.py:100
  191.9 21.5 %all-to-all-start.6 = ((bf16[8,160,512]{2,1,0:T(8,128)(2,1)}), bf16[8,160,512]{2,1,0:T(8,128)(2,1)S(1)}, u32[]{:S(2)}, u32[]{:S(2)}) async-start(bf16[8,160,512]{2,1,0:T(8,128)(2,1)} %broadcast_in_dim.54), calls=%async_computation.6 | async-start | bytes 2621440 | tf_op jit(solution)/shard_map/back/all_to_all | solution.py:138

commit v3 on v2

v3 whole, which is shorter than its diff:
```python
import jax
import jax.numpy as jnp
from jax import lax
from jax.sharding import PartitionSpec as P

NZ, NXL, NC = 16, 2, 2
NY, NXH = 4, 2
ZLO = 4
ZHI = NZ // ZLO


def latent_index(z, xl, c):
    return (z * NXL + xl) * NC + c


def layer_index(y, xh):
    return y * NXH + xh


NEAR = [
    [latent_index((zh * ZLO + zl - 2 * c) % NZ, xl, c) for zl in range(ZLO) for xl in range(NXL)]
    for zh in range(ZHI)
    for c in range(NC)
]
FAR = [
    [latent_index(zh * ZLO + zl, xl, c) for zh in range(ZHI)]
    for zl in range(ZLO)
    for xl in range(NXL)
    for c in range(NC)
]
CORE = [
    (latent_index(z, xl, c), latent_index(z, xl, 1 - c))
    for z in range(NZ)
    for xl in range(NXL)
    for c in range(NC)
]
LAYER_STEPS = [
    [(layer_index(y, xh), layer_index(y ^ 1, xh)) for y in range(NY) for xh in range(NXH)],
    [(layer_index(y, xh), layer_index(3 - y, xh)) for y in range(NY) for xh in range(NXH)],
    [(layer_index(y, xh), layer_index(y, 1 - xh)) for y in range(NY) for xh in range(NXH)],
]

F32 = jnp.float32
BF16 = jnp.bfloat16


def dot(a, b, dims):
    return lax.dot_general(a, b, (dims, ((), ())), preferred_element_type=F32)


def add_up(blocks, me, own):
    total = own
    for j in range(blocks.shape[0]):
        total = total + jnp.where(me == j, 0.0, blocks[j].astype(F32))
    return total


def spread(x, n):
    return jnp.broadcast_to(x, (n,) + x.shape).reshape((n * x.shape[0],) + x.shape[1:])


def per_device(acts, enc_weight, enc_bias, dec_weight, dec_bias):
    rows, feat = acts.shape
    lat = enc_weight.shape[1]
    scale = 1.0 / jnp.sqrt(F32(rows))
    sparsity = 1.0
    me_layer = lax.axis_index("layer")
    me_latent = lax.axis_index("latent")
    n_layer = NY * NXH
    n_near = ZLO * NXL
    part = lat // n_layer
    core = lax.rem(me_latent, NC)
    x_lo = lax.rem(lax.div(me_latent, NC), NXL)
    z = lax.div(me_latent, NC * NXL)
    near = lax.rem(z + 2 * core, ZLO) * NXL + x_lo
    half = rows // NC
    block = feat // n_near

    with jax.named_scope("local_rows"):
        acts_t = acts.T
        acts_t = jnp.concatenate(
            [
                lax.dynamic_slice_in_dim(acts_t, core * half, half, 1),
                lax.dynamic_slice_in_dim(acts_t, (1 - core) * half, half, 1),
            ],
            axis=1,
        )
        dec_t = dec_weight.T

    with jax.named_scope("encode"):
        partial_pre = dot(enc_weight, acts_t, ((0,), (0,))).astype(BF16)
        got = lax.all_to_all(partial_pre, "layer", 0, 0, tiled=True)
        own_enc = lax.dynamic_slice_in_dim(enc_weight, me_layer * part, part, 1)
        own_pre = lax.optimization_barrier(dot(own_enc, acts_t, ((0,), (0,))))
        own_bias = lax.dynamic_slice_in_dim(enc_bias, me_layer * part, part, 0)
        pre = add_up(got.reshape(n_layer, part, rows), me_layer, own_pre) + own_bias[:, None]
        codes_part = jax.nn.softplus(pre).astype(BF16)
        slope = jax.nn.sigmoid(pre)
        codes = lax.all_to_all(spread(codes_part, n_layer), "layer", 0, 0, tiled=True)

    with jax.named_scope("decode"):
        away = dot(dec_t, codes[:, half:], ((1,), (0,))).astype(BF16)
        arrived = lax.ppermute(away, "latent", CORE)
        recon = lax.optimization_barrier(dot(dec_t, codes[:, :half], ((1,), (0,))))
        recon = recon + arrived.astype(F32)
        got = lax.all_to_all(
            recon.astype(BF16), "latent", 0, 0, axis_index_groups=NEAR, tiled=True
        )
        own_recon = lax.dynamic_slice_in_dim(recon, near * block, block, 0)
        recon = add_up(got.reshape(n_near, block, half), near, own_recon).astype(BF16)

    with jax.named_scope("norms"):
        dec_f = dec_t.astype(F32)
        squares = jnp.sum(dec_f * dec_f, axis=0)
        squares, recon = lax.optimization_barrier((squares, recon))
        for pairs in LAYER_STEPS:
            squares = squares + lax.ppermute(squares, "layer", pairs)
        norms = jnp.sqrt(squares + 1e-06)

    with jax.named_scope("error"):
        got = lax.all_to_all(
            spread(recon, ZHI), "latent", 0, 0, axis_index_groups=FAR, tiled=True
        )
        own_dec_bias = lax.dynamic_slice_in_dim(dec_bias, near * block, block, 0)
        acts_part = lax.dynamic_slice(acts_t, (near * block, 0), (block, half))
        recon = jnp.sum(got.reshape(ZHI, block, half).astype(F32), axis=0) + own_dec_bias[:, None]
        err_part = (2.0 * scale * (recon - acts_part.astype(F32))).astype(BF16)
        err_part, norms = lax.optimization_barrier((err_part, norms))
        err_own = lax.all_to_all(
            spread(err_part, n_near), "latent", 0, 0, axis_index_groups=NEAR, tiled=True
        )
        err_other = lax.ppermute(err_own, "latent", CORE)
        err_t = jnp.concatenate([err_own, err_other], axis=1)

    with jax.named_scope("back"):
        partial_back = dot(dec_t, err_t, ((0,), (0,))).astype(BF16)
        got = lax.all_to_all(partial_back, "layer", 0, 0, tiled=True)
        own_dec = lax.dynamic_slice_in_dim(dec_t, me_layer * part, part, 1)
        own_back = lax.optimization_barrier(dot(own_dec, err_t, ((0,), (0,))))
        own_norms = lax.dynamic_slice_in_dim(norms, me_layer * part, part, 0)
        back = add_up(got.reshape(n_layer, part, rows), me_layer, own_back)
        back = back + (sparsity * scale * own_norms)[:, None]
        delta_part = (back * slope).astype(BF16)
        delta = lax.all_to_all(spread(delta_part, n_layer), "layer", 0, 0, tiled=True)

    with jax.named_scope("grads"):
        grad_dec_bias = jnp.sum(err_own.astype(F32), axis=1) + jnp.sum(err_other.astype(F32), axis=1)
        column = jnp.sum(codes.astype(F32), axis=1)
        grad_dec = dot(err_t, codes, ((1,), (1,)))
        grad_dec = grad_dec + (sparsity * scale * column / norms)[None, :] * dec_f
        grad_enc = dot(acts_t, delta, ((1,), (1,)))
        grad_enc_bias = jnp.sum(delta.astype(F32), axis=1)
    return (grad_enc, grad_enc_bias, grad_dec.T, grad_dec_bias)


def solution(mesh):
    return jax.shard_map(
        per_device,
        mesh=mesh,
        in_specs=(
            P(None, "layer"),
            P("layer", "latent"),
            P("latent"),
            P("latent", "layer"),
            P("layer"),
        ),
        out_specs=(P("layer", "latent"), P("latent"), P("latent", "layer"), P("layer")),
        check_vma=False,
    )
```

time: 222 us -> 204 us (0.919)
  waiting for transfers between devices: 83.2 us -> 71.7 us
  starting transfers between devices: 61 us -> 53.5 us
  other arithmetic: 8.24 us -> 12.2 us
    all_to_all x1, waiting for transfers between devices: 0.01 us -> 16.7 us  [per_device(): got = lax.all_to_all(partial_back, 'layer', 0, 0, tiled=True)]
    all_to_all x2, waiting for transfers between devices: 28.8 us -> 16 us  [the longest x1 11 us: per_device(): lax.all_to_all(spread(delta_part, n_layer), 'layer', 0, 0, tiled=True)]
    ppermute x3, waiting for transfers between devices: 16.6 us -> 8.45 us  [per_device(): squares = squares + lax.ppermute(squares, 'layer', pairs)]
    all_to_all x2, starting transfers between devices: 18.2 us -> 10.4 us  [the longest x1 6.86 us: per_device(): lax.all_to_all(spread(recon, ZHI), 'latent', 0, 0, axis_index_groups=FAR,...]
    all_to_all x1, starting transfers between devices: 7.91 us -> 15.4 us  [per_device(): lax.all_to_all(recon.astype(BF16), 'latent', 0, 0, axis_index_groups=NEAR...]
    all_to_all x1, waiting for transfers between devices: 18.3 us -> 12.3 us  [per_device(): lax.all_to_all(recon.astype(BF16), 'latent', 0, 0, axis_index_groups=NEAR...]
    ppermute x3, starting transfers between devices: 11 us -> 7.23 us  [per_device(): squares = squares + lax.ppermute(squares, 'layer', pairs)]
    convert_element_type x0 -> x2, other arithmetic: none -> 3.42 us  [the longest x1 2.12 us: per_device(): codes_part = jax.nn.softplus(pre).astype(BF16)]
  transfers between devices with their start and end apart: 10 -> 10, of which waited for: 9 -> 10; matrix products, arithmetic and copies ran while one was open for 4% -> 7% of each run, Pallas kernels for 0% -> 0%
where the time goes in v3:
time: 204 us; the launch traced here: 202 us
  waiting for transfers between devices  71.7 us (35%)
  starting transfers between devices  53.5 us (26%)
  blocking collectives  40.9 us (20%)
  matrix products  16.6 us (8%)
  other arithmetic  12.2 us (6%)
  local copies, waits for them, and re-layouts  5.95 us (3%)
    all_to_all x1, blocking collectives, per_device(): lax.all_to_all(spread(codes_part, n_layer), 'layer', 0, 0, tiled=True)  20.5 us
    all_to_all x1, blocking collectives, per_device(): lax.all_to_all(spread(err_part, n_near), 'latent', 0, 0, axis_index_group...  20.4 us
    all_to_all x1, waiting for transfers between devices, per_device(): got = lax.all_to_all(partial_back, 'layer', 0, 0, tiled=True)  16.7 us
    dot_general x8, matrix products, dot(): return lax.dot_general(a, b, (dims, ((), ())), preferred_element_type=F32)  16.6 us
    all_to_all x1, starting transfers between devices, per_device(): lax.all_to_all(recon.astype(BF16), 'latent', 0, 0, axis_index_groups=NEAR...  15.4 us
    all_to_all x1, waiting for transfers between devices, per_device(): got = lax.all_to_all(partial_pre, 'layer', 0, 0, tiled=True)  15.1 us
    all_to_all x1, waiting for transfers between devices, per_device(): lax.all_to_all(recon.astype(BF16), 'latent', 0, 0, axis_index_groups=NEAR...  12.3 us
    all_to_all x1, waiting for transfers between devices, per_device(): lax.all_to_all(spread(delta_part, n_layer), 'layer', 0, 0, tiled=True)  11 us
  transfers between devices with their start and end apart: 10, of which 10 were waited for; matrix products, arithmetic and copies ran while one was open for 7% of the time, Pallas kernels for 0%

profile of v3, /device:TPU:1, one launch (start us, length us, event | category | flops | bytes accessed | tf_op | source)
XLA Modules:
  0.0 201.7 jit_solution(10011942607512409528)
XLA Ops:
  2.2 2.3 %convolution_convert_fusion.1 = bf16[1280,512]{0,1:T(8,128)(2,1)} fusion(bf16[576,512]{1,0:T(8,128)(2,1)S(1)} %copy-done, bf16[576,640]{1,0:T(8,128)(2,1)S(1)} %get-tuple-element.17, bf16[576,640]{1,0:T(8,128)(2,1)S(1)} %get-tuple-element.16), kind=kOutput, calls=%fused_computation.1 | convolution fusion | flops 758579200 | bytes 3375104 | tf_op jit(solution)/shard_map/encode/dot_general | solution.py:48
  4.5 7.5 %all-to-all-start = ((bf16[8,64,1280]{2,1,0:T(8,128)(2,1)}), bf16[8,64,1280]{2,1,0:T(8,128)(2,1)S(1)}, u32[]{:S(2)}, u32[]{:S(2)}) async-start(bf16[8,64,1280]{2,1,0:T(8,128)(2,1)} %bitcast.141), calls=%async_computation | async-start | bytes 2621440 | tf_op jit(solution)/shard_map/encode/all_to_all | solution.py:92
  14.0 15.1 %all-to-all-done = bf16[8,64,1280]{2,1,0:T(8,128)(2,1)S(1)} async-done(((bf16[8,64,1280]{2,1,0:T(8,128)(2,1)}), bf16[8,64,1280]{2,1,0:T(8,128)(2,1)S(1)}, u32[]{:S(2)}, u32[]{:S(2)}) %all-to-all-start) | async-done | bytes 1310752 | tf_op jit(solution)/shard_map/encode/all_to_all | solution.py:92
  31.4 20.5 %all_to_all.60 = bf16[8,64,1280]{2,1,0:T(8,128)(2,1)S(1)} all-to-all(bf16[8,64,1280]{2,1,0:T(8,128)(2,1)S(1)} %broadcast_in_dim.50), channel_id=1, replica_groups=mesh['layer'=8,'latent'=64] {'layer'}, dimensions={0} | all-to-all | bytes 2621440 | tf_op jit(solution)/shard_map/encode/all_to_all | solution.py:99
  52.5 5.8 %collective-permute-start = (bf16[576,640]{1,0:T(8,128)(2,1)S(1)}, bf16[576,640]{1,0:T(8,128)(2,1)S(1)}, u32[]{:S(2)}, u32[]{:S(2)}) collective-permute-start(bf16[576,640]{1,0:T(8,128)(2,1)S(1)} %fusion), channel_id=1, source_target_pairs={{0,1},{1,0},{2,3},{3,2},{4,5},{5,4},{6,7},{7,6},{8,9},{9,8},{10,11... | collective-permute-start | bytes 2211848 | tf_op jit(solution)/shard_map/decode/ppermute | solution.py:103
  61.7 15.4 %all-to-all-start.2 = ((bf16[8,72,640]{2,1,0:T(8,128)(2,1)}), bf16[8,72,640]{2,1,0:T(8,128)(2,1)S(1)}, u32[]{:S(2)}, u32[]{:S(2)}) async-start(bf16[8,72,640]{2,1,0:T(8,128)(2,1)} %bitcast.136), calls=%async_computation.2 | async-start | bytes 1474560 | tf_op jit(solution)/shard_map/decode/all_to_all | solution.py:106
  78.3 12.3 %all-to-all-done.2 = bf16[8,72,640]{2,1,0:T(8,128)(2,1)S(1)} async-done(((bf16[8,72,640]{2,1,0:T(8,128)(2,1)}), bf16[8,72,640]{2,1,0:T(8,128)(2,1)S(1)}, u32[]{:S(2)}, u32[]{:S(2)}) %all-to-all-start.2) | async-done | bytes 737312 | tf_op jit(solution)/shard_map/decode/all_to_all | solution.py:106
  92.5 6.9 %all-to-all-start.3 = ((bf16[4,72,640]{2,1,0:T(8,128)(2,1)}), bf16[4,72,640]{2,1,0:T(8,128)(2,1)}, u32[]{:S(2)}, u32[]{:S(2)}) async-start(bf16[4,72,640]{2,1,0:T(8,128)(2,1)} %broadcast_in_dim.52), calls=%async_computation.3 | async-start | bytes 737280 | tf_op jit(solution)/shard_map/error/all_to_all | solution.py:121
  101.2 2.4 %collective-permute-done.1 = f32[512]{0:T(512)S(1)} collective-permute-done((f32[512]{0:T(512)S(1)}, f32[512]{0:T(512)S(1)}, u32[]{:S(2)}, u32[]{:S(2)}) %collective-permute-start.1) | collective-permute-done | bytes 2080 | tf_op jit(solution)/shard_map/norms/ppermute | solution.py:117
  103.6 2.4 %collective-permute-start.2 = (f32[512]{0:T(512)S(1)}, f32[512]{0:T(512)S(1)}, u32[]{:S(2)}, u32[]{:S(2)}) collective-permute-start(f32[512]{0:T(512)S(1)} %add.179), channel_id=1, source_target_pairs={{0,384},{64,448},{128,256},{192,320},{256,128},{320,192},{384,0},{... | collective-permute-start | bytes 6152 | tf_op jit(solution)/shard_map/norms/ppermute | solution.py:117
  106.0 3.6 %collective-permute-done.2 = f32[512]{0:T(512)S(1)} collective-permute-done((f32[512]{0:T(512)S(1)}, f32[512]{0:T(512)S(1)}, u32[]{:S(2)}, u32[]{:S(2)}) %collective-permute-start.2) | collective-permute-done | bytes 2080 | tf_op jit(solution)/shard_map/norms/ppermute | solution.py:117
  109.6 2.9 %collective-permute-start.3 = (f32[512]{0:T(512)S(1)}, f32[512]{0:T(512)S(1)}, u32[]{:S(2)}, u32[]{:S(2)}) collective-permute-start(f32[512]{0:T(512)S(1)} %add.180), channel_id=1, source_target_pairs={{0,64},{64,0},{128,192},{192,128},{256,320},{320,256},{384,448},{4... | collective-permute-start | bytes 6152 | tf_op jit(solution)/shard_map/norms/ppermute | solution.py:117
  113.3 2.5 %collective-permute-done.3 = f32[512]{0:T(512)S(1)} collective-permute-done((f32[512]{0:T(512)S(1)}, f32[512]{0:T(512)S(1)}, u32[]{:S(2)}, u32[]{:S(2)}) %collective-permute-start.3) | collective-permute-done | bytes 2080 | tf_op jit(solution)/shard_map/norms/ppermute | solution.py:117
  115.8 5.0 %all-to-all-done.3 = bf16[4,72,640]{2,1,0:T(8,128)(2,1)} async-done(((bf16[4,72,640]{2,1,0:T(8,128)(2,1)}), bf16[4,72,640]{2,1,0:T(8,128)(2,1)}, u32[]{:S(2)}, u32[]{:S(2)}) %all-to-all-start.3) | async-done | bytes 368672 | tf_op jit(solution)/shard_map/error/all_to_all | solution.py:121
  122.1 20.4 %all_to_all.61 = bf16[8,72,640]{2,1,0:T(8,128)(2,1)S(1)} all-to-all(bf16[8,72,640]{2,1,0:T(8,128)(2,1)S(1)} %broadcast_in_dim.53), channel_id=1, replica_groups={{0,2,4,6,8,10,12,14},{57,59,61,63,1,3,5,7},{16,18,20,22,24,26,28,30},{9..., dimensions={0} | all-to-all | bytes 1474560 | tf_op jit(solution)/shard_map/error/all_to_all | solution.py:129
  142.5 3.6 %collective-permute-start.4 = (bf16[576,640]{1,0:T(8,128)(2,1)S(1)}, bf16[576,640]{1,0:T(8,128)(2,1)S(1)}, u32[]{:S(2)}, u32[]{:S(2)}) collective-permute-start(bf16[576,640]{1,0:T(8,128)(2,1)S(1)} %bitcast.137), channel_id=1, source_target_pairs={{0,1},{1,0},{2,3},{3,2},{4,5},{5,4},{6,7},{7,6},{8,9},{9,8},{10,11... | collective-permute-start | bytes 2211848 | tf_op jit(solution)/shard_map/error/ppermute | solution.py:132
  147.9 2.3 %convolution_convert_fusion = bf16[1280,512]{0,1:T(8,128)(2,1)} fusion(bf16[512,576]{0,1:T(8,128)(2,1)S(1)} %copy-done.6, bf16[576,640]{1,0:T(8,128)(2,1)S(1)} %collective-permute-done.4, bf16[576,640]{1,0:T(8,128)(2,1)S(1)} %bitcast.138), kind=kOutput, calls=%fused_computation | convolution fusion | flops 758579200 | bytes 3375104 | tf_op jit(solution)/shard_map/back/dot_general | solution.py:48
  150.3 3.6 %all-to-all-start.5 = ((bf16[8,64,1280]{2,1,0:T(8,128)(2,1)}), bf16[8,64,1280]{2,1,0:T(8,128)(2,1)S(1)}, u32[]{:S(2)}, u32[]{:S(2)}) async-start(bf16[8,64,1280]{2,1,0:T(8,128)(2,1)} %bitcast.142), calls=%async_computation.5 | async-start | bytes 2621440 | tf_op jit(solution)/shard_map/back/all_to_all | solution.py:137
  153.9 2.7 %fusion.4 = f32[64,1280]{1,0:T(8,128)} fusion(bf16[576,640]{1,0:T(8,128)(2,1)} %copy-done.8, bf16[576,640]{1,0:T(8,128)(2,1)} %bitcast.139, bf16[512,576]{0,1:T(8,128)(2,1)} %param.8, s32[]{:T(128)S(6)} %select_n.227), kind=kOutput, calls=%fused_computation.24 | convolution fusion | flops 97320960 | bytes 1949700 | tf_op jit(solution)/shard_map/back/dot_general | solution.py:48
  156.6 16.7 %all-to-all-done.5 = bf16[8,64,1280]{2,1,0:T(8,128)(2,1)S(1)} async-done(((bf16[8,64,1280]{2,1,0:T(8,128)(2,1)}), bf16[8,64,1280]{2,1,0:T(8,128)(2,1)S(1)}, u32[]{:S(2)}, u32[]{:S(2)}) %all-to-all-start.5) | async-done | bytes 1310752 | tf_op jit(solution)/shard_map/back/all_to_all | solution.py:137
  175.7 3.6 %all-to-all-start.6 = ((bf16[8,64,1280]{2,1,0:T(8,128)(2,1)}), bf16[8,64,1280]{2,1,0:T(8,128)(2,1)S(1)}, u32[]{:S(2)}, u32[]{:S(2)}) async-start(bf16[8,64,1280]{2,1,0:T(8,128)(2,1)} %broadcast_in_dim.54), calls=%async_computation.6 | async-start | bytes 2621440 | tf_op jit(solution)/shard_map/back/all_to_all | solution.py:144
  183.0 3.5 %convolution_add_fusion = f32[512,576]{0,1:T(8,128)} fusion(bf16[512,1280]{1,0:T(8,128)(2,1)S(1)} %bitcast.134, bf16[512,576]{0,1:T(8,128)(2,1)} %param.8, f32[512]{0:T(512)S(1)} %div.27, bf16[576,640]{1,0:T(8,128)(2,1)} %copy-done.8, bf16[576,640]{1,0:T(8,128)(2,1)} %bitcast.140), kind=kOutput, calls=%fused_computation.14 | convolution fusion | flops 758808576 | bytes 4556800 | tf_op jit(solution)/shard_map/grads/dot_general | solution.py:48
  186.5 11.0 %all-to-all-done.6 = bf16[8,64,1280]{2,1,0:T(8,128)(2,1)S(1)} async-done(((bf16[8,64,1280]{2,1,0:T(8,128)(2,1)}), bf16[8,64,1280]{2,1,0:T(8,128)(2,1)S(1)}, u32[]{:S(2)}, u32[]{:S(2)}) %all-to-all-start.6) | async-done | bytes 1310752 | tf_op jit(solution)/shard_map/back/all_to_all | solution.py:144
  197.5 3.3 %fusion.5 = f32[576,512]{1,0:T(8,128)} fusion(bf16[512,1280]{1,0:T(8,128)(2,1)S(1)} %bitcast.135, bf16[576,640]{1,0:T(8,128)(2,1)} %copy-done.2, bf16[576,640]{1,0:T(8,128)(2,1)} %copy-done.1), kind=kOutput, calls=%fused_computation.25 | convolution fusion | flops 757923840 | bytes 3964928 | tf_op jit(solution)/shard_map/grads/dot_general | solution.py:48
  (52 shorter events, 25.6 us)
Async XLA Ops:
  0.6 1.6 copy-start
  2.2 9.8 %copy-start.2 = (bf16[576,640]{1,0:T(8,128)(2,1)}, bf16[576,640]{1,0:T(8,128)(2,1)S(1)}, u32[]{:S(2)}) copy-start(bf16[576,640]{1,0:T(8,128)(2,1)S(1)} %get-tuple-element.17) | copy-start | bytes 2211844
  2.2 119.7 %copy-start.1 = (bf16[576,640]{1,0:T(8,128)(2,1)}, bf16[576,640]{1,0:T(8,128)(2,1)S(1)}, u32[]{:S(2)}) copy-start(bf16[576,640]{1,0:T(8,128)(2,1)S(1)} %get-tuple-element.16) | copy-start | bytes 2211844
  4.5 24.6 %all-to-all-start = ((bf16[8,64,1280]{2,1,0:T(8,128)(2,1)}), bf16[8,64,1280]{2,1,0:T(8,128)(2,1)S(1)}, u32[]{:S(2)}, u32[]{:S(2)}) async-start(bf16[8,64,1280]{2,1,0:T(8,128)(2,1)} %bitcast.141), calls=%async_computation | async-start | bytes 2621440 | tf_op jit(solution)/shard_map/encode/all_to_all | solution.py:92
  31.3 20.5 %copy-start.5 = (bf16[512,576]{0,1:T(8,128)(2,1)S(1)}, bf16[512,576]{0,1:T(8,128)(2,1)}, u32[]{:S(2)}) copy-start(bf16[512,576]{0,1:T(8,128)(2,1)} %param.8) | copy-start | bytes 1769476
  52.5 7.7 %collective-permute-start = (bf16[576,640]{1,0:T(8,128)(2,1)S(1)}, bf16[576,640]{1,0:T(8,128)(2,1)S(1)}, u32[]{:S(2)}, u32[]{:S(2)}) collective-permute-start(bf16[576,640]{1,0:T(8,128)(2,1)S(1)} %fusion), channel_id=1, source_target_pairs={{0,1},{1,0},{2,3},{3,2},{4,5},{5,4},{6,7},{7,6},{8,9},{9,8},{10,11... | collective-permute-start | bytes 2211848 | tf_op jit(solution)/shard_map/decode/ppermute | solution.py:103
  61.7 28.9 %all-to-all-start.2 = ((bf16[8,72,640]{2,1,0:T(8,128)(2,1)}), bf16[8,72,640]{2,1,0:T(8,128)(2,1)S(1)}, u32[]{:S(2)}, u32[]{:S(2)}) async-start(bf16[8,72,640]{2,1,0:T(8,128)(2,1)} %bitcast.136), calls=%async_computation.2 | async-start | bytes 1474560 | tf_op jit(solution)/shard_map/decode/all_to_all | solution.py:106
  91.7 30.2 %copy-start.3 = (bf16[576,640]{1,0:T(8,128)(2,1)S(1)}, bf16[576,640]{1,0:T(8,128)(2,1)}, u32[]{:S(2)}) copy-start(bf16[576,640]{1,0:T(8,128)(2,1)} %copy-done.2) | copy-start | bytes 2211844
  92.5 28.3 %all-to-all-start.3 = ((bf16[4,72,640]{2,1,0:T(8,128)(2,1)}), bf16[4,72,640]{2,1,0:T(8,128)(2,1)}, u32[]{:S(2)}, u32[]{:S(2)}) async-start(bf16[4,72,640]{2,1,0:T(8,128)(2,1)} %broadcast_in_dim.52), calls=%async_computation.3 | async-start | bytes 737280 | tf_op jit(solution)/shard_map/error/all_to_all | solution.py:121
  99.3 4.3 %collective-permute-start.1 = (f32[512]{0:T(512)S(1)}, f32[512]{0:T(512)S(1)}, u32[]{:S(2)}, u32[]{:S(2)}) collective-permute-start(f32[512]{0:T(512)S(1)} %fusion.1), channel_id=1, source_target_pairs={{0,128},{64,192},{128,0},{192,64},{256,384},{320,448},{384,256},{4... | collective-permute-start | bytes 6152 | tf_op jit(solution)/shard_map/norms/ppermute | solution.py:117
  103.6 5.9 %collective-permute-start.2 = (f32[512]{0:T(512)S(1)}, f32[512]{0:T(512)S(1)}, u32[]{:S(2)}, u32[]{:S(2)}) collective-permute-start(f32[512]{0:T(512)S(1)} %add.179), channel_id=1, source_target_pairs={{0,384},{64,448},{128,256},{192,320},{256,128},{320,192},{384,0},{... | collective-permute-start | bytes 6152 | tf_op jit(solution)/shard_map/norms/ppermute | solution.py:117
  109.6 6.2 %collective-permute-start.3 = (f32[512]{0:T(512)S(1)}, f32[512]{0:T(512)S(1)}, u32[]{:S(2)}, u32[]{:S(2)}) collective-permute-start(f32[512]{0:T(512)S(1)} %add.180), channel_id=1, source_target_pairs={{0,64},{64,0},{128,192},{192,128},{256,320},{320,256},{384,448},{4... | collective-permute-start | bytes 6152 | tf_op jit(solution)/shard_map/norms/ppermute | solution.py:117
  122.0 25.9 %copy-start.6 = (bf16[512,576]{0,1:T(8,128)(2,1)S(1)}, bf16[512,576]{0,1:T(8,128)(2,1)}, u32[]{:S(2)}) copy-start(bf16[512,576]{0,1:T(8,128)(2,1)} %param.8) | copy-start | bytes 1769476
  142.5 7.8 %copy-start.4 = (bf16[8,72,640]{2,1,0:T(8,128)(2,1)}, bf16[8,72,640]{2,1,0:T(8,128)(2,1)S(1)}, u32[]{:S(2)}) copy-start(bf16[8,72,640]{2,1,0:T(8,128)(2,1)S(1)} %all_to_all.61) | copy-start | bytes 2211844
  142.5 5.5 %collective-permute-start.4 = (bf16[576,640]{1,0:T(8,128)(2,1)S(1)}, bf16[576,640]{1,0:T(8,128)(2,1)S(1)}, u32[]{:S(2)}, u32[]{:S(2)}) collective-permute-start(bf16[576,640]{1,0:T(8,128)(2,1)S(1)} %bitcast.137), channel_id=1, source_target_pairs={{0,1},{1,0},{2,3},{3,2},{4,5},{5,4},{6,7},{7,6},{8,9},{9,8},{10,11... | collective-permute-start | bytes 2211848 | tf_op jit(solution)/shard_map/error/ppermute | solution.py:132
  147.9 2.3 %copy-start.8 = (bf16[576,640]{1,0:T(8,128)(2,1)}, bf16[576,640]{1,0:T(8,128)(2,1)S(1)}, u32[]{:S(2)}) copy-start(bf16[576,640]{1,0:T(8,128)(2,1)S(1)} %collective-permute-done.4) | copy-start | bytes 2211844
  150.3 23.0 %all-to-all-start.5 = ((bf16[8,64,1280]{2,1,0:T(8,128)(2,1)}), bf16[8,64,1280]{2,1,0:T(8,128)(2,1)S(1)}, u32[]{:S(2)}, u32[]{:S(2)}) async-start(bf16[8,64,1280]{2,1,0:T(8,128)(2,1)} %bitcast.142), calls=%async_computation.5 | async-start | bytes 2621440 | tf_op jit(solution)/shard_map/back/all_to_all | solution.py:137
  153.8 19.5 %copy-start.7 = (f32[64,1280]{1,0:T(8,128)S(1)}, f32[64,1280]{1,0:T(8,128)}, u32[]{:S(2)}) copy-start(f32[64,1280]{1,0:T(8,128)} %get-tuple-element.15) | copy-start | bytes 983044
  175.7 21.8 %all-to-all-start.6 = ((bf16[8,64,1280]{2,1,0:T(8,128)(2,1)}), bf16[8,64,1280]{2,1,0:T(8,128)(2,1)S(1)}, u32[]{:S(2)}, u32[]{:S(2)}) async-start(bf16[8,64,1280]{2,1,0:T(8,128)(2,1)} %broadcast_in_dim.54), calls=%async_computation.6 | async-start | bytes 2621440 | tf_op jit(solution)/shard_map/back/all_to_all | solution.py:144

commit v4 on v3

v4 whole, which is shorter than its diff:
```python
import jax
import jax.numpy as jnp
from jax import lax
from jax.experimental import pallas as pl
from jax.experimental.pallas import tpu as pltpu
from jax.sharding import PartitionSpec as P

NZ, NXL, NC = 16, 2, 2
NY, NXH = 4, 2
ZLO = 4
ZHI = NZ // ZLO


def latent_index(z, xl, c):
    return (z * NXL + xl) * NC + c


def layer_index(y, xh):
    return y * NXH + xh


NEAR = [
    [latent_index((zh * ZLO + zl - 2 * c) % NZ, xl, c) for zl in range(ZLO) for xl in range(NXL)]
    for zh in range(ZHI)
    for c in range(NC)
]
FAR = [
    [latent_index(zh * ZLO + zl, xl, c) for zh in range(ZHI)]
    for zl in range(ZLO)
    for xl in range(NXL)
    for c in range(NC)
]
CORE = [
    (latent_index(z, xl, c), latent_index(z, xl, 1 - c))
    for z in range(NZ)
    for xl in range(NXL)
    for c in range(NC)
]
LAYER_STEPS = [
    [(layer_index(y, xh), layer_index(y ^ 1, xh)) for y in range(NY) for xh in range(NXH)],
    [(layer_index(y, xh), layer_index(3 - y, xh)) for y in range(NY) for xh in range(NXH)],
    [(layer_index(y, xh), layer_index(y, 1 - xh)) for y in range(NY) for xh in range(NXH)],
]

F32 = jnp.float32
BF16 = jnp.bfloat16


def dot(a, b, dims):
    return lax.dot_general(a, b, (dims, ((), ())), preferred_element_type=F32)


VMEM = pl.BlockSpec(memory_space=pltpu.VMEM)
SMEM = pl.BlockSpec(memory_space=pltpu.SMEM)


def local_call(body, name, **kwargs):
    params = pltpu.CompilerParams(vmem_limit_bytes=48 * 1024 * 1024)
    return pl.pallas_call(body, name=name, compiler_params=params, **kwargs)


def like(shape, dtype):
    return jax.ShapeDtypeStruct(shape, dtype)


def add_blocks(me, got, own):
    total = own
    for j in range(got.shape[0]):
        total = total + jnp.where(me == j, 0.0, got[j].astype(F32))
    return total


def encode(core, enc, acts_t):
    feat, lat = enc.shape
    rows = acts_t.shape[1]
    half = rows // NC

    def body(c, e, a, out):
        out[...] = dot(e[...], a[...], ((0,), (0,))).astype(BF16)

    return local_call(
        body, "encode",
        out_shape=like((lat, rows), BF16),
        grid_spec=pltpu.PrefetchScalarGridSpec(
            num_scalar_prefetch=1,
            grid=(NC,),
            in_specs=[
                pl.BlockSpec((feat, lat), lambda i, c: (0, 0)),
                pl.BlockSpec((feat, half), lambda i, c: (0, lax.rem(i + c[0], NC))),
            ],
            out_specs=pl.BlockSpec((lat, half), lambda i, c: (0, i)),
        ),
    )(core, enc, acts_t)


def activate(me, got, own, bias):
    n, part, rows = got.shape

    def body(m, g, o, b, codes, slope):
        pre = add_blocks(m[0], g, o[...]) + b[...]
        tail = jnp.exp(-jnp.abs(pre))
        value = (jnp.maximum(pre, 0.0) + jnp.log1p(tail)).astype(BF16)
        slope[...] = jnp.where(pre >= 0, 1.0, tail) / (1.0 + tail)
        for j in range(n):
            codes[j] = value

    return local_call(
        body, "activate",
        out_shape=(like((n, part, rows), BF16), like((part, rows), F32)),
        in_specs=[SMEM, VMEM, VMEM, VMEM],
        out_specs=(VMEM, VMEM),
    )(me, got, own, bias)


def merge_cores(near, own, arrived):
    n, block, half = own.shape

    def body(m, o, a, out, kept):
        for j in range(n):
            out[j] = (o[j] + a[j].astype(F32)).astype(BF16)
        kept[...] = o[m[0]] + a[m[0]].astype(F32)

    return local_call(
        body, "merge_cores",
        out_shape=(like((n, block, half), BF16), like((block, half), F32)),
        in_specs=[SMEM, VMEM, VMEM],
        out_specs=(VMEM, VMEM),
    )(near, own, arrived)


def near_sum(me, got, own, copies):
    block, half = own.shape

    def body(m, g, o, out):
        total = add_blocks(m[0], g, o[...]).astype(BF16)
        for j in range(copies):
            out[j] = total

    return local_call(
        body, "near_sum",
        out_shape=like((copies, block, half), BF16),
        in_specs=[SMEM, VMEM, VMEM],
        out_specs=VMEM,
    )(me, got, own)


def error(got, bias, acts, factor, copies):
    n, block, half = got.shape

    def body(f, g, b, a, out):
        recon = g[0].astype(F32)
        for j in range(1, n):
            recon = recon + g[j].astype(F32)
        err = (f[0] * (recon + b[...] - a[...].astype(F32))).astype(BF16)
        for j in range(copies):
            out[j] = err

    return local_call(
        body, "error",
        out_shape=like((copies, block, half), BF16),
        in_specs=[SMEM, VMEM, VMEM, VMEM],
        out_specs=VMEM,
    )(factor, got, bias, acts)


def back_half(dec_t, err, side, filled=None):
    feat, lat = dec_t.shape
    half = err.shape[1]

    def body(*refs):
        d, e, out = refs[0], refs[1], refs[-1]
        out[...] = dot(d[...], e[...], ((0,), (0,))).astype(BF16)

    args = [dec_t, err]
    specs = [
        pl.BlockSpec((feat, lat), lambda i: (0, 0)),
        pl.BlockSpec((feat, half), lambda i: (0, 0)),
    ]
    aliases = {}
    if filled is not None:
        args.append(filled)
        specs.append(pl.BlockSpec(memory_space=pl.ANY))
        aliases = {2: 0}
    return local_call(
        body, "back_half",
        out_shape=like((lat, NC * half), BF16),
        grid=(1,),
        in_specs=specs,
        out_specs=pl.BlockSpec((lat, half), lambda i: (0, side)),
        input_output_aliases=aliases,
    )(*args)


def weigh(me, got, own, penalty, slope):
    n, part, rows = got.shape

    def body(m, g, o, p, s, out):
        back = add_blocks(m[0], g, o[...]) + p[...]
        value = (back * s[...]).astype(BF16)
        for j in range(n):
            out[j] = value

    return local_call(
        body, "weigh",
        out_shape=like((n, part, rows), BF16),
        in_specs=[SMEM, VMEM, VMEM, VMEM, VMEM],
        out_specs=VMEM,
    )(me, got, own, penalty, slope)


def encoder_grads(acts_t, delta):
    feat, rows = acts_t.shape
    lat = delta.shape[0]

    def body(a, d, weight, bias):
        weight[...] = dot(a[...], d[...], ((1,), (1,)))
        bias[...] = dot(jnp.ones((8, rows), BF16), d[...], ((1,), (1,)))[:1]

    return local_call(
        body, "encoder_grads",
        out_shape=(like((feat, lat), F32), like((1, lat), F32)),
        in_specs=[VMEM, VMEM],
        out_specs=(VMEM, VMEM),
    )(acts_t, delta)


def exchange(x, axis, groups=None):
    return lax.all_to_all(x, axis, 0, 0, axis_index_groups=groups, tiled=True)


def per_device(acts, enc_weight, enc_bias, dec_weight, dec_bias):
    rows, feat = acts.shape
    lat = enc_weight.shape[1]
    scale = 1.0 / jnp.sqrt(F32(rows))
    sparsity = 1.0
    me_layer = lax.axis_index("layer")
    me_latent = lax.axis_index("latent")
    n_layer = NY * NXH
    n_near = ZLO * NXL
    part = lat // n_layer
    core = lax.rem(me_latent, NC)
    x_lo = lax.rem(lax.div(me_latent, NC), NXL)
    z = lax.div(me_latent, NC * NXL)
    near = lax.rem(z + 2 * core, ZLO) * NXL + x_lo
    half = rows // NC
    block = feat // n_near
    layer_ref = me_layer[None].astype(jnp.int32)
    near_ref = near[None].astype(jnp.int32)

    with jax.named_scope("encode"):
        partial_pre = encode(core[None].astype(jnp.int32), enc_weight, acts.T)
        got = exchange(partial_pre.reshape(n_layer, part, rows), "layer")
        acts_t = jnp.concatenate(
            [
                lax.dynamic_slice_in_dim(acts.T, core * half, half, 1),
                lax.dynamic_slice_in_dim(acts.T, (1 - core) * half, half, 1),
            ],
            axis=1,
        )
        own_enc = lax.dynamic_slice_in_dim(enc_weight, me_layer * part, part, 1)
        own_pre = dot(own_enc, acts_t, ((0,), (0,)))
        own_bias = lax.dynamic_slice_in_dim(enc_bias, me_layer * part, part, 0)
        codes_part, slope = activate(layer_ref, got, own_pre, own_bias[:, None])
        codes = exchange(codes_part, "layer").reshape(lat, rows)

    with jax.named_scope("decode"):
        dec_t = dec_weight.T
        away = dot(dec_t, codes[:, half:], ((1,), (0,))).astype(BF16)
        arrived = lax.ppermute(away, "latent", CORE)
        recon = dot(dec_t, codes[:, :half], ((1,), (0,)))
        shape = (n_near, block, half)
        recon, own_recon = merge_cores(near_ref, recon.reshape(shape), arrived.reshape(shape))
        got = exchange(recon, "latent", NEAR)
        recon = near_sum(near_ref, got, own_recon, ZHI)

    with jax.named_scope("norms"):
        dec_f = dec_t.astype(F32)
        squares = jnp.sum(dec_f * dec_f, axis=0)
        squares, recon = lax.optimization_barrier((squares, recon))
        for pairs in LAYER_STEPS:
            squares = squares + lax.ppermute(squares, "layer", pairs)
        norms = jnp.sqrt(squares + 1e-06)

    with jax.named_scope("error"):
        got = exchange(recon, "latent", FAR)
        own_dec_bias = lax.dynamic_slice_in_dim(dec_bias, near * block, block, 0)
        acts_part = lax.dynamic_slice(acts_t, (near * block, 0), (block, half))
        err = error(got, own_dec_bias[:, None], acts_part, (2.0 * scale)[None], n_near)
        err, norms = lax.optimization_barrier((err, norms))
        err_own = exchange(err, "latent", NEAR).reshape(feat, half)
        err_other = lax.ppermute(err_own, "latent", CORE)

    with jax.named_scope("back"):
        partial_back = back_half(dec_t, err_own, 0)
        partial_back = back_half(dec_t, err_other, 1, partial_back)
        got = exchange(partial_back.reshape(n_layer, part, rows), "layer")
        err_t = jnp.concatenate([err_own, err_other], axis=1)
        own_dec = lax.dynamic_slice_in_dim(dec_t, me_layer * part, part, 1)
        own_back = dot(own_dec, err_t, ((0,), (0,)))
        own_norms = lax.dynamic_slice_in_dim(norms, me_layer * part, part, 0)
        penalty = (sparsity * scale * own_norms)[:, None]
        delta_part = weigh(layer_ref, got, own_back, penalty, slope)
        delta = exchange(delta_part, "layer").reshape(lat, rows)

    with jax.named_scope("grads"):
        grad_dec_bias = jnp.sum(err_own.astype(F32), axis=1) + jnp.sum(err_other.astype(F32), axis=1)
        column = jnp.sum(codes.astype(F32), axis=1)
        grad_dec = dot(err_t, codes, ((1,), (1,)))
        grad_dec = grad_dec + (sparsity * scale * column / norms)[None, :] * dec_f
        grad_enc, grad_enc_bias = encoder_grads(acts_t, delta)
    return (grad_enc, grad_enc_bias.reshape(lat), grad_dec.T, grad_dec_bias)


def solution(mesh):
    return jax.shard_map(
        per_device,
        mesh=mesh,
        in_specs=(
            P(None, "layer"),
            P("layer", "latent"),
            P("latent"),
            P("latent", "layer"),
            P("layer"),
        ),
        out_specs=(P("layer", "latent"), P("latent"), P("latent", "layer"), P("layer")),
        check_vma=False,
    )
```

time: 204 us -> 202 us (level)
  Pallas kernels: 0 us -> 12.8 us
  matrix products: 16.6 us -> 6.27 us
  other arithmetic: 12.2 us -> 3.67 us
  local copies, waits for them, and re-layouts: 5.95 us -> 8.98 us
    pallas_call x0 -> x9, Pallas kernels: none -> 12.8 us  [the longest x2 3.32 us: back_half(): local_call(body, 'back_half', out_shape=like((lat, NC * half), BF16), gri...]
    dot_general x8 -> x5, matrix products: 16.6 us -> 6.27 us  [dot(): return lax.dot_general(a, b, (dims, ((), ())), preferred_element_type=F32)]
    unnamed x18 -> x32, local copies, waits for them, and re-layouts: 0.05 us -> 7.49 us
    convert_element_type x5 -> x0, other arithmetic: 6.12 us -> none  [the longest x1 2.12 us: per_device(): codes_part = jax.nn.softplus(pre).astype(BF16)]
    dynamic_slice x3 -> x1, local copies, waits for them, and re-layouts: 3.05 us -> 0.21 us  [per_device(): lax.dynamic_slice_in_dim(acts.T, core * half, half, 1)]
  transfers between devices with their start and end apart: 10 -> 10, of which waited for: 10 -> 10; matrix products, arithmetic and copies ran while one was open for 7% -> 5% of each run, Pallas kernels for 0% -> 1%
where the time goes in v4:
time: 202 us; the launch traced here: 200 us
  waiting for transfers between devices  72.1 us (36%)
  starting transfers between devices  53.7 us (27%)
  blocking collectives  41.5 us (21%)
  Pallas kernels  12.8 us (6%)
  local copies, waits for them, and re-layouts  8.98 us (4%)
  matrix products  6.27 us (3%)
  other arithmetic  3.67 us (2%)
    all_to_all x5, waiting for transfers between devices, exchange(): return lax.all_to_all(x, axis, 0, 0, axis_index_groups=groups, tiled=True)  62 us
    all_to_all x2, blocking collectives, exchange(): return lax.all_to_all(x, axis, 0, 0, axis_index_groups=groups, tiled=True)  41.5 us
    all_to_all x5, starting transfers between devices, exchange(): return lax.all_to_all(x, axis, 0, 0, axis_index_groups=groups, tiled=True)  37.7 us
    ppermute x3, waiting for transfers between devices, per_device(): squares = squares + lax.ppermute(squares, 'layer', pairs)  8.75 us
    unnamed x32, local copies, waits for them, and re-layouts  7.49 us
    ppermute x3, starting transfers between devices, per_device(): squares = squares + lax.ppermute(squares, 'layer', pairs)  7.24 us
    dot_general x5, matrix products, dot(): return lax.dot_general(a, b, (dims, ((), ())), preferred_element_type=F32)  6.27 us
    ppermute x1, starting transfers between devices, per_device(): arrived = lax.ppermute(away, 'latent', CORE)  5.84 us
  transfers between devices with their start and end apart: 10, of which 10 were waited for; matrix products, arithmetic and copies ran while one was open for 5% of the time, Pallas kernels for 1%

profile of v4, /device:TPU:1, one launch (start us, length us, event | category | flops | bytes accessed | tf_op | source)
XLA Modules:
  0.0 199.9 jit_solution(5758773811982136190)
XLA Ops:
  3.1 1.8 encode.1
  6.0 7.6 %all-to-all-start = ((bf16[8,64,1280]{2,1,0:T(8,128)(2,1)}), bf16[8,64,1280]{2,1,0:T(8,128)(2,1)S(1)}, u32[]{:S(2)}, u32[]{:S(2)}) async-start(bf16[8,64,1280]{2,1,0:T(8,128)(2,1)} %bitcast.39), calls=%async_computation | async-start | bytes 2621440 | tf_op jit(solution)/shard_map/encode/all_to_all | solution.py:228
  16.3 14.5 %all-to-all-done.g = bf16[8,64,1280]{2,1,0:T(8,128)(2,1)S(1)} async-done(((bf16[8,64,1280]{2,1,0:T(8,128)(2,1)}), bf16[8,64,1280]{2,1,0:T(8,128)(2,1)S(1)}, u32[]{:S(2)}, u32[]{:S(2)}) %all-to-all-start) | async-done | bytes 1310752 | tf_op jit(solution)/shard_map/encode/all_to_all | solution.py:228
  32.2 20.5 %all_to_all.35 = bf16[8,64,1280]{2,1,0:T(8,128)(2,1)S(1)} all-to-all(bf16[8,64,1280]{2,1,0:T(8,128)(2,1)S(1)} %get-tuple-element.14), channel_id=1, replica_groups=mesh['layer'=8,'latent'=64] {'layer'}, dimensions={0} | all-to-all | bytes 2621440 | tf_op jit(solution)/shard_map/encode/all_to_all | solution.py:228
  53.4 5.8 %collective-permute-start = (bf16[576,640]{1,0:T(8,128)(2,1)S(1)}, bf16[576,640]{1,0:T(8,128)(2,1)S(1)}, u32[]{:S(2)}, u32[]{:S(2)}) collective-permute-start(bf16[576,640]{1,0:T(8,128)(2,1)S(1)} %fusion), channel_id=1, source_target_pairs={{0,1},{1,0},{2,3},{3,2},{4,5},{5,4},{6,7},{7,6},{8,9},{9,8},{10,11... | collective-permute-start | bytes 2211848 | tf_op jit(solution)/shard_map/decode/ppermute | solution.py:269
  62.1 15.4 %all-to-all-start.2 = ((bf16[8,72,640]{2,1,0:T(8,128)(2,1)}), bf16[8,72,640]{2,1,0:T(8,128)(2,1)S(1)}, u32[]{:S(2)}, u32[]{:S(2)}) async-start(bf16[8,72,640]{2,1,0:T(8,128)(2,1)} %get-tuple-element.15), calls=%async_computation.2 | async-start | bytes 1474560 | tf_op jit(solution)/shard_map/decode/all_to_all | solution.py:228
  77.6 13.4 %all-to-all-done.2.g = bf16[8,72,640]{2,1,0:T(8,128)(2,1)S(1)} async-done(((bf16[8,72,640]{2,1,0:T(8,128)(2,1)}), bf16[8,72,640]{2,1,0:T(8,128)(2,1)S(1)}, u32[]{:S(2)}, u32[]{:S(2)}) %all-to-all-start.2) | async-done | bytes 737312 | tf_op jit(solution)/shard_map/decode/all_to_all | solution.py:228
  91.9 6.9 %all-to-all-start.3 = ((bf16[4,72,640]{2,1,0:T(8,128)(2,1)}), bf16[4,72,640]{2,1,0:T(8,128)(2,1)S(1)}, u32[]{:S(2)}, u32[]{:S(2)}) async-start(bf16[4,72,640]{2,1,0:T(8,128)(2,1)} %near_sum.1), calls=%async_computation.3 | async-start | bytes 737280 | tf_op jit(solution)/shard_map/error/all_to_all | solution.py:228
  98.7 1.9 collective-permute-start.1
  100.6 2.4 %collective-permute-done.1 = f32[512]{0:T(512)S(1)} collective-permute-done((f32[512]{0:T(512)S(1)}, f32[512]{0:T(512)S(1)}, u32[]{:S(2)}, u32[]{:S(2)}) %collective-permute-start.1) | collective-permute-done | bytes 2080 | tf_op jit(solution)/shard_map/norms/ppermute | solution.py:281
  103.0 2.4 %collective-permute-start.2 = (f32[512]{0:T(512)S(1)}, f32[512]{0:T(512)S(1)}, u32[]{:S(2)}, u32[]{:S(2)}) collective-permute-start(f32[512]{0:T(512)S(1)} %add.50), channel_id=1, source_target_pairs={{0,384},{64,448},{128,256},{192,320},{256,128},{320,192},{384,0},{... | collective-permute-start | bytes 6152 | tf_op jit(solution)/shard_map/norms/ppermute | solution.py:281
  105.5 3.4 %collective-permute-done.2 = f32[512]{0:T(512)S(1)} collective-permute-done((f32[512]{0:T(512)S(1)}, f32[512]{0:T(512)S(1)}, u32[]{:S(2)}, u32[]{:S(2)}) %collective-permute-start.2) | collective-permute-done | bytes 2080 | tf_op jit(solution)/shard_map/norms/ppermute | solution.py:281
  108.9 3.0 %collective-permute-start.3 = (f32[512]{0:T(512)S(1)}, f32[512]{0:T(512)S(1)}, u32[]{:S(2)}, u32[]{:S(2)}) collective-permute-start(f32[512]{0:T(512)S(1)} %add.51), channel_id=1, source_target_pairs={{0,64},{64,0},{128,192},{192,128},{256,320},{320,256},{384,448},{4... | collective-permute-start | bytes 6152 | tf_op jit(solution)/shard_map/norms/ppermute | solution.py:281
  112.0 3.0 %collective-permute-done.3 = f32[512]{0:T(512)S(1)} collective-permute-done((f32[512]{0:T(512)S(1)}, f32[512]{0:T(512)S(1)}, u32[]{:S(2)}, u32[]{:S(2)}) %collective-permute-start.3) | collective-permute-done | bytes 2080 | tf_op jit(solution)/shard_map/norms/ppermute | solution.py:281
  115.0 5.0 %all-to-all-done.3.g = bf16[4,72,640]{2,1,0:T(8,128)(2,1)S(1)} async-done(((bf16[4,72,640]{2,1,0:T(8,128)(2,1)}), bf16[4,72,640]{2,1,0:T(8,128)(2,1)S(1)}, u32[]{:S(2)}, u32[]{:S(2)}) %all-to-all-start.3) | async-done | bytes 368672 | tf_op jit(solution)/shard_map/error/all_to_all | solution.py:228
  120.2 21.0 %all_to_all.36 = bf16[8,72,640]{2,1,0:T(8,128)(2,1)S(1)} all-to-all(bf16[8,72,640]{2,1,0:T(8,128)(2,1)S(1)} %error.1), channel_id=1, replica_groups={{0,2,4,6,8,10,12,14},{57,59,61,63,1,3,5,7},{16,18,20,22,24,26,28,30},{9..., dimensions={0} | all-to-all | bytes 1474560 | tf_op jit(solution)/shard_map/error/all_to_all | solution.py:228
  141.2 3.0 %collective-permute-start.4 = (bf16[576,640]{1,0:T(8,128)(2,1)S(1)}, bf16[576,640]{1,0:T(8,128)(2,1)S(1)}, u32[]{:S(2)}, u32[]{:S(2)}) collective-permute-start(bf16[576,640]{1,0:T(8,128)(2,1)S(1)} %bitcast.33), channel_id=1, source_target_pairs={{0,1},{1,0},{2,3},{3,2},{4,5},{5,4},{6,7},{7,6},{8,9},{9,8},{10,11... | collective-permute-start | bytes 2211848 | tf_op jit(solution)/shard_map/error/ppermute | solution.py:291
  144.1 1.7 back_half.2.refs_2_
  147.6 3.6 %all-to-all-start.5 = ((bf16[8,64,1280]{2,1,0:T(8,128)(2,1)}), bf16[8,64,1280]{2,1,0:T(8,128)(2,1)S(1)}, u32[]{:S(2)}, u32[]{:S(2)}) async-start(bf16[8,64,1280]{2,1,0:T(8,128)(2,1)} %bitcast.16), calls=%async_computation.5 | async-start | bytes 2621440 | tf_op jit(solution)/shard_map/back/all_to_all | solution.py:228
  152.6 18.0 %all-to-all-done.5.g = bf16[8,64,1280]{2,1,0:T(8,128)(2,1)S(1)} async-done(((bf16[8,64,1280]{2,1,0:T(8,128)(2,1)}), bf16[8,64,1280]{2,1,0:T(8,128)(2,1)S(1)}, u32[]{:S(2)}, u32[]{:S(2)}) %all-to-all-start.5) | async-done | bytes 1310752 | tf_op jit(solution)/shard_map/back/all_to_all | solution.py:228
  174.2 4.3 %all-to-all-start.6 = ((bf16[8,64,1280]{2,1,0:T(8,128)(2,1)}), bf16[8,64,1280]{2,1,0:T(8,128)(2,1)}, u32[]{:S(2)}, u32[]{:S(2)}) async-start(bf16[8,64,1280]{2,1,0:T(8,128)(2,1)} %weigh.1), calls=%async_computation.6 | async-start | bytes 2621440 | tf_op jit(solution)/shard_map/back/all_to_all | solution.py:228
  182.2 3.3 %convolution_add_fusion = f32[512,576]{0,1:T(8,128)} fusion(bf16[512,1280]{1,0:T(8,128)(2,1)} %bitcast.43, bf16[512,576]{0,1:T(8,128)(2,1)S(1)} %copy-done.1, bf16[576,640]{1,0:T(8,128)(2,1)S(1)} %collective-permute-done.4.refs_1_, bf16[576,640]{1,0:T(8,128)(2,1)S(1)} %bitcast.36, f32[512]{0:T(512)S(1)} %copy-done.15), kind=kOutput, calls=%fused_computation.7 | convolution fusion | flops 758808576 | bytes 4556800 | tf_op jit(solution)/shard_map/grads/dot_general | solution.py:50
  185.5 11.2 %all-to-all-done.6 = bf16[8,64,1280]{2,1,0:T(8,128)(2,1)} async-done(((bf16[8,64,1280]{2,1,0:T(8,128)(2,1)}), bf16[8,64,1280]{2,1,0:T(8,128)(2,1)}, u32[]{:S(2)}, u32[]{:S(2)}) %all-to-all-start.6) | async-done | bytes 1310752 | tf_op jit(solution)/shard_map/back/all_to_all | solution.py:228
  196.7 3.3 %encoder_grads.1 = (f32[576,512]{1,0:T(8,128)}, f32[1,512]{1,0:T(1,128)}) custom-call(bf16[576,1280]{1,0:T(8,128)(2,1)S(1)} %pad_maximum_fusion.a, bf16[512,1280]{1,0:T(8,128)(2,1)} %bitcast.18.d), custom_call_target="tpu_custom_call" | custom-call | tf_op jit(solution)/shard_map/grads/encoder_grads/pallas_call | solution.py:219
  (65 shorter events, 23.0 us)
Async XLA Ops:
  0.6 111.2 %copy-start = (f32[576]{0:T(1024)S(1)}, f32[576]{0:T(1024)}, u32[]{:S(2)}) copy-start(f32[576]{0:T(1024)} %param.9) | copy-start | bytes 6916
  0.7 1.4 copy-start.2
  2.0 1.1 copy-start.5
  4.9 1.1 copy-start.4
  6.0 8.5 %copy-start.3 = (bf16[1280,576]{0,1:T(8,128)(2,1)S(1)}, bf16[1280,576]{0,1:T(8,128)(2,1)}, u32[]{:S(2)}) copy-start(bf16[1280,576]{0,1:T(8,128)(2,1)} %param.5) | copy-start | bytes 4423684
  6.0 24.7 %all-to-all-start = ((bf16[8,64,1280]{2,1,0:T(8,128)(2,1)}), bf16[8,64,1280]{2,1,0:T(8,128)(2,1)S(1)}, u32[]{:S(2)}, u32[]{:S(2)}) async-start(bf16[8,64,1280]{2,1,0:T(8,128)(2,1)} %bitcast.39), calls=%async_computation | async-start | bytes 2621440 | tf_op jit(solution)/shard_map/encode/all_to_all | solution.py:228
  14.7 1.1 copy-start.13
  32.2 20.5 %copy-start.1 = (bf16[512,576]{0,1:T(8,128)(2,1)S(1)}, bf16[512,576]{0,1:T(8,128)(2,1)}, u32[]{:S(2)}) copy-start(bf16[512,576]{0,1:T(8,128)(2,1)} %param.8) | copy-start | bytes 1769476
  52.7 7.1 %copy-start.9 = (bf16[8,64,1280]{2,1,0:T(8,128)(2,1)}, bf16[8,64,1280]{2,1,0:T(8,128)(2,1)S(1)}, u32[]{:S(2)}) copy-start(bf16[8,64,1280]{2,1,0:T(8,128)(2,1)S(1)} %all_to_all.35) | copy-start | bytes 3932164
  53.4 7.7 %collective-permute-start = (bf16[576,640]{1,0:T(8,128)(2,1)S(1)}, bf16[576,640]{1,0:T(8,128)(2,1)S(1)}, u32[]{:S(2)}, u32[]{:S(2)}) collective-permute-start(bf16[576,640]{1,0:T(8,128)(2,1)S(1)} %fusion), channel_id=1, source_target_pairs={{0,1},{1,0},{2,3},{3,2},{4,5},{5,4},{6,7},{7,6},{8,9},{9,8},{10,11... | collective-permute-start | bytes 2211848 | tf_op jit(solution)/shard_map/decode/ppermute | solution.py:269
  62.1 28.9 %all-to-all-start.2 = ((bf16[8,72,640]{2,1,0:T(8,128)(2,1)}), bf16[8,72,640]{2,1,0:T(8,128)(2,1)S(1)}, u32[]{:S(2)}, u32[]{:S(2)}) async-start(bf16[8,72,640]{2,1,0:T(8,128)(2,1)} %get-tuple-element.15), calls=%async_computation.2 | async-start | bytes 1474560 | tf_op jit(solution)/shard_map/decode/all_to_all | solution.py:228
  77.4 28.0 %copy-start.12 = (bf16[576,640]{1,0:T(8,128)(2,1)S(1)}, bf16[576,640]{1,0:T(8,128)(2,1)}, u32[]{:S(2)}) copy-start(bf16[576,640]{1,0:T(8,128)(2,1)} %copy-done.11) | copy-start | bytes 2211844
  77.4 28.0 %copy-start.14 = (bf16[576,640]{1,0:T(8,128)(2,1)S(1)}, bf16[576,640]{1,0:T(8,128)(2,1)}, u32[]{:S(2)}) copy-start(bf16[576,640]{1,0:T(8,128)(2,1)} %copy-done.13) | copy-start | bytes 2211844
  91.9 28.2 %all-to-all-start.3 = ((bf16[4,72,640]{2,1,0:T(8,128)(2,1)}), bf16[4,72,640]{2,1,0:T(8,128)(2,1)S(1)}, u32[]{:S(2)}, u32[]{:S(2)}) async-start(bf16[4,72,640]{2,1,0:T(8,128)(2,1)} %near_sum.1), calls=%async_computation.3 | async-start | bytes 737280 | tf_op jit(solution)/shard_map/error/all_to_all | solution.py:228
  98.7 4.3 %collective-permute-start.1 = (f32[512]{0:T(512)S(1)}, f32[512]{0:T(512)S(1)}, u32[]{:S(2)}, u32[]{:S(2)}) collective-permute-start(f32[512]{0:T(512)S(1)} %multiply_reduce_fusion), channel_id=1, source_target_pairs={{0,128},{64,192},{128,0},{192,64},{256,384},{320,448},{384,256},{4... | collective-permute-start | bytes 6152 | tf_op jit(solution)/shard_map/norms/ppermute | solution.py:281
  103.0 5.8 %collective-permute-start.2 = (f32[512]{0:T(512)S(1)}, f32[512]{0:T(512)S(1)}, u32[]{:S(2)}, u32[]{:S(2)}) collective-permute-start(f32[512]{0:T(512)S(1)} %add.50), channel_id=1, source_target_pairs={{0,384},{64,448},{128,256},{192,320},{256,128},{320,192},{384,0},{... | collective-permute-start | bytes 6152 | tf_op jit(solution)/shard_map/norms/ppermute | solution.py:281
  108.9 6.1 %collective-permute-start.3 = (f32[512]{0:T(512)S(1)}, f32[512]{0:T(512)S(1)}, u32[]{:S(2)}, u32[]{:S(2)}) collective-permute-start(f32[512]{0:T(512)S(1)} %add.51), channel_id=1, source_target_pairs={{0,64},{64,0},{128,192},{192,128},{256,320},{320,256},{384,448},{4... | collective-permute-start | bytes 6152 | tf_op jit(solution)/shard_map/norms/ppermute | solution.py:281
  141.2 4.8 %collective-permute-start.4 = (bf16[576,640]{1,0:T(8,128)(2,1)S(1)}, bf16[576,640]{1,0:T(8,128)(2,1)S(1)}, u32[]{:S(2)}, u32[]{:S(2)}) collective-permute-start(bf16[576,640]{1,0:T(8,128)(2,1)S(1)} %bitcast.33), channel_id=1, source_target_pairs={{0,1},{1,0},{2,3},{3,2},{4,5},{5,4},{6,7},{7,6},{8,9},{9,8},{10,11... | collective-permute-start | bytes 2211848 | tf_op jit(solution)/shard_map/error/ppermute | solution.py:291
  147.6 23.0 %all-to-all-start.5 = ((bf16[8,64,1280]{2,1,0:T(8,128)(2,1)}), bf16[8,64,1280]{2,1,0:T(8,128)(2,1)S(1)}, u32[]{:S(2)}, u32[]{:S(2)}) async-start(bf16[8,64,1280]{2,1,0:T(8,128)(2,1)} %bitcast.16), calls=%async_computation.5 | async-start | bytes 2621440 | tf_op jit(solution)/shard_map/back/all_to_all | solution.py:228
  170.6 1.0 copy-start.7
  171.6 1.0 copy-start.8
  174.2 22.5 %all-to-all-start.6 = ((bf16[8,64,1280]{2,1,0:T(8,128)(2,1)}), bf16[8,64,1280]{2,1,0:T(8,128)(2,1)}, u32[]{:S(2)}, u32[]{:S(2)}) async-start(bf16[8,64,1280]{2,1,0:T(8,128)(2,1)} %weigh.1), calls=%async_computation.6 | async-start | bytes 2621440 | tf_op jit(solution)/shard_map/back/all_to_all | solution.py:228
  178.4 1.8 copy-start.10
  181.1 1.1 copy-start.15
  (2 other events, 1.6 us)

commit v5 on v4

v5 whole, which is shorter than its diff:
```python
import jax
import jax.numpy as jnp
from jax import lax
from jax.experimental import pallas as pl
from jax.experimental.pallas import tpu as pltpu
from jax.sharding import PartitionSpec as P

NZ, NXL, NC = 16, 2, 2
NY, NXH = 4, 2
ZLO = 4
ZHI = NZ // ZLO


def latent_index(z, xl, c):
    return (z * NXL + xl) * NC + c


def layer_index(y, xh):
    return y * NXH + xh


NEAR = [
    [latent_index((zh * ZLO + zl - 2 * c) % NZ, xl, c) for zl in range(ZLO) for xl in range(NXL)]
    for zh in range(ZHI)
    for c in range(NC)
]
FAR = [
    [latent_index(zh * ZLO + zl, xl, c) for zh in range(ZHI)]
    for zl in range(ZLO)
    for xl in range(NXL)
    for c in range(NC)
]
CORE = [
    (latent_index(z, xl, c), latent_index(z, xl, 1 - c))
    for z in range(NZ)
    for xl in range(NXL)
    for c in range(NC)
]
LAYER_STEPS = [
    [(layer_index(y, xh), layer_index(y ^ 1, xh)) for y in range(NY) for xh in range(NXH)],
    [(layer_index(y, xh), layer_index(3 - y, xh)) for y in range(NY) for xh in range(NXH)],
    [(layer_index(y, xh), layer_index(y, 1 - xh)) for y in range(NY) for xh in range(NXH)],
]

F32 = jnp.float32
BF16 = jnp.bfloat16


def dot(a, b, dims):
    return lax.dot_general(a, b, (dims, ((), ())), preferred_element_type=F32)


VMEM = pl.BlockSpec(memory_space=pltpu.VMEM)
SMEM = pl.BlockSpec(memory_space=pltpu.SMEM)
HBM = pl.BlockSpec(memory_space=pltpu.HBM)
ALONE = 58


def local_call(body, name, grant=16, **kwargs):
    params = pltpu.CompilerParams(vmem_limit_bytes=grant * 1024 * 1024)
    return pl.pallas_call(body, name=name, compiler_params=params, **kwargs)


def copies(count):
    return pltpu.SemaphoreType.DMA((count,))


def like(shape, dtype):
    return jax.ShapeDtypeStruct(shape, dtype)


def add_blocks(me, got, own):
    total = own
    for j in range(got.shape[0]):
        total = total + jnp.where(me == j, 0.0, got[j].astype(F32))
    return total


def half_columns(core, rows, i):
    half = rows // NC
    return pl.ds(pl.multiple_of(lax.rem(core + i, NC) * half, half), half)


def encode(core, me, enc, bias, acts_t, loads_of_acts=4, steps=2):
    feat, lat = enc.shape
    rows = acts_t.shape[1]
    half = rows // NC
    part = lat // (NY * NXH)
    piece = feat // loads_of_acts
    size = lat // steps

    def body(c, m, e_hbm, b, a_hbm, out_hbm, own_hbm, acts, e, e_rows, b_rows, out, own, e_sem, a_sems, out_sems):
        loads = [pltpu.make_async_copy(e_hbm, e, e_sem.at[0])]
        for i in range(loads_of_acts):
            here = slice(i * piece, (i + 1) * piece)
            loads.append(pltpu.make_async_copy(a_hbm.at[here], acts.at[here], a_sems.at[i]))
        for load in loads:
            load.start()
        b_rows[...] = jnp.broadcast_to(b[...], (128, lat)).T
        loads[0].wait()
        e_rows[...] = e[...].T
        for load in loads[1:]:
            load.wait()
        stores = []
        for i in range(steps):
            here = slice(i * size, (i + 1) * size)
            for j in range(NC):
                side = slice(j * half, (j + 1) * half)
                out[here, side] = dot(e_rows[here], acts[:, half_columns(c[0], rows, j)], ((1,), (0,))).astype(BF16)
            stores.append(pltpu.make_async_copy(out.at[here], out_hbm.at[here], out_sems.at[i]))
            stores[i].start()
        mine = pl.ds(pl.multiple_of(m[0] * part, part), part)
        for j in range(NC):
            side = slice(j * half, (j + 1) * half)
            own[:, side] = dot(e_rows[mine], acts[:, half_columns(c[0], rows, j)], ((1,), (0,))) + b_rows[mine][:, :1]
        stores.append(pltpu.make_async_copy(own, own_hbm, out_sems.at[steps]))
        stores[steps].start()
        for store in stores:
            store.wait()

    return local_call(
        body, "encode", grant=ALONE,
        out_shape=(like((lat, rows), BF16), like((part, rows), F32)),
        in_specs=[SMEM, SMEM, HBM, VMEM, HBM],
        out_specs=(HBM, HBM),
        scratch_shapes=[
            pltpu.VMEM((feat, rows), BF16),
            pltpu.VMEM((feat, lat), BF16),
            pltpu.VMEM((lat, feat), BF16),
            pltpu.VMEM((lat, 128), F32),
            pltpu.VMEM((lat, rows), BF16),
            pltpu.VMEM((part, rows), F32),
            copies(1),
            copies(loads_of_acts),
            copies(steps + 1),
        ],
    )(core, me, enc, bias, acts_t)


def activate(me, got, own):
    n, part, rows = got.shape

    def body(m, g, o, codes, slope):
        pre = add_blocks(m[0], g, o[...])
        tail = jnp.exp(-jnp.abs(pre))
        value = (jnp.maximum(pre, 0.0) + jnp.log1p(tail)).astype(BF16)
        slope[...] = jnp.where(pre >= 0, 1.0, tail) / (1.0 + tail)
        for j in range(n):
            codes[j] = value

    return local_call(
        body, "activate",
        out_shape=(like((n, part, rows), BF16), like((part, rows), F32)),
        in_specs=[SMEM, VMEM, VMEM],
        out_specs=(VMEM, VMEM),
    )(me, got, own)


def merge_cores(near, own, arrived):
    n, block, half = own.shape

    def body(m, o, a, out, kept):
        for j in range(n):
            out[j] = (o[j] + a[j].astype(F32)).astype(BF16)
        kept[...] = o[m[0]] + a[m[0]].astype(F32)

    return local_call(
        body, "merge_cores",
        out_shape=(like((n, block, half), BF16), like((block, half), F32)),
        in_specs=[SMEM, VMEM, VMEM],
        out_specs=(VMEM, VMEM),
    )(near, own, arrived)


def near_sum(me, got, own, count):
    block, half = own.shape

    def body(m, g, o, out):
        total = add_blocks(m[0], g, o[...]).astype(BF16)
        for j in range(count):
            out[j] = total

    return local_call(
        body, "near_sum",
        out_shape=like((count, block, half), BF16),
        in_specs=[SMEM, VMEM, VMEM],
        out_specs=VMEM,
    )(me, got, own)


def error(got, bias, acts, factor, count):
    n, block, half = got.shape

    def body(f, g, b, a, out):
        recon = g[0].astype(F32)
        for j in range(1, n):
            recon = recon + g[j].astype(F32)
        err = (f[0] * (recon + b[...] - a[...].astype(F32))).astype(BF16)
        for j in range(count):
            out[j] = err

    return local_call(
        body, "error",
        out_shape=like((count, block, half), BF16),
        in_specs=[SMEM, VMEM, VMEM, VMEM],
        out_specs=VMEM,
    )(factor, got, bias, acts)


def squares_and_rows(dec_t):
    feat, lat = dec_t.shape

    def body(d, squares, d_rows):
        wide = d[...].astype(F32)
        squares[...] = jnp.sum(wide * wide, axis=0, keepdims=True)
        d_rows[...] = d[...].T

    return local_call(
        body, "squares_and_rows",
        out_shape=(like((1, lat), F32), like((lat, feat), BF16)),
        in_specs=[VMEM],
        out_specs=(VMEM, VMEM),
    )(dec_t)


def back_half(dec, err, side, filled=None):
    lat, feat = dec.shape
    half = err.shape[1]
    steps = 2
    size = lat // steps

    def body(d, e, *refs):
        out_hbm, out, sems = refs[-3:]
        stores = []
        for i in range(steps):
            here = slice(i * size, (i + 1) * size)
            out[here] = dot(d[here], e[...], ((1,), (0,))).astype(BF16)
            there = out_hbm.at[here, side * half : (side + 1) * half]
            stores.append(pltpu.make_async_copy(out.at[here], there, sems.at[i]))
            stores[i].start()
        for store in stores:
            store.wait()

    more = [] if filled is None else [filled]
    return local_call(
        body, "back_half",
        out_shape=like((lat, NC * half), BF16),
        in_specs=[VMEM, VMEM] + [HBM] * len(more),
        out_specs=HBM,
        scratch_shapes=[pltpu.VMEM((lat, half), BF16), copies(steps)],
        input_output_aliases={2: 0} if more else {},
    )(dec, err, *more)


def at_hand(me, norms, slope, factor):
    part, rows = slope.shape
    lat = norms.shape[1]

    def body(m, f, n, s, penalty, kept, columns):
        columns[...] = jnp.broadcast_to(f[0] * n[...], (128, lat)).T
        penalty[...] = columns[pl.ds(pl.multiple_of(m[0] * part, part), part)][:, :1]
        kept[...] = s[...]

    return local_call(
        body, "at_hand",
        out_shape=(like((part, 1), F32), like((part, rows), F32)),
        in_specs=[SMEM, SMEM, VMEM, VMEM],
        out_specs=(VMEM, VMEM),
        scratch_shapes=[pltpu.VMEM((lat, 128), F32)],
    )(me, factor, norms, slope)


def weigh(got, penalty, slope):
    n, part, rows = got.shape

    def body(g, p, s, out):
        back = g[0].astype(F32)
        for j in range(1, n):
            back = back + g[j].astype(F32)
        value = ((back + p[...]) * s[...]).astype(BF16)
        for j in range(n):
            out[j] = value

    return local_call(
        body, "weigh",
        out_shape=like((n, part, rows), BF16),
        in_specs=[VMEM, VMEM, VMEM],
        out_specs=VMEM,
    )(got, penalty, slope)


def encoder_grads(core, acts_t, delta, steps=3):
    feat, rows = acts_t.shape
    lat = delta.shape[0]
    size = feat // steps
    half = rows // NC

    def body(c, a, d, weight_hbm, bias, weight, sems):
        stores = []
        for i in range(steps):
            here = slice(i * size, (i + 1) * size)
            first, second = (
                dot(a[here, half_columns(c[0], rows, j)], d[:, j * half : (j + 1) * half], ((1,), (1,)))
                for j in range(NC)
            )
            weight[here] = first + second
            stores.append(pltpu.make_async_copy(weight.at[here], weight_hbm.at[here], sems.at[i]))
            stores[i].start()
        bias[...] = dot(jnp.ones((8, rows), BF16), d[...], ((1,), (1,)))[:1]
        for store in stores:
            store.wait()

    return local_call(
        body, "encoder_grads",
        out_shape=(like((feat, lat), F32), like((1, lat), F32)),
        in_specs=[SMEM, VMEM, VMEM],
        out_specs=(HBM, VMEM),
        scratch_shapes=[pltpu.VMEM((feat, lat), F32), copies(steps)],
    )(core, acts_t, delta)


def exchange(x, axis, groups=None):
    return lax.all_to_all(x, axis, 0, 0, axis_index_groups=groups, tiled=True)


def per_device(acts, enc_weight, enc_bias, dec_weight, dec_bias):
    rows, feat = acts.shape
    lat = enc_weight.shape[1]
    scale = 1.0 / jnp.sqrt(F32(rows))
    sparsity = 1.0
    me_layer = lax.axis_index("layer")
    me_latent = lax.axis_index("latent")
    n_layer = NY * NXH
    n_near = ZLO * NXL
    part = lat // n_layer
    core = lax.rem(me_latent, NC)
    x_lo = lax.rem(lax.div(me_latent, NC), NXL)
    z = lax.div(me_latent, NC * NXL)
    near = lax.rem(z + 2 * core, ZLO) * NXL + x_lo
    half = rows // NC
    block = feat // n_near
    core_ref = core[None].astype(jnp.int32)
    layer_ref = me_layer[None].astype(jnp.int32)
    near_ref = near[None].astype(jnp.int32)

    acts_t = acts.T
    dec_t = dec_weight.T
    with jax.named_scope("encode"):
        partial_pre, own_pre = encode(core_ref, layer_ref, enc_weight, enc_bias.reshape(1, lat), acts_t)
        got = exchange(partial_pre.reshape(n_layer, part, rows), "layer")
        codes_part, slope = activate(layer_ref, got, own_pre)
        codes = exchange(codes_part, "layer").reshape(lat, rows)

    with jax.named_scope("decode"):
        away = dot(dec_t, codes[:, half:], ((1,), (0,))).astype(BF16)
        arrived = lax.ppermute(away, "latent", CORE)
        recon = dot(dec_t, codes[:, :half], ((1,), (0,)))
        shape = (n_near, block, half)
        recon, own_recon = merge_cores(near_ref, recon.reshape(shape), arrived.reshape(shape))
        got = exchange(recon, "latent", NEAR)
        recon = near_sum(near_ref, got, own_recon, ZHI)

    with jax.named_scope("norms"):
        late_dec_t, recon = lax.optimization_barrier((dec_t, recon))
        squares, dec_rows = squares_and_rows(late_dec_t)
        squares = squares.reshape(lat)
        for pairs in LAYER_STEPS:
            squares = squares + lax.ppermute(squares, "layer", pairs)
        norms = jnp.sqrt(squares + 1e-06)

    with jax.named_scope("error"):
        got = exchange(recon, "latent", FAR)
        own_dec_bias = lax.dynamic_slice_in_dim(dec_bias, near * block, block, 0)
        acts_part = lax.dynamic_slice(acts_t, (near * block, core * half), (block, half))
        err = error(got, own_dec_bias[:, None], acts_part, (2.0 * scale)[None], n_near)
        err, norms = lax.optimization_barrier((err, norms))
        err_own = exchange(err, "latent", NEAR).reshape(feat, half)
        err_other = lax.ppermute(err_own, "latent", CORE)

    with jax.named_scope("back"):
        partial_back = back_half(dec_rows, err_own, 0)
        partial_back = back_half(dec_rows, err_other, 1, partial_back)
        got = exchange(partial_back.reshape(n_layer, part, rows), "layer")

    with jax.named_scope("decoder_grads"):
        grad_dec_bias = jnp.sum(err_own.astype(F32), axis=1) + jnp.sum(err_other.astype(F32), axis=1)
        column = jnp.sum(codes.astype(F32), axis=1)
        err_t = jnp.concatenate([err_own, err_other], axis=1)
        grad_dec = dot(err_t, codes, ((1,), (1,)))
        grad_dec = grad_dec + (sparsity * scale * column / norms)[None, :] * dec_t.astype(F32)

    with jax.named_scope("encoder_grads"):
        late_slope, grad_dec, grad_dec_bias = lax.optimization_barrier((slope, grad_dec, grad_dec_bias))
        factor = (sparsity * scale)[None]
        penalty, late_slope = at_hand(layer_ref, norms.reshape(1, lat), late_slope, factor)
        got, penalty, late_slope = lax.optimization_barrier((got, penalty, late_slope))
        delta_part = weigh(got, penalty, late_slope)
        delta = exchange(delta_part, "layer").reshape(lat, rows)
        grad_enc, grad_enc_bias = encoder_grads(core_ref, acts_t, delta)
    return (grad_enc, grad_enc_bias.reshape(lat), grad_dec.T, grad_dec_bias)


def solution(mesh):
    return jax.shard_map(
        per_device,
        mesh=mesh,
        in_specs=(
            P(None, "layer"),
            P("layer", "latent"),
            P("latent"),
            P("latent", "layer"),
            P("layer"),
        ),
        out_specs=(P("layer", "latent"), P("latent"), P("latent", "layer"), P("layer")),
        check_vma=False,
    )
```

time: 202 us -> 195 us (0.965)
  blocking collectives: 41.5 us -> 118 us
  waiting for transfers between devices: 72.1 us -> 23.4 us
  starting transfers between devices: 53.7 us -> 28.6 us
  local copies, waits for them, and re-layouts: 8.98 us -> 0.39 us
    all_to_all x2 -> x5, blocking collectives: 41.5 us -> 118 us  [exchange(): return lax.all_to_all(x, axis, 0, 0, axis_index_groups=groups, tiled=True)]
    all_to_all x5 -> x2, waiting for transfers between devices: 62 us -> 14.2 us  [exchange(): return lax.all_to_all(x, axis, 0, 0, axis_index_groups=groups, tiled=True)]
    all_to_all x5 -> x2, starting transfers between devices: 37.7 us -> 12.6 us  [exchange(): return lax.all_to_all(x, axis, 0, 0, axis_index_groups=groups, tiled=True)]
    unnamed x32 -> x16, local copies, waits for them, and re-layouts: 7.49 us -> 0.04 us
    pallas_call x5 -> x7, Pallas kernels: 6.18 us -> 9.08 us  [the longest x1 4.69 us: encode(): local_call(body, 'encode', grant=ALONE, out_shape=(like((lat, rows), BF16...]
    dot_general x5 -> x3, matrix products: 6.27 us -> 6.04 us  [dot(): return lax.dot_general(a, b, (dims, ((), ())), preferred_element_type=F32)]
  transfers between devices with their start and end apart: 10 -> 7, of which waited for: 10 -> 7; matrix products, arithmetic and copies ran while one was open for 5% -> 5% of each run, Pallas kernels for 1% -> 1%
where the time goes in v5:
time: 195 us; the launch traced here: 194 us
  blocking collectives  118 us (61%)
  starting transfers between devices  28.6 us (15%)
  waiting for transfers between devices  23.4 us (12%)
  Pallas kernels  12.9 us (7%)
  matrix products  6.04 us (3%)
  other arithmetic  3.71 us (2%)
    all_to_all x5, blocking collectives, exchange(): return lax.all_to_all(x, axis, 0, 0, axis_index_groups=groups, tiled=True)  118 us
    all_to_all x2, waiting for transfers between devices, exchange(): return lax.all_to_all(x, axis, 0, 0, axis_index_groups=groups, tiled=True)  14.2 us
    all_to_all x2, starting transfers between devices, exchange(): return lax.all_to_all(x, axis, 0, 0, axis_index_groups=groups, tiled=True)  12.6 us
    ppermute x3, waiting for transfers between devices, per_device(): squares = squares + lax.ppermute(squares, 'layer', pairs)  8.51 us
    ppermute x3, starting transfers between devices, per_device(): squares = squares + lax.ppermute(squares, 'layer', pairs)  7.49 us
    ppermute x1, starting transfers between devices, per_device(): arrived = lax.ppermute(away, 'latent', CORE)  6.56 us
    dot_general x3, matrix products, dot(): return lax.dot_general(a, b, (dims, ((), ())), preferred_element_type=F32)  6.04 us
    pallas_call x1, Pallas kernels, encode(): local_call(body, 'encode', grant=ALONE, out_shape=(like((lat, rows), BF16...  4.69 us
  transfers between devices with their start and end apart: 7, of which 7 were waited for; matrix products, arithmetic and copies ran while one was open for 5% of the time, Pallas kernels for 1%

profile of v5, /device:TPU:1, one launch (start us, length us, event | category | flops | bytes accessed | tf_op | source)
XLA Modules:
  0.0 194.0 jit_solution(8952020661678499826)
XLA Ops:
  0.7 4.7 %encode.1 = (bf16[512,1280]{1,0:T(8,128)(2,1)}, f32[64,1280]{1,0:T(8,128)}) custom-call(s32[1]{0:T(128)} %bitcast.c, s32[1]{0:T(128)} %bitcast.4.m, bf16[576,512]{1,0:T(8,128)(2,1)} %e_hbm.1, f32[1,512]{1,0:T(1,128)} %bitcast.45, bf16[576,1280]{1,0:T(8,128)(2,1)} %bitcast.32), custom_call_target="tpu_custom_call" | custom-call | tf_op jit(solution)/shard_map/encode/encode/pallas_call | solution.py:121
  5.4 24.8 %all_to_all.35.g = bf16[8,64,1280]{2,1,0:T(8,128)(2,1)S(1)} all-to-all(bf16[8,64,1280]{2,1,0:T(8,128)(2,1)} %bitcast.44), channel_id=1, replica_groups=mesh['layer'=8,'latent'=64] {'layer'}, dimensions={0} | all-to-all | bytes 2621440 | tf_op jit(solution)/shard_map/encode/all_to_all | solution.py:323
  30.7 19.1 %all_to_all.36 = bf16[8,64,1280]{2,1,0:T(8,128)(2,1)S(1)} all-to-all(bf16[8,64,1280]{2,1,0:T(8,128)(2,1)S(1)} %get-tuple-element.28), channel_id=1, replica_groups=mesh['layer'=8,'latent'=64] {'layer'}, dimensions={0} | all-to-all | bytes 2621440 | tf_op jit(solution)/shard_map/encode/all_to_all | solution.py:323
  50.4 6.6 %collective-permute-start = (bf16[576,640]{1,0:T(8,128)(2,1)S(1)}, bf16[576,640]{1,0:T(8,128)(2,1)S(1)}, u32[]{:S(2)}, u32[]{:S(2)}) collective-permute-start(bf16[576,640]{1,0:T(8,128)(2,1)S(1)} %fusion.7), channel_id=1, source_target_pairs={{0,1},{1,0},{2,3},{3,2},{4,5},{5,4},{6,7},{7,6},{8,9},{9,8},{10,11... | collective-permute-start | bytes 2211848 | tf_op jit(solution)/shard_map/decode/ppermute | solution.py:356
  57.0 1.7 fusion.9
  58.9 26.3 %all_to_all.37.g = bf16[8,72,640]{2,1,0:T(8,128)(2,1)S(1)} all-to-all(bf16[8,72,640]{2,1,0:T(8,128)(2,1)S(1)} %get-tuple-element.29), channel_id=1, replica_groups={{0,2,4,6,8,10,12,14},{57,59,61,63,1,3,5,7},{16,18,20,22,24,26,28,30},{9..., dimensions={0} | all-to-all | bytes 1474560 | tf_op jit(solution)/shard_map/decode/all_to_all | solution.py:323
  86.1 9.0 %all-to-all-start.3 = ((bf16[4,72,640]{2,1,0:T(8,128)(2,1)}), bf16[4,72,640]{2,1,0:T(8,128)(2,1)S(1)}, u32[]{:S(2)}, u32[]{:S(2)}) async-start(bf16[4,72,640]{2,1,0:T(8,128)(2,1)} %near_sum.1), calls=%async_computation.3 | async-start | bytes 737280 | tf_op jit(solution)/shard_map/error/all_to_all | solution.py:323
  95.3 1.9 collective-permute-start.1
  97.3 2.4 %collective-permute-done.1 = f32[512]{0:T(512)S(1)} collective-permute-done((f32[512]{0:T(512)S(1)}, f32[512]{0:T(512)S(1)}, u32[]{:S(2)}, u32[]{:S(2)}) %collective-permute-start.1) | collective-permute-done | bytes 2080 | tf_op jit(solution)/shard_map/norms/ppermute | solution.py:368
  99.7 2.5 %collective-permute-start.2 = (f32[512]{0:T(512)S(1)}, f32[512]{0:T(512)S(1)}, u32[]{:S(2)}, u32[]{:S(2)}) collective-permute-start(f32[512]{0:T(512)S(1)} %add.38), channel_id=1, source_target_pairs={{0,384},{64,448},{128,256},{192,320},{256,128},{320,192},{384,0},{... | collective-permute-start | bytes 6152 | tf_op jit(solution)/shard_map/norms/ppermute | solution.py:368
  102.2 3.3 %collective-permute-done.2 = f32[512]{0:T(512)S(1)} collective-permute-done((f32[512]{0:T(512)S(1)}, f32[512]{0:T(512)S(1)}, u32[]{:S(2)}, u32[]{:S(2)}) %collective-permute-start.2) | collective-permute-done | bytes 2080 | tf_op jit(solution)/shard_map/norms/ppermute | solution.py:368
  105.5 3.1 %collective-permute-start.3 = (f32[512]{0:T(512)S(1)}, f32[512]{0:T(512)S(1)}, u32[]{:S(2)}, u32[]{:S(2)}) collective-permute-start(f32[512]{0:T(512)S(1)} %add.39), channel_id=1, source_target_pairs={{0,64},{64,0},{128,192},{192,128},{256,320},{320,256},{384,448},{4... | collective-permute-start | bytes 6152 | tf_op jit(solution)/shard_map/norms/ppermute | solution.py:368
  108.8 2.8 %collective-permute-done.3 = f32[512]{0:T(512)S(1)} collective-permute-done((f32[512]{0:T(512)S(1)}, f32[512]{0:T(512)S(1)}, u32[]{:S(2)}, u32[]{:S(2)}) %collective-permute-start.3) | collective-permute-done | bytes 2080 | tf_op jit(solution)/shard_map/norms/ppermute | solution.py:368
  111.6 1.9 all-to-all-done.3.g
  113.7 26.2 %all_to_all.38 = bf16[8,72,640]{2,1,0:T(8,128)(2,1)S(1)} all-to-all(bf16[8,72,640]{2,1,0:T(8,128)(2,1)S(1)} %error.1), channel_id=1, replica_groups={{0,2,4,6,8,10,12,14},{57,59,61,63,1,3,5,7},{16,18,20,22,24,26,28,30},{9..., dimensions={0} | all-to-all | bytes 1474560 | tf_op jit(solution)/shard_map/error/all_to_all | solution.py:323
  139.8 1.9 collective-permute-start.4
  141.7 1.5 back_half.2.refs_0_
  143.9 1.5 back_half.3
  145.4 3.6 %all-to-all-start.5 = ((bf16[8,64,1280]{2,1,0:T(8,128)(2,1)}), bf16[8,64,1280]{2,1,0:T(8,128)(2,1)S(1)}, u32[]{:S(2)}, u32[]{:S(2)}) async-start(bf16[8,64,1280]{2,1,0:T(8,128)(2,1)} %bitcast.16), calls=%async_computation.5 | async-start | bytes 2621440 | tf_op jit(solution)/shard_map/back/all_to_all | solution.py:323
  149.0 1.6 convert_reduce_fusion
  152.9 3.7 %fusion.4 = f32[576,512]{1,0:T(8,128)} fusion(bf16[512,1280]{1,0:T(8,128)(2,1)} %bitcast.43, bf16[576,640]{1,0:T(8,128)(2,1)} %copy-done.2, bf16[576,640]{1,0:T(8,128)(2,1)S(1)} %bitcast.31, f32[512]{0:T(512)S(1)} %div.23, bf16[512,576]{0,1:T(8,128)(2,1)} %param.8), kind=kOutput, calls=%fused_computation.7 | convolution fusion | flops 758808576 | bytes 4556800 | tf_op jit(solution)/shard_map/decoder_grads/dot_general | solution.py:50
  156.7 12.2 %all-to-all-done.5.g = bf16[8,64,1280]{2,1,0:T(8,128)(2,1)S(1)} async-done(((bf16[8,64,1280]{2,1,0:T(8,128)(2,1)}), bf16[8,64,1280]{2,1,0:T(8,128)(2,1)S(1)}, u32[]{:S(2)}, u32[]{:S(2)}) %all-to-all-start.5) | async-done | bytes 1310752 | tf_op jit(solution)/shard_map/back/all_to_all | solution.py:323
  169.4 21.8 %all_to_all.39 = bf16[8,64,1280]{2,1,0:T(8,128)(2,1)S(1)} all-to-all(bf16[8,64,1280]{2,1,0:T(8,128)(2,1)S(1)} %weigh.1), channel_id=1, replica_groups=mesh['layer'=8,'latent'=64] {'layer'}, dimensions={0} | all-to-all | bytes 2621440 | tf_op jit(solution)/shard_map/encoder_grads/all_to_all | solution.py:323
  191.1 2.8 %encoder_grads.1 = (f32[576,512]{1,0:T(8,128)}, f32[1,512]{1,0:T(1,128)}) custom-call(s32[1]{0:T(128)} %bitcast.c, bf16[576,1280]{1,0:T(8,128)(2,1)S(1)} %bitcast.33, bf16[512,1280]{1,0:T(8,128)(2,1)S(1)} %bitcast.35), custom_call_target="tpu_custom_call" | custom-call | tf_op jit(solution)/shard_map/encoder_grads/encoder_grads/pallas_call | solution.py:313
  (39 shorter events, 6.3 us)
Async XLA Ops:
  0.6 108.0 %copy-start = (f32[576]{0:T(1024)S(1)}, f32[576]{0:T(1024)}, u32[]{:S(2)}) copy-start(f32[576]{0:T(1024)} %param.9) | copy-start | bytes 6916
  5.4 24.8 %copy-start.6 = (f32[64,1280]{1,0:T(8,128)S(1)}, f32[64,1280]{1,0:T(8,128)}, u32[]{:S(2)}) copy-start(f32[64,1280]{1,0:T(8,128)} %get-tuple-element.27.o) | copy-start | bytes 983044
  30.7 19.1 %copy-start.4 = (f32[64,1280]{1,0:T(8,128)}, f32[64,1280]{1,0:T(8,128)S(1)}, u32[]{:S(2)}) copy-start(f32[64,1280]{1,0:T(8,128)S(1)} %get-tuple-element.38.s) | copy-start | bytes 983044
  30.7 19.1 %copy-start.3 = (bf16[512,576]{0,1:T(8,128)(2,1)S(1)}, bf16[512,576]{0,1:T(8,128)(2,1)}, u32[]{:S(2)}) copy-start(bf16[512,576]{0,1:T(8,128)(2,1)} %param.8) | copy-start | bytes 1769476
  49.7 7.2 %copy-start.7 = (bf16[8,64,1280]{2,1,0:T(8,128)(2,1)}, bf16[8,64,1280]{2,1,0:T(8,128)(2,1)S(1)}, u32[]{:S(2)}) copy-start(bf16[8,64,1280]{2,1,0:T(8,128)(2,1)S(1)} %all_to_all.36) | copy-start | bytes 3932164
  50.4 8.4 %collective-permute-start = (bf16[576,640]{1,0:T(8,128)(2,1)S(1)}, bf16[576,640]{1,0:T(8,128)(2,1)S(1)}, u32[]{:S(2)}, u32[]{:S(2)}) collective-permute-start(bf16[576,640]{1,0:T(8,128)(2,1)S(1)} %fusion.7), channel_id=1, source_target_pairs={{0,1},{1,0},{2,3},{3,2},{4,5},{5,4},{6,7},{7,6},{8,9},{9,8},{10,11... | collective-permute-start | bytes 2211848 | tf_op jit(solution)/shard_map/decode/ppermute | solution.py:356
  85.2 17.0 %copy-start.1 = (bf16[1280,576]{0,1:T(8,128)(2,1)S(1)}, bf16[1280,576]{0,1:T(8,128)(2,1)}, u32[]{:S(2)}) copy-start(bf16[1280,576]{0,1:T(8,128)(2,1)} %param.5) | copy-start | bytes 4423684
  86.1 27.4 %all-to-all-start.3 = ((bf16[4,72,640]{2,1,0:T(8,128)(2,1)}), bf16[4,72,640]{2,1,0:T(8,128)(2,1)S(1)}, u32[]{:S(2)}, u32[]{:S(2)}) async-start(bf16[4,72,640]{2,1,0:T(8,128)(2,1)} %near_sum.1), calls=%async_computation.3 | async-start | bytes 737280 | tf_op jit(solution)/shard_map/error/all_to_all | solution.py:323
  95.3 4.3 %collective-permute-start.1 = (f32[512]{0:T(512)S(1)}, f32[512]{0:T(512)S(1)}, u32[]{:S(2)}, u32[]{:S(2)}) collective-permute-start(f32[512]{0:T(512)S(1)} %bitcast.39), channel_id=1, source_target_pairs={{0,128},{64,192},{128,0},{192,64},{256,384},{320,448},{384,256},{4... | collective-permute-start | bytes 6152 | tf_op jit(solution)/shard_map/norms/ppermute | solution.py:368
  99.7 5.8 %collective-permute-start.2 = (f32[512]{0:T(512)S(1)}, f32[512]{0:T(512)S(1)}, u32[]{:S(2)}, u32[]{:S(2)}) collective-permute-start(f32[512]{0:T(512)S(1)} %add.38), channel_id=1, source_target_pairs={{0,384},{64,448},{128,256},{192,320},{256,128},{320,192},{384,0},{... | collective-permute-start | bytes 6152 | tf_op jit(solution)/shard_map/norms/ppermute | solution.py:368
  105.5 6.1 %collective-permute-start.3 = (f32[512]{0:T(512)S(1)}, f32[512]{0:T(512)S(1)}, u32[]{:S(2)}, u32[]{:S(2)}) collective-permute-start(f32[512]{0:T(512)S(1)} %add.39), channel_id=1, source_target_pairs={{0,64},{64,0},{128,192},{192,128},{256,320},{320,256},{384,448},{4... | collective-permute-start | bytes 6152 | tf_op jit(solution)/shard_map/norms/ppermute | solution.py:368
  139.8 4.1 %collective-permute-start.4 = (bf16[576,640]{1,0:T(8,128)(2,1)S(1)}, bf16[576,640]{1,0:T(8,128)(2,1)S(1)}, u32[]{:S(2)}, u32[]{:S(2)}) collective-permute-start(bf16[576,640]{1,0:T(8,128)(2,1)S(1)} %bitcast.29), channel_id=1, source_target_pairs={{0,1},{1,0},{2,3},{3,2},{4,5},{5,4},{6,7},{7,6},{8,9},{9,8},{10,11... | collective-permute-start | bytes 2211848 | tf_op jit(solution)/shard_map/error/ppermute | solution.py:378
  143.9 1.5 copy-start.2
  145.4 23.5 %all-to-all-start.5 = ((bf16[8,64,1280]{2,1,0:T(8,128)(2,1)}), bf16[8,64,1280]{2,1,0:T(8,128)(2,1)S(1)}, u32[]{:S(2)}, u32[]{:S(2)}) async-start(bf16[8,64,1280]{2,1,0:T(8,128)(2,1)} %bitcast.16), calls=%async_computation.5 | async-start | bytes 2621440 | tf_op jit(solution)/shard_map/back/all_to_all | solution.py:323
  152.9 3.7 %copy-start.5 = (f32[64,1280]{1,0:T(8,128)S(1)}, f32[64,1280]{1,0:T(8,128)}, u32[]{:S(2)}) copy-start(f32[64,1280]{1,0:T(8,128)} %copy-done.4) | copy-start | bytes 983044

commit v6 on v5

--- a/solution.py
+++ b/solution.py
@@ -89,14 +89,14 @@
     piece = feat // loads_of_acts
     size = lat // steps
 
-    def body(c, m, e_hbm, b, a_hbm, out_hbm, own_hbm, acts, e, e_rows, b_rows, out, own, e_sem, a_sems, out_sems):
+    def body(c, m, e_hbm, b_hbm, a_hbm, out_hbm, own_hbm, acts, e, e_rows, b, b_rows, out, own, e_sem, a_sems, out_sems):
         loads = [pltpu.make_async_copy(e_hbm, e, e_sem.at[0])]
         for i in range(loads_of_acts):
             here = slice(i * piece, (i + 1) * piece)
             loads.append(pltpu.make_async_copy(a_hbm.at[here], acts.at[here], a_sems.at[i]))
+        loads.append(pltpu.make_async_copy(b_hbm, b, e_sem.at[1]))
         for load in loads:
             load.start()
-        b_rows[...] = jnp.broadcast_to(b[...], (128, lat)).T
         loads[0].wait()
         e_rows[...] = e[...].T
         for load in loads[1:]:
@@ -109,6 +109,7 @@
                 out[here, side] = dot(e_rows[here], acts[:, half_columns(c[0], rows, j)], ((1,), (0,))).astype(BF16)
             stores.append(pltpu.make_async_copy(out.at[here], out_hbm.at[here], out_sems.at[i]))
             stores[i].start()
+        b_rows[...] = jnp.broadcast_to(b[...], (128, lat)).T
         mine = pl.ds(pl.multiple_of(m[0] * part, part), part)
         for j in range(NC):
             side = slice(j * half, (j + 1) * half)
@@ -121,16 +122,17 @@
     return local_call(
         body, "encode", grant=ALONE,
         out_shape=(like((lat, rows), BF16), like((part, rows), F32)),
-        in_specs=[SMEM, SMEM, HBM, VMEM, HBM],
+        in_specs=[SMEM, SMEM, HBM, HBM, HBM],
         out_specs=(HBM, HBM),
         scratch_shapes=[
             pltpu.VMEM((feat, rows), BF16),
             pltpu.VMEM((feat, lat), BF16),
             pltpu.VMEM((lat, feat), BF16),
+            pltpu.VMEM((1, lat), F32),
             pltpu.VMEM((lat, 128), F32),
             pltpu.VMEM((lat, rows), BF16),
             pltpu.VMEM((part, rows), F32),
-            copies(1),
+            copies(2),
             copies(loads_of_acts),
             copies(steps + 1),
         ],
@@ -289,7 +291,7 @@
     )(got, penalty, slope)
 
 
-def encoder_grads(core, acts_t, delta, steps=3):
+def encoder_grads(core, acts_t, delta, steps=2):
     feat, rows = acts_t.shape
     lat = delta.shape[0]
     size = feat // steps

time: 195 us -> 194 us (level)
  no operation moved by 1% of the time
where the time goes in v6:
time: 194 us; the launch traced here: 193 us
  blocking collectives  118 us (61%)
  starting transfers between devices  28.6 us (15%)
  waiting for transfers between devices  23.4 us (12%)
  Pallas kernels  11.8 us (6%)
  matrix products  6.04 us (3%)
  other arithmetic  3.71 us (2%)
    all_to_all x5, blocking collectives, exchange(): return lax.all_to_all(x, axis, 0, 0, axis_index_groups=groups, tiled=True)  118 us
    all_to_all x2, waiting for transfers between devices, exchange(): return lax.all_to_all(x, axis, 0, 0, axis_index_groups=groups, tiled=True)  14.1 us
    all_to_all x2, starting transfers between devices, exchange(): return lax.all_to_all(x, axis, 0, 0, axis_index_groups=groups, tiled=True)  12.6 us
    ppermute x3, waiting for transfers between devices, per_device(): squares = squares + lax.ppermute(squares, 'layer', pairs)  8.51 us
    ppermute x3, starting transfers between devices, per_device(): squares = squares + lax.ppermute(squares, 'layer', pairs)  7.49 us
    ppermute x1, starting transfers between devices, per_device(): arrived = lax.ppermute(away, 'latent', CORE)  6.56 us
    dot_general x3, matrix products, dot(): return lax.dot_general(a, b, (dims, ((), ())), preferred_element_type=F32)  6.04 us
    pallas_call x1, Pallas kernels, encode(): local_call(body, 'encode', grant=ALONE, out_shape=(like((lat, rows), BF16...  3.91 us
  transfers between devices with their start and end apart: 7, of which 7 were waited for; matrix products, arithmetic and copies ran while one was open for 5% of the time, Pallas kernels for 1%

profile of v6, /device:TPU:1, one launch (start us, length us, event | category | flops | bytes accessed | tf_op | source)
XLA Modules:
  0.0 192.9 jit_solution(11215473841761143531)
XLA Ops:
  0.7 3.9 %encode.1 = (bf16[512,1280]{1,0:T(8,128)(2,1)}, f32[64,1280]{1,0:T(8,128)}) custom-call(s32[1]{0:T(128)} %bitcast.c, s32[1]{0:T(128)} %bitcast.4.m, bf16[576,512]{1,0:T(8,128)(2,1)} %e_hbm.1, f32[1,512]{1,0:T(1,128)} %bitcast.45, bf16[576,1280]{1,0:T(8,128)(2,1)} %bitcast.32), custom_call_target="tpu_custom_call" | custom-call | tf_op jit(solution)/shard_map/encode/encode/pallas_call | solution.py:122
  4.6 24.8 %all_to_all.35.g = bf16[8,64,1280]{2,1,0:T(8,128)(2,1)S(1)} all-to-all(bf16[8,64,1280]{2,1,0:T(8,128)(2,1)} %bitcast.44), channel_id=1, replica_groups=mesh['layer'=8,'latent'=64] {'layer'}, dimensions={0} | all-to-all | bytes 2621440 | tf_op jit(solution)/shard_map/encode/all_to_all | solution.py:325
  29.9 19.1 %all_to_all.36 = bf16[8,64,1280]{2,1,0:T(8,128)(2,1)S(1)} all-to-all(bf16[8,64,1280]{2,1,0:T(8,128)(2,1)S(1)} %get-tuple-element.28), channel_id=1, replica_groups=mesh['layer'=8,'latent'=64] {'layer'}, dimensions={0} | all-to-all | bytes 2621440 | tf_op jit(solution)/shard_map/encode/all_to_all | solution.py:325
  49.6 6.6 %collective-permute-start = (bf16[576,640]{1,0:T(8,128)(2,1)S(1)}, bf16[576,640]{1,0:T(8,128)(2,1)S(1)}, u32[]{:S(2)}, u32[]{:S(2)}) collective-permute-start(bf16[576,640]{1,0:T(8,128)(2,1)S(1)} %fusion.7), channel_id=1, source_target_pairs={{0,1},{1,0},{2,3},{3,2},{4,5},{5,4},{6,7},{7,6},{8,9},{9,8},{10,11... | collective-permute-start | bytes 2211848 | tf_op jit(solution)/shard_map/decode/ppermute | solution.py:358
  56.2 1.7 fusion.9
  58.1 26.3 %all_to_all.37.g = bf16[8,72,640]{2,1,0:T(8,128)(2,1)S(1)} all-to-all(bf16[8,72,640]{2,1,0:T(8,128)(2,1)S(1)} %get-tuple-element.29), channel_id=1, replica_groups={{0,2,4,6,8,10,12,14},{57,59,61,63,1,3,5,7},{16,18,20,22,24,26,28,30},{9..., dimensions={0} | all-to-all | bytes 1474560 | tf_op jit(solution)/shard_map/decode/all_to_all | solution.py:325
  85.3 9.0 %all-to-all-start.3 = ((bf16[4,72,640]{2,1,0:T(8,128)(2,1)}), bf16[4,72,640]{2,1,0:T(8,128)(2,1)S(1)}, u32[]{:S(2)}, u32[]{:S(2)}) async-start(bf16[4,72,640]{2,1,0:T(8,128)(2,1)} %near_sum.1), calls=%async_computation.3 | async-start | bytes 737280 | tf_op jit(solution)/shard_map/error/all_to_all | solution.py:325
  94.6 1.9 collective-permute-start.1
  96.5 2.4 %collective-permute-done.1 = f32[512]{0:T(512)S(1)} collective-permute-done((f32[512]{0:T(512)S(1)}, f32[512]{0:T(512)S(1)}, u32[]{:S(2)}, u32[]{:S(2)}) %collective-permute-start.1) | collective-permute-done | bytes 2080 | tf_op jit(solution)/shard_map/norms/ppermute | solution.py:370
  98.9 2.5 %collective-permute-start.2 = (f32[512]{0:T(512)S(1)}, f32[512]{0:T(512)S(1)}, u32[]{:S(2)}, u32[]{:S(2)}) collective-permute-start(f32[512]{0:T(512)S(1)} %add.38), channel_id=1, source_target_pairs={{0,384},{64,448},{128,256},{192,320},{256,128},{320,192},{384,0},{... | collective-permute-start | bytes 6152 | tf_op jit(solution)/shard_map/norms/ppermute | solution.py:370
  101.4 3.3 %collective-permute-done.2 = f32[512]{0:T(512)S(1)} collective-permute-done((f32[512]{0:T(512)S(1)}, f32[512]{0:T(512)S(1)}, u32[]{:S(2)}, u32[]{:S(2)}) %collective-permute-start.2) | collective-permute-done | bytes 2080 | tf_op jit(solution)/shard_map/norms/ppermute | solution.py:370
  104.7 3.1 %collective-permute-start.3 = (f32[512]{0:T(512)S(1)}, f32[512]{0:T(512)S(1)}, u32[]{:S(2)}, u32[]{:S(2)}) collective-permute-start(f32[512]{0:T(512)S(1)} %add.39), channel_id=1, source_target_pairs={{0,64},{64,0},{128,192},{192,128},{256,320},{320,256},{384,448},{4... | collective-permute-start | bytes 6152 | tf_op jit(solution)/shard_map/norms/ppermute | solution.py:370
  108.0 2.8 %collective-permute-done.3 = f32[512]{0:T(512)S(1)} collective-permute-done((f32[512]{0:T(512)S(1)}, f32[512]{0:T(512)S(1)}, u32[]{:S(2)}, u32[]{:S(2)}) %collective-permute-start.3) | collective-permute-done | bytes 2080 | tf_op jit(solution)/shard_map/norms/ppermute | solution.py:370
  110.8 1.9 all-to-all-done.3.g
  112.9 26.2 %all_to_all.38 = bf16[8,72,640]{2,1,0:T(8,128)(2,1)S(1)} all-to-all(bf16[8,72,640]{2,1,0:T(8,128)(2,1)S(1)} %error.1), channel_id=1, replica_groups={{0,2,4,6,8,10,12,14},{57,59,61,63,1,3,5,7},{16,18,20,22,24,26,28,30},{9..., dimensions={0} | all-to-all | bytes 1474560 | tf_op jit(solution)/shard_map/error/all_to_all | solution.py:325
  139.0 1.9 collective-permute-start.4
  141.0 1.5 back_half.2.refs_0_
  143.1 1.5 back_half.3
  144.7 3.6 %all-to-all-start.5 = ((bf16[8,64,1280]{2,1,0:T(8,128)(2,1)}), bf16[8,64,1280]{2,1,0:T(8,128)(2,1)S(1)}, u32[]{:S(2)}, u32[]{:S(2)}) async-start(bf16[8,64,1280]{2,1,0:T(8,128)(2,1)} %bitcast.16), calls=%async_computation.5 | async-start | bytes 2621440 | tf_op jit(solution)/shard_map/back/all_to_all | solution.py:325
  148.2 1.6 convert_reduce_fusion
  152.1 3.7 %fusion.4 = f32[576,512]{1,0:T(8,128)} fusion(bf16[512,1280]{1,0:T(8,128)(2,1)} %bitcast.43, bf16[576,640]{1,0:T(8,128)(2,1)} %copy-done.2, bf16[576,640]{1,0:T(8,128)(2,1)S(1)} %bitcast.31, f32[512]{0:T(512)S(1)} %div.23, bf16[512,576]{0,1:T(8,128)(2,1)} %param.8), kind=kOutput, calls=%fused_computation.7 | convolution fusion | flops 758808576 | bytes 4556800 | tf_op jit(solution)/shard_map/decoder_grads/dot_general | solution.py:50
  155.9 12.2 %all-to-all-done.5.g = bf16[8,64,1280]{2,1,0:T(8,128)(2,1)S(1)} async-done(((bf16[8,64,1280]{2,1,0:T(8,128)(2,1)}), bf16[8,64,1280]{2,1,0:T(8,128)(2,1)S(1)}, u32[]{:S(2)}, u32[]{:S(2)}) %all-to-all-start.5) | async-done | bytes 1310752 | tf_op jit(solution)/shard_map/back/all_to_all | solution.py:325
  168.6 21.8 %all_to_all.39 = bf16[8,64,1280]{2,1,0:T(8,128)(2,1)S(1)} all-to-all(bf16[8,64,1280]{2,1,0:T(8,128)(2,1)S(1)} %weigh.1), channel_id=1, replica_groups=mesh['layer'=8,'latent'=64] {'layer'}, dimensions={0} | all-to-all | bytes 2621440 | tf_op jit(solution)/shard_map/encoder_grads/all_to_all | solution.py:325
  190.3 2.5 %encoder_grads.1 = (f32[576,512]{1,0:T(8,128)}, f32[1,512]{1,0:T(1,128)}) custom-call(s32[1]{0:T(128)} %bitcast.c, bf16[576,1280]{1,0:T(8,128)(2,1)S(1)} %bitcast.33, bf16[512,1280]{1,0:T(8,128)(2,1)S(1)} %bitcast.35), custom_call_target="tpu_custom_call" | custom-call | tf_op jit(solution)/shard_map/encoder_grads/encoder_grads/pallas_call | solution.py:315
  (39 shorter events, 6.3 us)
Async XLA Ops:
  0.6 107.2 %copy-start = (f32[576]{0:T(1024)S(1)}, f32[576]{0:T(1024)}, u32[]{:S(2)}) copy-start(f32[576]{0:T(1024)} %param.9) | copy-start | bytes 6916
  4.6 24.8 %copy-start.6 = (f32[64,1280]{1,0:T(8,128)S(1)}, f32[64,1280]{1,0:T(8,128)}, u32[]{:S(2)}) copy-start(f32[64,1280]{1,0:T(8,128)} %get-tuple-element.27.o) | copy-start | bytes 983044
  29.9 19.1 %copy-start.4 = (f32[64,1280]{1,0:T(8,128)}, f32[64,1280]{1,0:T(8,128)S(1)}, u32[]{:S(2)}) copy-start(f32[64,1280]{1,0:T(8,128)S(1)} %get-tuple-element.38.s) | copy-start | bytes 983044
  29.9 19.1 %copy-start.3 = (bf16[512,576]{0,1:T(8,128)(2,1)S(1)}, bf16[512,576]{0,1:T(8,128)(2,1)}, u32[]{:S(2)}) copy-start(bf16[512,576]{0,1:T(8,128)(2,1)} %param.8) | copy-start | bytes 1769476
  49.0 7.2 %copy-start.7 = (bf16[8,64,1280]{2,1,0:T(8,128)(2,1)}, bf16[8,64,1280]{2,1,0:T(8,128)(2,1)S(1)}, u32[]{:S(2)}) copy-start(bf16[8,64,1280]{2,1,0:T(8,128)(2,1)S(1)} %all_to_all.36) | copy-start | bytes 3932164
  49.6 8.4 %collective-permute-start = (bf16[576,640]{1,0:T(8,128)(2,1)S(1)}, bf16[576,640]{1,0:T(8,128)(2,1)S(1)}, u32[]{:S(2)}, u32[]{:S(2)}) collective-permute-start(bf16[576,640]{1,0:T(8,128)(2,1)S(1)} %fusion.7), channel_id=1, source_target_pairs={{0,1},{1,0},{2,3},{3,2},{4,5},{5,4},{6,7},{7,6},{8,9},{9,8},{10,11... | collective-permute-start | bytes 2211848 | tf_op jit(solution)/shard_map/decode/ppermute | solution.py:358
  84.4 17.0 %copy-start.1 = (bf16[1280,576]{0,1:T(8,128)(2,1)S(1)}, bf16[1280,576]{0,1:T(8,128)(2,1)}, u32[]{:S(2)}) copy-start(bf16[1280,576]{0,1:T(8,128)(2,1)} %param.5) | copy-start | bytes 4423684
  85.3 27.4 %all-to-all-start.3 = ((bf16[4,72,640]{2,1,0:T(8,128)(2,1)}), bf16[4,72,640]{2,1,0:T(8,128)(2,1)S(1)}, u32[]{:S(2)}, u32[]{:S(2)}) async-start(bf16[4,72,640]{2,1,0:T(8,128)(2,1)} %near_sum.1), calls=%async_computation.3 | async-start | bytes 737280 | tf_op jit(solution)/shard_map/error/all_to_all | solution.py:325
  94.6 4.3 %collective-permute-start.1 = (f32[512]{0:T(512)S(1)}, f32[512]{0:T(512)S(1)}, u32[]{:S(2)}, u32[]{:S(2)}) collective-permute-start(f32[512]{0:T(512)S(1)} %bitcast.39), channel_id=1, source_target_pairs={{0,128},{64,192},{128,0},{192,64},{256,384},{320,448},{384,256},{4... | collective-permute-start | bytes 6152 | tf_op jit(solution)/shard_map/norms/ppermute | solution.py:370
  98.9 5.8 %collective-permute-start.2 = (f32[512]{0:T(512)S(1)}, f32[512]{0:T(512)S(1)}, u32[]{:S(2)}, u32[]{:S(2)}) collective-permute-start(f32[512]{0:T(512)S(1)} %add.38), channel_id=1, source_target_pairs={{0,384},{64,448},{128,256},{192,320},{256,128},{320,192},{384,0},{... | collective-permute-start | bytes 6152 | tf_op jit(solution)/shard_map/norms/ppermute | solution.py:370
  104.7 6.1 %collective-permute-start.3 = (f32[512]{0:T(512)S(1)}, f32[512]{0:T(512)S(1)}, u32[]{:S(2)}, u32[]{:S(2)}) collective-permute-start(f32[512]{0:T(512)S(1)} %add.39), channel_id=1, source_target_pairs={{0,64},{64,0},{128,192},{192,128},{256,320},{320,256},{384,448},{4... | collective-permute-start | bytes 6152 | tf_op jit(solution)/shard_map/norms/ppermute | solution.py:370
  139.0 4.1 %collective-permute-start.4 = (bf16[576,640]{1,0:T(8,128)(2,1)S(1)}, bf16[576,640]{1,0:T(8,128)(2,1)S(1)}, u32[]{:S(2)}, u32[]{:S(2)}) collective-permute-start(bf16[576,640]{1,0:T(8,128)(2,1)S(1)} %bitcast.29), channel_id=1, source_target_pairs={{0,1},{1,0},{2,3},{3,2},{4,5},{5,4},{6,7},{7,6},{8,9},{9,8},{10,11... | collective-permute-start | bytes 2211848 | tf_op jit(solution)/shard_map/error/ppermute | solution.py:380
  143.1 1.5 copy-start.2
  144.7 23.5 %all-to-all-start.5 = ((bf16[8,64,1280]{2,1,0:T(8,128)(2,1)}), bf16[8,64,1280]{2,1,0:T(8,128)(2,1)S(1)}, u32[]{:S(2)}, u32[]{:S(2)}) async-start(bf16[8,64,1280]{2,1,0:T(8,128)(2,1)} %bitcast.16), calls=%async_computation.5 | async-start | bytes 2621440 | tf_op jit(solution)/shard_map/back/all_to_all | solution.py:325
  152.1 3.7 %copy-start.5 = (f32[64,1280]{1,0:T(8,128)S(1)}, f32[64,1280]{1,0:T(8,128)}, u32[]{:S(2)}) copy-start(f32[64,1280]{1,0:T(8,128)} %copy-done.4) | copy-start | bytes 983044

commit v7 on v6

--- a/solution.py
+++ b/solution.py
@@ -81,20 +81,18 @@
     return pl.ds(pl.multiple_of(lax.rem(core + i, NC) * half, half), half)
 
 
-def encode(core, me, enc, bias, acts_t, loads_of_acts=4, steps=2):
+def encode(core, enc, acts_t, loads_of_acts=4, steps=2):
     feat, lat = enc.shape
     rows = acts_t.shape[1]
     half = rows // NC
-    part = lat // (NY * NXH)
     piece = feat // loads_of_acts
     size = lat // steps
 
-    def body(c, m, e_hbm, b_hbm, a_hbm, out_hbm, own_hbm, acts, e, e_rows, b, b_rows, out, own, e_sem, a_sems, out_sems):
+    def body(c, e_hbm, a_hbm, out_hbm, acts, e, e_rows, out, e_sem, a_sems, out_sems):
         loads = [pltpu.make_async_copy(e_hbm, e, e_sem.at[0])]
         for i in range(loads_of_acts):
             here = slice(i * piece, (i + 1) * piece)
             loads.append(pltpu.make_async_copy(a_hbm.at[here], acts.at[here], a_sems.at[i]))
-        loads.append(pltpu.make_async_copy(b_hbm, b, e_sem.at[1]))
         for load in loads:
             load.start()
         loads[0].wait()
@@ -109,32 +107,61 @@
                 out[here, side] = dot(e_rows[here], acts[:, half_columns(c[0], rows, j)], ((1,), (0,))).astype(BF16)
             stores.append(pltpu.make_async_copy(out.at[here], out_hbm.at[here], out_sems.at[i]))
             stores[i].start()
+        for store in stores:
+            store.wait()
+
+    return local_call(
+        body, "encode", grant=ALONE,
+        out_shape=like((lat, rows), BF16),
+        in_specs=[SMEM, HBM, HBM],
+        out_specs=HBM,
+        scratch_shapes=[
+            pltpu.VMEM((feat, rows), BF16),
+            pltpu.VMEM((feat, lat), BF16),
+            pltpu.VMEM((lat, feat), BF16),
+            pltpu.VMEM((lat, rows), BF16),
+            copies(1),
+            copies(loads_of_acts),
+            copies(steps),
+        ],
+    )(core, enc, acts_t)
+
+
+def own_block(core, me, enc, bias, acts_t):
+    feat, lat = enc.shape
+    rows = acts_t.shape[1]
+    half = rows // NC
+    part = lat // (NY * NXH)
+
+    def body(c, m, e_hbm, b_hbm, a_hbm, own, acts, e, e_rows, b, b_rows, sems):
+        loads = [
+            pltpu.make_async_copy(e_hbm, e, sems.at[0]),
+            pltpu.make_async_copy(b_hbm, b, sems.at[1]),
+            pltpu.make_async_copy(a_hbm, acts, sems.at[2]),
+        ]
+        for load in loads:
+            load.start()
+        for load in loads:
+            load.wait()
+        e_rows[...] = e[...].T
         b_rows[...] = jnp.broadcast_to(b[...], (128, lat)).T
         mine = pl.ds(pl.multiple_of(m[0] * part, part), part)
         for j in range(NC):
             side = slice(j * half, (j + 1) * half)
             own[:, side] = dot(e_rows[mine], acts[:, half_columns(c[0], rows, j)], ((1,), (0,))) + b_rows[mine][:, :1]
-        stores.append(pltpu.make_async_copy(own, own_hbm, out_sems.at[steps]))
-        stores[steps].start()
-        for store in stores:
-            store.wait()
-
-    return local_call(
-        body, "encode", grant=ALONE,
-        out_shape=(like((lat, rows), BF16), like((part, rows), F32)),
+
+    return local_call(
+        body, "own_block", grant=ALONE,
+        out_shape=like((part, rows), F32),
         in_specs=[SMEM, SMEM, HBM, HBM, HBM],
-        out_specs=(HBM, HBM),
+        out_specs=VMEM,
         scratch_shapes=[
             pltpu.VMEM((feat, rows), BF16),
             pltpu.VMEM((feat, lat), BF16),
             pltpu.VMEM((lat, feat), BF16),
             pltpu.VMEM((1, lat), F32),
             pltpu.VMEM((lat, 128), F32),
-            pltpu.VMEM((lat, rows), BF16),
-            pltpu.VMEM((part, rows), F32),
-            copies(2),
-            copies(loads_of_acts),
-            copies(steps + 1),
+            copies(3),
         ],
     )(core, me, enc, bias, acts_t)
 
@@ -348,7 +375,9 @@
     acts_t = acts.T
     dec_t = dec_weight.T
     with jax.named_scope("encode"):
-        partial_pre, own_pre = encode(core_ref, layer_ref, enc_weight, enc_bias.reshape(1, lat), acts_t)
+        partial_pre = encode(core_ref, enc_weight, acts_t)
+        late_bias, partial_pre = lax.optimization_barrier((enc_bias.reshape(1, lat), partial_pre))
+        own_pre = own_block(core_ref, layer_ref, enc_weight, late_bias, acts_t)
         got = exchange(partial_pre.reshape(n_layer, part, rows), "layer")
         codes_part, slope = activate(layer_ref, got, own_pre)
         codes = exchange(codes_part, "layer").reshape(lat, rows)

time: 194 us -> 197 us (1.015)
  blocking collectives: 118 us -> 95.3 us
  waiting for transfers between devices: 23.4 us -> 38.1 us
  starting transfers between devices: 28.6 us -> 35.2 us
  Pallas kernels: 11.8 us -> 14.7 us
  local copies, waits for them, and re-layouts: 0.39 us -> 3.05 us
    all_to_all x5 -> x4, blocking collectives: 118 us -> 95.3 us  [exchange(): return lax.all_to_all(x, axis, 0, 0, axis_index_groups=groups, tiled=True)]
    all_to_all x2 -> x3, waiting for transfers between devices: 14.1 us -> 27.5 us  [exchange(): return lax.all_to_all(x, axis, 0, 0, axis_index_groups=groups, tiled=True)]
    all_to_all x2 -> x3, starting transfers between devices: 12.6 us -> 20.1 us  [exchange(): return lax.all_to_all(x, axis, 0, 0, axis_index_groups=groups, tiled=True)]
    pallas_call x1 -> x2, Pallas kernels: 3.91 us -> 6.81 us  [the longest x1 3.9 us: encode(): local_call(body, 'encode', grant=ALONE, out_shape=like((lat, rows), BF16)...]
    unnamed x16 -> x20, local copies, waits for them, and re-layouts: 0.04 us -> 2.7 us
  transfers between devices with their start and end apart: 7 -> 8, of which waited for: 7 -> 8; matrix products, arithmetic and copies ran while one was open for 5% -> 4% of each run, Pallas kernels for 1% -> 2%
where the time goes in v7:
time: 197 us; the launch traced here: 196 us
  blocking collectives  95.3 us (48%)
  waiting for transfers between devices  38.1 us (19%)
  starting transfers between devices  35.2 us (18%)
  Pallas kernels  14.7 us (7%)
  matrix products  4.94 us (3%)
  other arithmetic  3.71 us (2%)
  local copies, waits for them, and re-layouts  3.05 us (2%)
    all_to_all x4, blocking collectives, exchange(): return lax.all_to_all(x, axis, 0, 0, axis_index_groups=groups, tiled=True)  95.3 us
    all_to_all x3, waiting for transfers between devices, exchange(): return lax.all_to_all(x, axis, 0, 0, axis_index_groups=groups, tiled=True)  27.5 us
    all_to_all x3, starting transfers between devices, exchange(): return lax.all_to_all(x, axis, 0, 0, axis_index_groups=groups, tiled=True)  20.1 us
    ppermute x3, waiting for transfers between devices, per_device(): squares = squares + lax.ppermute(squares, 'layer', pairs)  8.73 us
    ppermute x3, starting transfers between devices, per_device(): squares = squares + lax.ppermute(squares, 'layer', pairs)  7.27 us
    ppermute x1, starting transfers between devices, per_device(): arrived = lax.ppermute(away, 'latent', CORE)  5.84 us
    dot_general x3, matrix products, dot(): return lax.dot_general(a, b, (dims, ((), ())), preferred_element_type=F32)  4.94 us
  transfers between devices with their start and end apart: 8, of which 8 were waited for; matrix products, arithmetic and copies ran while one was open for 4% of the time, Pallas kernels for 2%

profile of v7, /device:TPU:1, one launch (start us, length us, event | category | flops | bytes accessed | tf_op | source)
XLA Modules:
  0.0 195.9 jit_solution(8967905155148071174)
XLA Ops:
  0.7 3.9 %encode.1 = bf16[512,1280]{1,0:T(8,128)(2,1)} custom-call(s32[1]{0:T(128)} %bitcast.c, bf16[576,512]{1,0:T(8,128)(2,1)} %e_hbm.3, bf16[576,1280]{1,0:T(8,128)(2,1)} %bitcast.29), custom_call_target="tpu_custom_call" | custom-call | tf_op jit(solution)/shard_map/encode/encode/pallas_call | solution.py:113
  4.6 7.5 %all-to-all-start = ((bf16[8,64,1280]{2,1,0:T(8,128)(2,1)}), bf16[8,64,1280]{2,1,0:T(8,128)(2,1)S(1)}, u32[]{:S(2)}, u32[]{:S(2)}) async-start(bf16[8,64,1280]{2,1,0:T(8,128)(2,1)} %bitcast.45), calls=%async_computation | async-start | bytes 2621440 | tf_op jit(solution)/shard_map/encode/all_to_all | solution.py:352
  12.0 2.9 %own_block.1.o = f32[64,1280]{1,0:T(8,128)} custom-call(s32[1]{0:T(128)} %bitcast.c, s32[1]{0:T(128)} %bitcast.4.m, bf16[576,512]{1,0:T(8,128)(2,1)} %e_hbm.3, f32[1,512]{1,0:T(1,128)} %bitcast.46, bf16[576,1280]{1,0:T(8,128)(2,1)} %bitcast.30), custom_call_target="tpu_custom_call" | custom-call | tf_op jit(solution)/shard_map/encode/own_block/pallas_call | solution.py:153
  15.0 14.2 %all-to-all-done.g = bf16[8,64,1280]{2,1,0:T(8,128)(2,1)S(1)} async-done(((bf16[8,64,1280]{2,1,0:T(8,128)(2,1)}), bf16[8,64,1280]{2,1,0:T(8,128)(2,1)S(1)}, u32[]{:S(2)}, u32[]{:S(2)}) %all-to-all-start) | async-done | bytes 1310752 | tf_op jit(solution)/shard_map/encode/all_to_all | solution.py:352
  30.7 20.5 %all_to_all.35 = bf16[8,64,1280]{2,1,0:T(8,128)(2,1)S(1)} all-to-all(bf16[8,64,1280]{2,1,0:T(8,128)(2,1)S(1)} %get-tuple-element.28), channel_id=1, replica_groups=mesh['layer'=8,'latent'=64] {'layer'}, dimensions={0} | all-to-all | bytes 2621440 | tf_op jit(solution)/shard_map/encode/all_to_all | solution.py:352
  51.8 5.8 %collective-permute-start = (bf16[576,640]{1,0:T(8,128)(2,1)S(1)}, bf16[576,640]{1,0:T(8,128)(2,1)S(1)}, u32[]{:S(2)}, u32[]{:S(2)}) collective-permute-start(bf16[576,640]{1,0:T(8,128)(2,1)S(1)} %fusion.7), channel_id=1, source_target_pairs={{0,1},{1,0},{2,3},{3,2},{4,5},{5,4},{6,7},{7,6},{8,9},{9,8},{10,11... | collective-permute-start | bytes 2211848 | tf_op jit(solution)/shard_map/decode/ppermute | solution.py:387
  59.7 26.8 %all_to_all.36.g = bf16[8,72,640]{2,1,0:T(8,128)(2,1)S(1)} all-to-all(bf16[8,72,640]{2,1,0:T(8,128)(2,1)S(1)} %get-tuple-element.29), channel_id=1, replica_groups={{0,2,4,6,8,10,12,14},{57,59,61,63,1,3,5,7},{16,18,20,22,24,26,28,30},{9..., dimensions={0} | all-to-all | bytes 1474560 | tf_op jit(solution)/shard_map/decode/all_to_all | solution.py:352
  87.3 9.1 %all-to-all-start.3 = ((bf16[4,72,640]{2,1,0:T(8,128)(2,1)}), bf16[4,72,640]{2,1,0:T(8,128)(2,1)S(1)}, u32[]{:S(2)}, u32[]{:S(2)}) async-start(bf16[4,72,640]{2,1,0:T(8,128)(2,1)} %near_sum.1), calls=%async_computation.3 | async-start | bytes 737280 | tf_op jit(solution)/shard_map/error/all_to_all | solution.py:352
  96.6 1.9 collective-permute-start.1
  98.6 2.4 %collective-permute-done.1 = f32[512]{0:T(512)S(1)} collective-permute-done((f32[512]{0:T(512)S(1)}, f32[512]{0:T(512)S(1)}, u32[]{:S(2)}, u32[]{:S(2)}) %collective-permute-start.1) | collective-permute-done | bytes 2080 | tf_op jit(solution)/shard_map/norms/ppermute | solution.py:399
  101.0 2.4 %collective-permute-start.2 = (f32[512]{0:T(512)S(1)}, f32[512]{0:T(512)S(1)}, u32[]{:S(2)}, u32[]{:S(2)}) collective-permute-start(f32[512]{0:T(512)S(1)} %add.38), channel_id=1, source_target_pairs={{0,384},{64,448},{128,256},{192,320},{256,128},{320,192},{384,0},{... | collective-permute-start | bytes 6152 | tf_op jit(solution)/shard_map/norms/ppermute | solution.py:399
  103.4 3.4 %collective-permute-done.2 = f32[512]{0:T(512)S(1)} collective-permute-done((f32[512]{0:T(512)S(1)}, f32[512]{0:T(512)S(1)}, u32[]{:S(2)}, u32[]{:S(2)}) %collective-permute-start.2) | collective-permute-done | bytes 2080 | tf_op jit(solution)/shard_map/norms/ppermute | solution.py:399
  106.8 3.0 %collective-permute-start.3 = (f32[512]{0:T(512)S(1)}, f32[512]{0:T(512)S(1)}, u32[]{:S(2)}, u32[]{:S(2)}) collective-permute-start(f32[512]{0:T(512)S(1)} %add.39), channel_id=1, source_target_pairs={{0,64},{64,0},{128,192},{192,128},{256,320},{320,256},{384,448},{4... | collective-permute-start | bytes 6152 | tf_op jit(solution)/shard_map/norms/ppermute | solution.py:399
  110.0 2.9 %collective-permute-done.3 = f32[512]{0:T(512)S(1)} collective-permute-done((f32[512]{0:T(512)S(1)}, f32[512]{0:T(512)S(1)}, u32[]{:S(2)}, u32[]{:S(2)}) %collective-permute-start.3) | collective-permute-done | bytes 2080 | tf_op jit(solution)/shard_map/norms/ppermute | solution.py:399
  112.9 1.8 all-to-all-done.3.g
  114.8 26.3 %all_to_all.37 = bf16[8,72,640]{2,1,0:T(8,128)(2,1)S(1)} all-to-all(bf16[8,72,640]{2,1,0:T(8,128)(2,1)S(1)} %error.1), channel_id=1, replica_groups={{0,2,4,6,8,10,12,14},{57,59,61,63,1,3,5,7},{16,18,20,22,24,26,28,30},{9..., dimensions={0} | all-to-all | bytes 1474560 | tf_op jit(solution)/shard_map/error/all_to_all | solution.py:352
  141.1 1.9 collective-permute-start.4
  145.2 1.5 back_half.3
  146.7 3.6 %all-to-all-start.5 = ((bf16[8,64,1280]{2,1,0:T(8,128)(2,1)}), bf16[8,64,1280]{2,1,0:T(8,128)(2,1)S(1)}, u32[]{:S(2)}, u32[]{:S(2)}) async-start(bf16[8,64,1280]{2,1,0:T(8,128)(2,1)} %bitcast.16), calls=%async_computation.5 | async-start | bytes 2621440 | tf_op jit(solution)/shard_map/back/all_to_all | solution.py:352
  150.3 1.6 convert_reduce_fusion
  154.2 3.7 %fusion.4 = f32[576,512]{1,0:T(8,128)} fusion(bf16[512,1280]{1,0:T(8,128)(2,1)} %bitcast.44, bf16[576,640]{1,0:T(8,128)(2,1)} %copy-done.2, bf16[576,640]{1,0:T(8,128)(2,1)S(1)} %bitcast.34, f32[512]{0:T(512)S(1)} %div.23, bf16[512,576]{0,1:T(8,128)(2,1)} %param.8), kind=kOutput, calls=%fused_computation.7 | convolution fusion | flops 758808576 | bytes 4556800 | tf_op jit(solution)/shard_map/decoder_grads/dot_general | solution.py:50
  158.8 11.5 %all-to-all-done.5.g = bf16[8,64,1280]{2,1,0:T(8,128)(2,1)S(1)} async-done(((bf16[8,64,1280]{2,1,0:T(8,128)(2,1)}), bf16[8,64,1280]{2,1,0:T(8,128)(2,1)S(1)}, u32[]{:S(2)}, u32[]{:S(2)}) %all-to-all-start.5) | async-done | bytes 1310752 | tf_op jit(solution)/shard_map/back/all_to_all | solution.py:352
  171.6 21.8 %all_to_all.38 = bf16[8,64,1280]{2,1,0:T(8,128)(2,1)S(1)} all-to-all(bf16[8,64,1280]{2,1,0:T(8,128)(2,1)S(1)} %weigh.1), channel_id=1, replica_groups=mesh['layer'=8,'latent'=64] {'layer'}, dimensions={0} | all-to-all | bytes 2621440 | tf_op jit(solution)/shard_map/encoder_grads/all_to_all | solution.py:352
  193.4 2.5 %encoder_grads.1 = (f32[576,512]{1,0:T(8,128)}, f32[1,512]{1,0:T(1,128)}) custom-call(s32[1]{0:T(128)} %bitcast.c, bf16[576,1280]{1,0:T(8,128)(2,1)S(1)} %bitcast.31, bf16[512,1280]{1,0:T(8,128)(2,1)S(1)} %bitcast.36), custom_call_target="tpu_custom_call" | custom-call | tf_op jit(solution)/shard_map/encoder_grads/encoder_grads/pallas_call | solution.py:342
  (45 shorter events, 12.2 us)
Async XLA Ops:
  0.6 109.1 %copy-start = (f32[576]{0:T(1024)S(1)}, f32[576]{0:T(1024)}, u32[]{:S(2)}) copy-start(f32[576]{0:T(1024)} %param.9) | copy-start | bytes 6916
  4.6 24.6 %all-to-all-start = ((bf16[8,64,1280]{2,1,0:T(8,128)(2,1)}), bf16[8,64,1280]{2,1,0:T(8,128)(2,1)S(1)}, u32[]{:S(2)}, u32[]{:S(2)}) async-start(bf16[8,64,1280]{2,1,0:T(8,128)(2,1)} %bitcast.45), calls=%async_computation | async-start | bytes 2621440 | tf_op jit(solution)/shard_map/encode/all_to_all | solution.py:352
  29.2 1.0 copy-start.4
  30.7 20.5 %copy-start.7 = (f32[64,1280]{1,0:T(8,128)}, f32[64,1280]{1,0:T(8,128)S(1)}, u32[]{:S(2)}) copy-start(f32[64,1280]{1,0:T(8,128)S(1)} %get-tuple-element.38.s) | copy-start | bytes 983044
  30.7 20.5 %copy-start.3 = (bf16[512,576]{0,1:T(8,128)(2,1)S(1)}, bf16[512,576]{0,1:T(8,128)(2,1)}, u32[]{:S(2)}) copy-start(bf16[512,576]{0,1:T(8,128)(2,1)} %param.8) | copy-start | bytes 1769476
  51.2 35.2 %copy-start.9 = (bf16[8,64,1280]{2,1,0:T(8,128)(2,1)}, bf16[8,64,1280]{2,1,0:T(8,128)(2,1)S(1)}, u32[]{:S(2)}) copy-start(bf16[8,64,1280]{2,1,0:T(8,128)(2,1)S(1)} %all_to_all.35) | copy-start | bytes 3932164
  51.8 7.7 %collective-permute-start = (bf16[576,640]{1,0:T(8,128)(2,1)S(1)}, bf16[576,640]{1,0:T(8,128)(2,1)S(1)}, u32[]{:S(2)}, u32[]{:S(2)}) collective-permute-start(bf16[576,640]{1,0:T(8,128)(2,1)S(1)} %fusion.7), channel_id=1, source_target_pairs={{0,1},{1,0},{2,3},{3,2},{4,5},{5,4},{6,7},{7,6},{8,9},{9,8},{10,11... | collective-permute-start | bytes 2211848 | tf_op jit(solution)/shard_map/decode/ppermute | solution.py:387
  86.4 16.9 %copy-start.1 = (bf16[1280,576]{0,1:T(8,128)(2,1)S(1)}, bf16[1280,576]{0,1:T(8,128)(2,1)}, u32[]{:S(2)}) copy-start(bf16[1280,576]{0,1:T(8,128)(2,1)} %param.5) | copy-start | bytes 4423684
  87.3 27.4 %all-to-all-start.3 = ((bf16[4,72,640]{2,1,0:T(8,128)(2,1)}), bf16[4,72,640]{2,1,0:T(8,128)(2,1)S(1)}, u32[]{:S(2)}, u32[]{:S(2)}) async-start(bf16[4,72,640]{2,1,0:T(8,128)(2,1)} %near_sum.1), calls=%async_computation.3 | async-start | bytes 737280 | tf_op jit(solution)/shard_map/error/all_to_all | solution.py:352
  96.6 4.3 %collective-permute-start.1 = (f32[512]{0:T(512)S(1)}, f32[512]{0:T(512)S(1)}, u32[]{:S(2)}, u32[]{:S(2)}) collective-permute-start(f32[512]{0:T(512)S(1)} %bitcast.40), channel_id=1, source_target_pairs={{0,128},{64,192},{128,0},{192,64},{256,384},{320,448},{384,256},{4... | collective-permute-start | bytes 6152 | tf_op jit(solution)/shard_map/norms/ppermute | solution.py:399
  101.0 5.8 %collective-permute-start.2 = (f32[512]{0:T(512)S(1)}, f32[512]{0:T(512)S(1)}, u32[]{:S(2)}, u32[]{:S(2)}) collective-permute-start(f32[512]{0:T(512)S(1)} %add.38), channel_id=1, source_target_pairs={{0,384},{64,448},{128,256},{192,320},{256,128},{320,192},{384,0},{... | collective-permute-start | bytes 6152 | tf_op jit(solution)/shard_map/norms/ppermute | solution.py:399
  106.8 6.1 %collective-permute-start.3 = (f32[512]{0:T(512)S(1)}, f32[512]{0:T(512)S(1)}, u32[]{:S(2)}, u32[]{:S(2)}) collective-permute-start(f32[512]{0:T(512)S(1)} %add.39), channel_id=1, source_target_pairs={{0,64},{64,0},{128,192},{192,128},{256,320},{320,256},{384,448},{4... | collective-permute-start | bytes 6152 | tf_op jit(solution)/shard_map/norms/ppermute | solution.py:399
  141.1 4.1 %collective-permute-start.4 = (bf16[576,640]{1,0:T(8,128)(2,1)S(1)}, bf16[576,640]{1,0:T(8,128)(2,1)S(1)}, u32[]{:S(2)}, u32[]{:S(2)}) collective-permute-start(bf16[576,640]{1,0:T(8,128)(2,1)S(1)} %bitcast.32), channel_id=1, source_target_pairs={{0,1},{1,0},{2,3},{3,2},{4,5},{5,4},{6,7},{7,6},{8,9},{9,8},{10,11... | collective-permute-start | bytes 2211848 | tf_op jit(solution)/shard_map/error/ppermute | solution.py:409
  145.2 1.5 copy-start.2
  146.7 23.5 %all-to-all-start.5 = ((bf16[8,64,1280]{2,1,0:T(8,128)(2,1)}), bf16[8,64,1280]{2,1,0:T(8,128)(2,1)S(1)}, u32[]{:S(2)}, u32[]{:S(2)}) async-start(bf16[8,64,1280]{2,1,0:T(8,128)(2,1)} %bitcast.16), calls=%async_computation.5 | async-start | bytes 2621440 | tf_op jit(solution)/shard_map/back/all_to_all | solution.py:352
  154.2 3.7 %copy-start.8 = (f32[64,1280]{1,0:T(8,128)S(1)}, f32[64,1280]{1,0:T(8,128)}, u32[]{:S(2)}) copy-start(f32[64,1280]{1,0:T(8,128)} %copy-done.7) | copy-start | bytes 983044
  158.0 0.7 copy-start.5
  170.3 1.0 copy-start.6
